TPU v7x, 256 devices: a whole 4x4x8 slice. The times are simulated.
256 devices in a mesh: tile: 64 (over z, x, core), ka: 4 (over y).
Axes of the slice: x: 4, y: 4, z: 8, core: 2. Of those that a mesh axis runs over, the one named last changes fastest.
Arguments:
- amplitudes: bfloat16 [1024, 256, 512], P(('tile', 'ka')), may hold values from -6 to 6
- integrals: bfloat16 [512, 512, 4096], P('tile', None, 'ka'), may hold values from -0.015625 to 0.015625
- slot_block: int32 [512], replicated, may hold values from 0 to 256, as said below
- rest: bfloat16 [1024, 4096], P('tile', 'ka'), may hold values from -12 to 12
- occ_energy: float32 [1024], P('tile'), may hold values from -2 to -0.5
- vir_energy: float32 [4096], P('ka'), may hold values from 0.5 to 3
Outputs:
- new_amp: bfloat16 [1024, 4096], P('tile', 'ka')
Inputs may be any that keep to these rules, and one draw needn't show every extreme that they name: `slot_block`: each of the 256 blocks is stored in exactly one slot; the value 256 marks an empty slot. Slots s*8 to s*8 + 7 belong to owner s along tile; an owner holds 0 to 8 blocks, and some owner holds exactly 8.
All inputs are finite; a program needn't handle non-finite values.
Results may differ from a plain program's by a relative error of at most 0.001.
Values may be sent and summed in bfloat16 or wider, within the bound.
No kernel may reach another device: no remote copies, remote signals or barrier semaphores. Data moves between devices by JAX's collectives and lax.ppermute only.
A program may use at most 128 MiB of HBM per device.

v0:
```python
import jax
import jax.numpy as jnp
from jax import lax
from jax.sharding import PartitionSpec as P


def per_device(amplitudes, integrals, slot_block, rest, occ_energy, vir_energy):
    capacity = integrals.shape[0]
    block_width = integrals.shape[1]
    tile_count = slot_block.shape[0] // capacity
    nblocks = amplitudes.shape[1]
    picker = (slot_block[:, None] == jnp.arange(nblocks, dtype=jnp.int32)[None, :]).astype(
        jnp.bfloat16
    )
    own_rows = amplitudes[None]
    stacked = lax.all_gather(own_rows, "ka", axis=0, tiled=True)
    group_rows = stacked.reshape(-1, nblocks, block_width)
    rows_per_tile = group_rows.shape[0]
    outgoing = jnp.einsum(
        "sg,rgb->srb", picker, group_rows, preferred_element_type=jnp.float32
    ).astype(jnp.bfloat16)
    outgoing = outgoing.reshape(tile_count, capacity, rows_per_tile, block_width)
    routed = lax.all_to_all(outgoing, "tile", split_axis=0, concat_axis=0, tiled=True)
    partial_value = jnp.einsum(
        "tsrb,sbn->trn", routed, integrals, preferred_element_type=jnp.float32
    )
    ladder = lax.psum_scatter(
        partial_value.reshape(lax.axis_size("tile") * rows_per_tile, partial_value.shape[2]),
        "tile",
        scatter_dimension=0,
        tiled=True,
    )
    denominator = vir_energy[None, :] - occ_energy[:, None]
    return ((rest.astype(jnp.float32) + ladder) / denominator).astype(jnp.bfloat16)


def solution(mesh):
    in_specs = (
        P(("tile", "ka"), None, None),
        P("tile", None, "ka"),
        P(),
        P("tile", "ka"),
        P("tile"),
        P("ka"),
    )
    out_specs = P("tile", "ka")
    return jax.shard_map(
        per_device, mesh=mesh, in_specs=in_specs, out_specs=out_specs, check_vma=False
    )
```

profile of v0, /device:TPU:2, one launch (start us, length us, event | category | flops | bytes accessed | tf_op | source)
XLA Modules:
  0.0 442.5 jit_solution(11806106959478373481)
XLA Ops:
  6.5 0.0 all-gather.3.cloned.1.call-start
  6.5 0.7 all-gather.3.cloned.1.call-update
  7.3 0.0 reduce-scatter.2.cloned.1.call-start
  7.3 55.7 %all-gather.3.cloned.1.call-done = bf16[16,256,512]{2,1,0:T(8,128)(2,1)} async-done(((bf16[4,256,512]{2,1,0:T(8,128)(2,1)}), bf16[16,256,512]{2,1,0:T(8,128)(2,1)}) %all-gather.3.cloned.1.call-update) | async-done | bytes 4194320 | tf_op jit(solution)/shard_map/all_gather | solution.py:16
  63.0 7.8 %convert_bitcast_fusion = bf16[64,8,16,512]{3,1,0,2:T(8,128)(2,1)} fusion(bf16[16,256,512]{2,1,0:T(8,128)(2,1)} %all-gather.3.cloned.1.call-done, s32[512]{0:T(512)} %param.8), kind=kOutput, calls=%fused_computation.2 | convolution fusion | flops 2151809024 | bytes 12584960 | tf_op jit(solution)/shard_map/sg,rgb->srb/dot_general | solution.py:19
  70.8 15.7 %copy.8 = bf16[64,8,16,512]{3,2,1,0:T(8,128)(2,1)} copy(bf16[64,8,16,512]{3,1,0,2:T(8,128)(2,1)} %convert_bitcast_fusion) | data formatting | bytes 16777216 | tf_op jit(solution)/shard_map/reshape | solution.py:22
  86.5 196.6 %all_to_all.5 = bf16[64,8,16,512]{3,2,1,0:T(8,128)(2,1)S(1)} all-to-all(bf16[64,8,16,512]{3,2,1,0:T(8,128)(2,1)} %copy.8), channel_id=1, replica_groups=mesh['tile'=64,'ka'=4] {'tile'}, dimensions={0} | all-to-all | bytes 16777216 | tf_op jit(solution)/shard_map/all_to_all | solution.py:23
  283.1 0.0 copy-start
  283.1 0.0 copy-start.1
  283.1 0.0 copy-start.2
  283.1 12.5 %fusion = f32[64,16,1024,1]{2,1,3,0:T(8,128)} fusion(bf16[64,8,16,512]{3,2,1,0:T(8,128)(2,1)S(1)} %all_to_all.5, bf16[8,512,1024]{2,1,0:T(8,128)(2,1)} %param.7), kind=kOutput, calls=%fused_computation | convolution fusion | flops 8589934592 | bytes 20971520 | tf_op jit(solution)/shard_map/tsrb,sbn->trn/dot_general | solution.py:24
  295.7 0.0 reduce-scatter.2.cloned.1.call-update
  295.7 138.4 %reduce-scatter.2.cloned.1.call-done = f32[16,1024]{1,0:T(8,128)} async-done(((f32[1024,1024]{1,0:T(8,128)}), f32[16,1024]{1,0:T(8,128)}) %reduce-scatter.2.cloned.1.call-update) | async-done | bytes 65552 | tf_op jit(solution)/shard_map/reduce_scatter | solution.py:27
  434.1 0.0 copy-done
  434.1 0.0 copy-done.1
  434.1 0.0 copy-done.2
  434.1 1.5 divide_convert_fusion
Async XLA Ops:
  6.5 56.5 %all-gather.3.cloned.1.call-start = ((), (), s32[]{:S(2)}) async-start(), calls=%async_computation.3 | async-start | bytes 5242880 | tf_op jit(solution)/shard_map/all_gather | solution.py:16
  7.3 426.9 %reduce-scatter.2.cloned.1.call-start = ((), (), s32[]{:S(2)}) async-start(), calls=%async_computation.2 | async-start | bytes 4259840 | tf_op jit(solution)/shard_map/reduce_scatter | solution.py:27
  283.1 151.0 %copy-start = (bf16[16,1024]{1,0:T(8,128)(2,1)S(1)}, bf16[16,1024]{1,0:T(8,128)(2,1)}, u32[]{:S(2)}) copy-start(bf16[16,1024]{1,0:T(8,128)(2,1)} %param.9) | copy-start | bytes 98308
  283.1 151.0 %copy-start.1 = (f32[1024]{0:T(1024)S(1)}, f32[1024]{0:T(1024)}, u32[]{:S(2)}) copy-start(f32[1024]{0:T(1024)} %param.11) | copy-start | bytes 12292
  283.1 151.0 %copy-start.2 = (f32[16]{0:T(128)S(1)}, f32[16]{0:T(128)}, u32[]{:S(2)}) copy-start(f32[16]{0:T(128)} %param.10) | copy-start | bytes 196
Sparse Core Ops, SparseCore 0:
  9.2 53.7 all-gather.2
  295.8 138.2 reduce-scatter.1
where the time goes:
time: 443 us
  blocking collectives  197 us (44%)
  waiting for transfers between devices  195 us (44%)
  matrix products  20.3 us (5%)
  local copies, waits for them, and re-layouts  15.7 us (4%)
  between operations  13.4 us (3%)
    all_to_all x1, blocking collectives, per_device(): lax.all_to_all(outgoing, 'tile', split_axis=0, concat_axis=0, tiled=True)  197 us
    reduce_scatter x1, waiting for transfers between devices, per_device(): lax.psum_scatter(partial_value.reshape(lax.axis_size('tile') * rows_per_t...  138 us
    all_gather x1, waiting for transfers between devices, per_device(): stacked = lax.all_gather(own_rows, 'ka', axis=0, tiled=True)  55.7 us
    reshape x1, local copies, waits for them, and re-layouts, per_device(): outgoing.reshape(tile_count, capacity, rows_per_tile, block_width)  15.7 us
    dot_general x1, matrix products, per_device(): jnp.einsum('tsrb,sbn->trn', routed, integrals, preferred_element_type=jnp...  12.5 us
  transfers between devices with their start and end apart: 2, of which 2 were waited for; matrix products, arithmetic and copies ran while one was open for 0% of the time, Pallas kernels for 0%

commit v1 on v0

v1 whole, which is shorter than its diff:
```python
import jax
import jax.numpy as jnp
from jax import lax
from jax.sharding import Mesh, PartitionSpec as P

NZ, NX, NC, NY = 8, 4, 2, 4
CHUNKS = 2


def ring(size, shift):
    return [(i, (i + shift) % size) for i in range(size)]


def route(amp_rows, picker):
    rows, _, width = amp_rows.shape
    tiles = NZ * NX * NC
    with jax.named_scope("pick"):
        outgoing = jnp.einsum(
            "tsg,rgb->trsb", picker, amp_rows, preferred_element_type=jnp.float32
        ).astype(jnp.bfloat16)
    cap = outgoing.shape[2]
    with jax.named_scope("route"):
        routed = lax.all_to_all(outgoing, ("z", "x", "core"), 0, 0, tiled=True)
    routed = routed.reshape(NZ, NX, NC, rows, cap, width)
    return routed.transpose(3, 4, 2, 1, 0, 5).reshape(rows, cap, tiles, width)


def replicate(own):
    half = own.shape[0] // 2
    after = lax.ppermute(own, "y", ring(NY, -1))
    before = lax.ppermute(own, "y", ring(NY, 1))
    low = lax.ppermute(before[:half], "y", ring(NY, 1))
    high = lax.ppermute(after[half:], "y", ring(NY, -1))
    return after, low, high, before


def contract(rows, integrals):
    return jnp.einsum("rsme,sen->rmn", rows, integrals, preferred_element_type=jnp.float32)


def reduce_tiles(partial):
    core = lax.axis_index("core")
    rows, n = partial.shape[0], partial.shape[-1]
    with jax.named_scope("reduce_core"):
        away = lax.dynamic_index_in_dim(partial, 1 - core, 1, keepdims=False)
        kept = lax.dynamic_index_in_dim(partial, core, 1, keepdims=False)
        summed = kept + lax.ppermute(away, "core", ring(NC, 1))
    with jax.named_scope("reduce_zx"):
        outgoing = summed.transpose(2, 1, 0, 3).reshape(NZ * NX, rows, n)
        got = lax.all_to_all(outgoing, ("z", "x"), 0, 0, tiled=True)
        return jnp.sum(got, axis=0)


def per_device(amplitudes, integrals, slot_block, rest, occ_energy, vir_energy):
    nblocks = amplitudes.shape[1]
    cap = integrals.shape[0]
    n = integrals.shape[2]
    picker = (slot_block[:, None] == jnp.arange(nblocks, dtype=jnp.int32)[None, :]).astype(
        jnp.bfloat16
    )
    picker = picker.reshape(-1, cap, nblocks)
    step = amplitudes.shape[0] // CHUNKS
    pieces = []
    for c in range(CHUNKS):
        own = route(amplitudes[c * step : (c + 1) * step], picker)
        after, low, high, before = replicate(own)
        everything = [own, after, low, high, before]
        partial = jnp.concatenate([contract(rows, integrals) for rows in everything])
        partial = partial.reshape(-1, NC, NX, NZ, n)
        pieces.append(reduce_tiles(partial).reshape(NY, step, n))
    relative = jnp.concatenate(pieces, axis=1)
    k = lax.axis_index("y")
    doubled = jnp.concatenate([relative, relative], axis=0)
    ladder = lax.dynamic_slice_in_dim(doubled, (NY - k) % NY, NY, 0).reshape(rest.shape)
    denominator = vir_energy[None, :] - occ_energy[:, None]
    return ((rest.astype(jnp.float32) + ladder) / denominator).astype(jnp.bfloat16)


def solution(mesh):
    grid = Mesh(mesh.devices.reshape(NZ, NX, NC, NY), ("z", "x", "core", "y"))
    tile = ("z", "x", "core")
    in_specs = (
        P(tile + ("y",), None, None),
        P(tile, None, "y"),
        P(),
        P(tile, "y"),
        P(tile),
        P("y"),
    )
    return jax.shard_map(
        per_device, mesh=grid, in_specs=in_specs, out_specs=P(tile, "y"), check_vma=False
    )
```

time: 443 us -> 203 us (0.46)
  blocking collectives: 197 us -> 0 us
  waiting for transfers between devices: 195 us -> 118 us
  starting transfers between devices: 0.04 us -> 43.1 us
  between operations: 13.4 us -> 0.41 us
  matrix products: 20.3 us -> 30 us
  local copies, waits for them, and re-layouts: 15.7 us -> 9.86 us
    all_to_all x1 -> x0, blocking collectives: 197 us -> none  [per_device(): lax.all_to_all(outgoing, 'tile', split_axis=0, concat_axis=0, tiled=True)]
    reduce_scatter x1 -> x0, waiting for transfers between devices: 138 us -> none  [per_device(): lax.psum_scatter(partial_value.reshape(lax.axis_size('tile') * rows_per_t...]
    all_to_all x0 -> x4, waiting for transfers between devices: none -> 99 us  [the longest x2 51.5 us: route(): routed = lax.all_to_all(outgoing, ('z', 'x', 'core'), 0, 0, tiled=True)]
    all_gather x1 -> x0, waiting for transfers between devices: 55.7 us -> none  [per_device(): stacked = lax.all_gather(own_rows, 'ka', axis=0, tiled=True)]
    all_to_all x0 -> x4, starting transfers between devices: none -> 29.6 us  [the longest x2 17.7 us: route(): routed = lax.all_to_all(outgoing, ('z', 'x', 'core'), 0, 0, tiled=True)]
    ppermute x0 -> x10, waiting for transfers between devices: none -> 19 us  [the longest x2 11 us: replicate(): before = lax.ppermute(own, 'y', ring(NY, 1))]
    reshape x1 -> x3, local copies, waits for them, and re-layouts: 15.7 us -> 0.07 us  [the longest x2 0.05 us: per_device(): pieces.append(reduce_tiles(partial).reshape(NY, step, n))]
    ppermute x0 -> x10, starting transfers between devices: none -> 13.5 us  [the longest x2 6.11 us: replicate(): after = lax.ppermute(own, 'y', ring(NY, -1))]
  transfers between devices with their start and end apart: 2 -> 14, of which waited for: 2 -> 8; matrix products, arithmetic and copies ran while one was open for 0% -> 17% of each run, Pallas kernels for 0% -> 0%
where the time goes in v1:
time: 203 us
  waiting for transfers between devices  118 us (58%)
  starting transfers between devices  43.1 us (21%)
  matrix products  30 us (15%)
  local copies, waits for them, and re-layouts  9.86 us (5%)
    all_to_all x2, waiting for transfers between devices, route(): routed = lax.all_to_all(outgoing, ('z', 'x', 'core'), 0, 0, tiled=True)  51.5 us
    all_to_all x2, waiting for transfers between devices, reduce_tiles(): got = lax.all_to_all(outgoing, ('z', 'x'), 0, 0, tiled=True)  47.4 us
    dot_general x10, matrix products, contract(): jnp.einsum('rsme,sen->rmn', rows, integrals, preferred_element_type=jnp.f...  26 us
    all_to_all x2, starting transfers between devices, route(): routed = lax.all_to_all(outgoing, ('z', 'x', 'core'), 0, 0, tiled=True)  17.7 us
    all_to_all x2, starting transfers between devices, reduce_tiles(): got = lax.all_to_all(outgoing, ('z', 'x'), 0, 0, tiled=True)  11.9 us
    ppermute x2, waiting for transfers between devices, replicate(): before = lax.ppermute(own, 'y', ring(NY, 1))  11 us
    ppermute x2, starting transfers between devices, replicate(): after = lax.ppermute(own, 'y', ring(NY, -1))  6.11 us
    ppermute x2, starting transfers between devices, replicate(): high = lax.ppermute(after[half:], 'y', ring(NY, -1))  6.03 us
  transfers between devices with their start and end apart: 14, of which 8 were waited for; matrix products, arithmetic and copies ran while one was open for 17% of the time, Pallas kernels for 0%

profile of v1, /device:TPU:2, one launch (start us, length us, event | category | flops | bytes accessed | tf_op | source)
XLA Modules:
  0.0 202.5 jit_solution(17252434187564942974)
XLA Ops:
  0.9 2.5 %fusion.21 = bf16[64,2,8,512]{3,2,1,0:T(8,128)(2,1)} fusion(bf16[4,256,512]{2,1,0:T(8,128)(2,1)} %param.6, s32[64,8]{1,0:T(8,128)S(1)} %eq.18), kind=kOutput, calls=%fused_computation.23 | convolution fusion | flops 269090816 | bytes 1574912 | tf_op jit(solution)/shard_map/pick/tsg,rgb->trsb/dot_general | solution.py:18
  3.4 12.0 %all-to-all-start.2 = ((bf16[64,2,8,512]{3,2,1,0:T(8,128)(2,1)}), bf16[64,2,8,512]{3,2,1,0:T(8,128)(2,1)S(1)}, u32[]{:S(2)}, u32[]{:S(2)}) async-start(bf16[64,2,8,512]{3,2,1,0:T(8,128)(2,1)} %fusion.21), calls=%async_computation.2 | async-start | bytes 2097152 | tf_op jit(solution)/shard_map/route/all_to_all | solution.py:23
  15.4 1.5 fusion.20
  16.9 27.3 %all-to-all-done.2 = bf16[64,2,8,512]{3,2,1,0:T(8,128)(2,1)S(1)} async-done(((bf16[64,2,8,512]{3,2,1,0:T(8,128)(2,1)}), bf16[64,2,8,512]{3,2,1,0:T(8,128)(2,1)S(1)}, u32[]{:S(2)}, u32[]{:S(2)}) %all-to-all-start.2) | async-done | bytes 1048608 | tf_op jit(solution)/shard_map/route/all_to_all | solution.py:23
  44.2 5.7 %all-to-all-start = ((bf16[64,2,8,512]{3,2,1,0:T(8,128)(2,1)}), bf16[64,2,8,512]{3,2,1,0:T(8,128)(2,1)S(1)}, u32[]{:S(2)}, u32[]{:S(2)}) async-start(bf16[64,2,8,512]{3,2,1,0:T(8,128)(2,1)} %fusion.20), calls=%async_computation | async-start | bytes 2097152 | tf_op jit(solution)/shard_map/route/all_to_all | solution.py:23
  49.9 1.5 copy.31
  51.4 3.0 %collective-permute-start.5 = (bf16[2,8,64,512]{3,2,1,0:T(8,128)(2,1)}, bf16[2,8,64,512]{3,2,1,0:T(8,128)(2,1)}, u32[]{:S(2)}, u32[]{:S(2)}) collective-permute-start(bf16[2,8,64,512]{3,2,1,0:T(8,128)(2,1)} %bitcast.42), channel_id=1, source_target_pairs={{0,3},{1,0},{2,1},{3,2},{4,7},{5,4},{6,5},{7,6},{8,11},{9,8},{10,9... | collective-permute-start | bytes 3145736 | tf_op jit(solution)/shard_map/ppermute | solution.py:30
  54.4 24.2 %all-to-all-done = bf16[64,2,8,512]{3,2,1,0:T(8,128)(2,1)S(1)} async-done(((bf16[64,2,8,512]{3,2,1,0:T(8,128)(2,1)}), bf16[64,2,8,512]{3,2,1,0:T(8,128)(2,1)S(1)}, u32[]{:S(2)}, u32[]{:S(2)}) %all-to-all-start) | async-done | bytes 1048608 | tf_op jit(solution)/shard_map/route/all_to_all | solution.py:23
  79.2 3.1 %collective-permute-start = (bf16[2,8,64,512]{3,2,1,0:T(8,128)(2,1)S(1)}, bf16[2,8,64,512]{3,2,1,0:T(8,128)(2,1)S(1)}, u32[]{:S(2)}, u32[]{:S(2)}) collective-permute-start(bf16[2,8,64,512]{3,2,1,0:T(8,128)(2,1)S(1)} %bitcast.173), channel_id=1, source_target_pairs={{0,3},{1,0},{2,1},{3,2},{4,7},{5,4},{6,5},{7,6},{8,11},{9,8},{10,9... | collective-permute-start | bytes 3145736 | tf_op jit(solution)/shard_map/ppermute | solution.py:30
  82.3 5.8 %fusion.31 = f32[8,2,4,8,1024]{4,3,2,1,0:T(8,128)S(1)} fusion(bf16[8,512,1024]{2,1,0:T(8,128)(2,1)} %param.7, bf16[2,2,4,8,512,8]{4,5,0,1,2,3:T(8,128)(2,1)S(1)} %bitcast.166), kind=kOutput, calls=%fused_computation.27 | convolution fusion | flops 1073741824 | bytes 9961472 | tf_op jit(solution)/shard_map/rsme,sen->rmn/dot_general | solution.py:38
  88.1 5.8 %fusion.25 = f32[8,2,4,8,1024]{4,3,2,1,0:T(8,128)S(1)} fusion(bf16[8,512,1024]{2,1,0:T(8,128)(2,1)} %param.7, bf16[2,2,4,8,512,8]{4,5,0,1,2,3:T(8,128)(2,1)S(1)} %bitcast.168), kind=kOutput, calls=%fused_computation.25 | convolution fusion | flops 1073741824 | bytes 9961472 | tf_op jit(solution)/shard_map/rsme,sen->rmn/dot_general | solution.py:38
  94.8 1.1 slice.27
  95.9 2.7 %collective-permute-start.8 = (bf16[1,8,64,512]{3,2,1,0:T(8,128)(2,1)S(1)}, bf16[1,8,64,512]{3,2,1,0:T(8,128)(2,1)S(1)}, u32[]{:S(2)}, u32[]{:S(2)}) collective-permute-start(bf16[1,8,64,512]{3,2,1,0:T(8,128)(2,1)S(1)} %slice.27), channel_id=1, source_target_pairs={{0,3},{1,0},{2,1},{3,2},{4,7},{5,4},{6,5},{7,6},{8,11},{9,8},{10,9... | collective-permute-start | bytes 1572872 | tf_op jit(solution)/shard_map/ppermute | solution.py:33
  98.6 11.0 %collective-permute-done.1 = bf16[2,8,64,512]{3,2,1,0:T(8,128)(2,1)S(1)} collective-permute-done((bf16[2,8,64,512]{3,2,1,0:T(8,128)(2,1)S(1)}, bf16[2,8,64,512]{3,2,1,0:T(8,128)(2,1)S(1)}, u32[]{:S(2)}, u32[]{:S(2)}) %collective-permute-start.1) | collective-permute-done | bytes 1048608 | tf_op jit(solution)/shard_map/ppermute | solution.py:31
  109.8 3.3 %collective-permute-start.3 = (bf16[1,8,64,512]{3,2,1,0:T(8,128)(2,1)S(1)}, bf16[1,8,64,512]{3,2,1,0:T(8,128)(2,1)S(1)}, u32[]{:S(2)}, u32[]{:S(2)}) collective-permute-start(bf16[1,8,64,512]{3,2,1,0:T(8,128)(2,1)S(1)} %slice.25), channel_id=1, source_target_pairs={{0,3},{1,0},{2,1},{3,2},{4,7},{5,4},{6,5},{7,6},{8,11},{9,8},{10,9... | collective-permute-start | bytes 1572872 | tf_op jit(solution)/shard_map/ppermute | solution.py:33
  113.1 2.6 %fusion.14 = f32[2,64,1024,1]{2,1,3,0:T(8,128)S(1)} fusion(bf16[2,8,64,512]{3,2,1,0:T(8,128)(2,1)} %collective-permute-done.5, bf16[8,512,1024]{2,1,0:T(8,128)(2,1)S(1)} %bitcast.164), kind=kOutput, calls=%fused_computation.14 | convolution fusion | flops 1073741824 | bytes 9961472 | tf_op jit(solution)/shard_map/rsme,sen->rmn/dot_general | solution.py:38
  115.8 1.3 fusion.18
  117.1 1.4 fusion.12
  118.5 2.0 %fusion.16 = f32[2,64,1024,1]{2,1,3,0:T(8,128)} fusion(bf16[2,8,64,512]{3,2,1,0:T(8,128)(2,1)S(1)} %collective-permute-done.1, bf16[8,512,1024]{2,1,0:T(8,128)(2,1)S(1)} %bitcast.164), kind=kOutput, calls=%fused_computation.16 | convolution fusion | flops 1073741824 | bytes 9961472 | tf_op jit(solution)/shard_map/rsme,sen->rmn/dot_general | solution.py:38
  120.9 1.6 fusion.40
  122.5 1.6 fusion.43
  124.6 5.0 %collective-permute-done.2 = bf16[1,8,64,512]{3,2,1,0:T(8,128)(2,1)S(1)} collective-permute-done((bf16[1,8,64,512]{3,2,1,0:T(8,128)(2,1)S(1)}, bf16[1,8,64,512]{3,2,1,0:T(8,128)(2,1)S(1)}, u32[]{:S(2)}, u32[]{:S(2)}) %collective-permute-start.2) | collective-permute-done | bytes 524320 | tf_op jit(solution)/shard_map/ppermute | solution.py:32
  129.6 1.6 fusion.34
  131.3 2.3 %fusion.37 = f32[2,4,8,1024]{3,2,0,1:T(8,128)} fusion(bf16[8,512,1024]{2,1,0:T(8,128)(2,1)S(1)} %bitcast.164, bf16[2,4,8,512,8]{3,2,1,0,4:T(8,128)(2,1)S(1)} %bitcast.176), kind=kOutput, calls=%fused_computation.29 | convolution fusion | flops 536870912 | bytes 9175040 | tf_op jit(solution)/shard_map/rsme,sen->rmn/dot_general | solution.py:38
  133.7 1.6 copy.38
  135.3 6.2 %all-to-all-start.3 = ((f32[32,8,1024]{2,1,0:T(8,128)}), f32[32,8,1024]{2,1,0:T(8,128)S(1)}, u32[]{:S(2)}, u32[]{:S(2)}) async-start(f32[32,8,1024]{2,1,0:T(8,128)} %bitcast.67), calls=%async_computation.3 | async-start | bytes 2097152 | tf_op jit(solution)/shard_map/reduce_zx/all_to_all | solution.py:50
  142.6 1.1 constant_dynamic-update-slice_fusion
  143.9 2.6 %collective-permute-done.4 = f32[8,4,8,1024]{3,2,1,0:T(8,128)S(1)} collective-permute-done((f32[8,4,8,1024]{3,2,1,0:T(8,128)S(1)}, f32[8,4,8,1024]{3,2,1,0:T(8,128)S(1)}, u32[]{:S(2)}, u32[]{:S(2)}) %collective-permute-start.4) | collective-permute-done | bytes 1048608 | tf_op jit(solution)/shard_map/reduce_core/ppermute | solution.py:47
  146.7 1.6 copy.30
  148.3 20.8 %all-to-all-done.3 = f32[32,8,1024]{2,1,0:T(8,128)S(1)} async-done(((f32[32,8,1024]{2,1,0:T(8,128)}), f32[32,8,1024]{2,1,0:T(8,128)S(1)}, u32[]{:S(2)}, u32[]{:S(2)}) %all-to-all-start.3) | async-done | bytes 1048608 | tf_op jit(solution)/shard_map/reduce_zx/all_to_all | solution.py:50
  169.2 5.7 %all-to-all-start.1 = ((f32[32,8,1024]{2,1,0:T(8,128)}), f32[32,8,1024]{2,1,0:T(8,128)S(1)}, u32[]{:S(2)}, u32[]{:S(2)}) async-start(f32[32,8,1024]{2,1,0:T(8,128)} %bitcast.36), calls=%async_computation.1 | async-start | bytes 2097152 | tf_op jit(solution)/shard_map/reduce_zx/all_to_all | solution.py:50
  175.0 26.6 %all-to-all-done.1 = f32[32,8,1024]{2,1,0:T(8,128)S(1)} async-done(((f32[32,8,1024]{2,1,0:T(8,128)}), f32[32,8,1024]{2,1,0:T(8,128)S(1)}, u32[]{:S(2)}, u32[]{:S(2)}) %all-to-all-start.1) | async-done | bytes 1048608 | tf_op jit(solution)/shard_map/reduce_zx/all_to_all | solution.py:50
  (53 shorter events, 5.9 us)
Async XLA Ops:
  0.0 15.4 %copy-start.2 = (bf16[4,256,512]{2,1,0:T(8,128)(2,1)S(1)}, bf16[4,256,512]{2,1,0:T(8,128)(2,1)}, u32[]{:S(2)}) copy-start(bf16[4,256,512]{2,1,0:T(8,128)(2,1)} %param.6) | copy-start | bytes 3145732
  3.4 40.8 %all-to-all-start.2 = ((bf16[64,2,8,512]{3,2,1,0:T(8,128)(2,1)}), bf16[64,2,8,512]{3,2,1,0:T(8,128)(2,1)S(1)}, u32[]{:S(2)}, u32[]{:S(2)}) async-start(bf16[64,2,8,512]{3,2,1,0:T(8,128)(2,1)} %fusion.21), calls=%async_computation.2 | async-start | bytes 2097152 | tf_op jit(solution)/shard_map/route/all_to_all | solution.py:23
  44.2 34.5 %all-to-all-start = ((bf16[64,2,8,512]{3,2,1,0:T(8,128)(2,1)}), bf16[64,2,8,512]{3,2,1,0:T(8,128)(2,1)S(1)}, u32[]{:S(2)}, u32[]{:S(2)}) async-start(bf16[64,2,8,512]{3,2,1,0:T(8,128)(2,1)} %fusion.20), calls=%async_computation | async-start | bytes 2097152 | tf_op jit(solution)/shard_map/route/all_to_all | solution.py:23
  51.4 43.4 %collective-permute-start.5 = (bf16[2,8,64,512]{3,2,1,0:T(8,128)(2,1)}, bf16[2,8,64,512]{3,2,1,0:T(8,128)(2,1)}, u32[]{:S(2)}, u32[]{:S(2)}) collective-permute-start(bf16[2,8,64,512]{3,2,1,0:T(8,128)(2,1)} %bitcast.42), channel_id=1, source_target_pairs={{0,3},{1,0},{2,1},{3,2},{4,7},{5,4},{6,5},{7,6},{8,11},{9,8},{10,9... | collective-permute-start | bytes 3145736 | tf_op jit(solution)/shard_map/ppermute | solution.py:30
  54.4 39.5 %collective-permute-start.6 = (bf16[2,8,64,512]{3,2,1,0:T(8,128)(2,1)}, bf16[2,8,64,512]{3,2,1,0:T(8,128)(2,1)S(1)}, u32[]{:S(2)}, u32[]{:S(2)}) collective-permute-start(bf16[2,8,64,512]{3,2,1,0:T(8,128)(2,1)} %bitcast.42), channel_id=1, source_target_pairs={{0,1},{1,2},{2,3},{3,0},{4,5},{5,6},{6,7},{7,4},{8,9},{9,10},{10,1... | collective-permute-start | bytes 3145736 | tf_op jit(solution)/shard_map/ppermute | solution.py:31
  79.2 30.5 %collective-permute-start = (bf16[2,8,64,512]{3,2,1,0:T(8,128)(2,1)S(1)}, bf16[2,8,64,512]{3,2,1,0:T(8,128)(2,1)S(1)}, u32[]{:S(2)}, u32[]{:S(2)}) collective-permute-start(bf16[2,8,64,512]{3,2,1,0:T(8,128)(2,1)S(1)} %bitcast.173), channel_id=1, source_target_pairs={{0,3},{1,0},{2,1},{3,2},{4,7},{5,4},{6,5},{7,6},{8,11},{9,8},{10,9... | collective-permute-start | bytes 3145736 | tf_op jit(solution)/shard_map/ppermute | solution.py:30
  82.3 27.3 %collective-permute-start.1 = (bf16[2,8,64,512]{3,2,1,0:T(8,128)(2,1)S(1)}, bf16[2,8,64,512]{3,2,1,0:T(8,128)(2,1)S(1)}, u32[]{:S(2)}, u32[]{:S(2)}) collective-permute-start(bf16[2,8,64,512]{3,2,1,0:T(8,128)(2,1)S(1)} %bitcast.174), channel_id=1, source_target_pairs={{0,1},{1,2},{2,3},{3,0},{4,5},{5,6},{6,7},{7,4},{8,9},{9,10},{10,1... | collective-permute-start | bytes 3145736 | tf_op jit(solution)/shard_map/ppermute | solution.py:31
  82.3 30.8 %slice-start = ((s8[8388608]{0:T(1024)(128)(4,1)}), s8[4194304]{0:T(1024)(128)(4,1)S(1)}, s32[]{:S(2)}) async-start(s8[8388608]{0:T(1024)(128)(4,1)} %bitcast.163), calls=%async_computation.4 | async-start | bytes 8388608
  88.1 25.0 %slice-start.1 = ((s8[8388608]{0:T(1024)(128)(4,1)}), s8[4194304]{0:T(1024)(128)(4,1)S(1)}, s32[]{:S(2)}) async-start(s8[8388608]{0:T(1024)(128)(4,1)} %bitcast.163), calls=%async_computation.5 | async-start | bytes 8388608
  93.9 26.9 %collective-permute-start.7 = (bf16[1,8,64,512]{3,2,1,0:T(8,128)(2,1)S(1)}, bf16[1,8,64,512]{3,2,1,0:T(8,128)(2,1)S(1)}, u32[]{:S(2)}, u32[]{:S(2)}) collective-permute-start(bf16[1,8,64,512]{3,2,1,0:T(8,128)(2,1)S(1)} %slice.26), channel_id=1, source_target_pairs={{0,1},{1,2},{2,3},{3,0},{4,5},{5,6},{6,7},{7,4},{8,9},{9,10},{10,1... | collective-permute-start | bytes 1572872 | tf_op jit(solution)/shard_map/ppermute | solution.py:32
  95.9 26.6 %collective-permute-start.8 = (bf16[1,8,64,512]{3,2,1,0:T(8,128)(2,1)S(1)}, bf16[1,8,64,512]{3,2,1,0:T(8,128)(2,1)S(1)}, u32[]{:S(2)}, u32[]{:S(2)}) collective-permute-start(bf16[1,8,64,512]{3,2,1,0:T(8,128)(2,1)S(1)} %slice.27), channel_id=1, source_target_pairs={{0,3},{1,0},{2,1},{3,2},{4,7},{5,4},{6,5},{7,6},{8,11},{9,8},{10,9... | collective-permute-start | bytes 1572872 | tf_op jit(solution)/shard_map/ppermute | solution.py:33
  109.7 20.0 %collective-permute-start.2 = (bf16[1,8,64,512]{3,2,1,0:T(8,128)(2,1)S(1)}, bf16[1,8,64,512]{3,2,1,0:T(8,128)(2,1)S(1)}, u32[]{:S(2)}, u32[]{:S(2)}) collective-permute-start(bf16[1,8,64,512]{3,2,1,0:T(8,128)(2,1)S(1)} %slice.24), channel_id=1, source_target_pairs={{0,1},{1,2},{2,3},{3,0},{4,5},{5,6},{6,7},{7,4},{8,9},{9,10},{10,1... | collective-permute-start | bytes 1572872 | tf_op jit(solution)/shard_map/ppermute | solution.py:32
  109.8 21.4 %collective-permute-start.3 = (bf16[1,8,64,512]{3,2,1,0:T(8,128)(2,1)S(1)}, bf16[1,8,64,512]{3,2,1,0:T(8,128)(2,1)S(1)}, u32[]{:S(2)}, u32[]{:S(2)}) collective-permute-start(bf16[1,8,64,512]{3,2,1,0:T(8,128)(2,1)S(1)} %slice.25), channel_id=1, source_target_pairs={{0,3},{1,0},{2,1},{3,2},{4,7},{5,4},{6,5},{7,6},{8,11},{9,8},{10,9... | collective-permute-start | bytes 1572872 | tf_op jit(solution)/shard_map/ppermute | solution.py:33
  117.1 1.4 copy-start
  124.3 9.3 %collective-permute-start.9 = (f32[8,4,8,1024]{3,2,1,0:T(8,128)S(1)}, f32[8,4,8,1024]{3,2,1,0:T(8,128)S(1)}, u32[]{:S(2)}, u32[]{:S(2)}) collective-permute-start(f32[8,4,8,1024]{3,2,1,0:T(8,128)S(1)} %dynamic-slice_bitcast_fusion), channel_id=1, source_target_pairs={{0,4},{4,0},{1,5},{5,1},{2,6},{6,2},{3,7},{7,3},{8,12},{12,8},{9,1... | collective-permute-start | bytes 3145736 | tf_op jit(solution)/shard_map/reduce_core/ppermute | solution.py:47
  133.7 7.8 %copy-start.1 = (f32[8,2,4,8,1024]{4,3,2,1,0:T(8,128)S(1)}, f32[8,2,4,8,1024]{4,3,2,1,0:T(8,128)}, u32[]{:S(2)}) copy-start(f32[8,2,4,8,1024]{4,3,2,1,0:T(8,128)} %copy-done) | copy-start | bytes 6291460
  135.3 33.8 %all-to-all-start.3 = ((f32[32,8,1024]{2,1,0:T(8,128)}), f32[32,8,1024]{2,1,0:T(8,128)S(1)}, u32[]{:S(2)}, u32[]{:S(2)}) async-start(f32[32,8,1024]{2,1,0:T(8,128)} %bitcast.67), calls=%async_computation.3 | async-start | bytes 2097152 | tf_op jit(solution)/shard_map/reduce_zx/all_to_all | solution.py:50
  143.8 2.7 %collective-permute-start.4 = (f32[8,4,8,1024]{3,2,1,0:T(8,128)S(1)}, f32[8,4,8,1024]{3,2,1,0:T(8,128)S(1)}, u32[]{:S(2)}, u32[]{:S(2)}) collective-permute-start(f32[8,4,8,1024]{3,2,1,0:T(8,128)S(1)} %dynamic-slice_bitcast_fusion.1), channel_id=1, source_target_pairs={{0,4},{4,0},{1,5},{5,1},{2,6},{6,2},{3,7},{7,3},{8,12},{12,8},{9,1... | collective-permute-start | bytes 3145736 | tf_op jit(solution)/shard_map/reduce_core/ppermute | solution.py:47
  169.1 32.7 %copy-start.3 = (bf16[16,1024]{1,0:T(8,128)(2,1)S(1)}, bf16[16,1024]{1,0:T(8,128)(2,1)}, u32[]{:S(2)}) copy-start(bf16[16,1024]{1,0:T(8,128)(2,1)} %param.9) | copy-start | bytes 98308
  169.2 32.7 %copy-start.4 = (f32[1024]{0:T(1024)S(1)}, f32[1024]{0:T(1024)}, u32[]{:S(2)}) copy-start(f32[1024]{0:T(1024)} %param.11) | copy-start | bytes 12292
  169.2 32.7 %copy-start.5 = (f32[16]{0:T(128)S(1)}, f32[16]{0:T(128)}, u32[]{:S(2)}) copy-start(f32[16]{0:T(128)} %param.10) | copy-start | bytes 196
  169.2 32.4 %all-to-all-start.1 = ((f32[32,8,1024]{2,1,0:T(8,128)}), f32[32,8,1024]{2,1,0:T(8,128)S(1)}, u32[]{:S(2)}, u32[]{:S(2)}) async-start(f32[32,8,1024]{2,1,0:T(8,128)} %bitcast.36), calls=%async_computation.1 | async-start | bytes 2097152 | tf_op jit(solution)/shard_map/reduce_zx/all_to_all | solution.py:50

commit v2 on v1

v2 whole, which is shorter than its diff:
```python
import jax
import jax.numpy as jnp
from jax import lax
from jax.sharding import Mesh, PartitionSpec as P

NZ, NX, NC, NY = 8, 4, 2, 4


def ring(size, shift):
    return [(i, (i + shift) % size) for i in range(size)]


def route(amp_rows, picker):
    rows, _, width = amp_rows.shape
    tiles = NZ * NX * NC
    with jax.named_scope("pick"):
        outgoing = jnp.einsum(
            "tsg,rgb->trsb", picker, amp_rows, preferred_element_type=jnp.float32
        ).astype(jnp.bfloat16)
    cap = outgoing.shape[2]
    with jax.named_scope("route"):
        routed = lax.all_to_all(outgoing, ("z", "x", "core"), 0, 0, tiled=True)
    routed = routed.reshape(NZ, NX, NC, rows, cap, width)
    return routed.transpose(3, 4, 2, 1, 0, 5).reshape(rows, cap, tiles, width)


def neighbours(own):
    return lax.ppermute(own, "y", ring(NY, -1)), lax.ppermute(own, "y", ring(NY, 1))


def opposite(after, before):
    half = after.shape[0] // 2
    low = lax.ppermute(before[:half], "y", ring(NY, 1))
    high = lax.ppermute(after[half:], "y", ring(NY, -1))
    return low, high


def contract(rows, integrals):
    partial = jnp.einsum("rsme,sen->rmn", rows, integrals, preferred_element_type=jnp.float32)
    return partial.reshape(rows.shape[0], NC, NX, NZ, -1)


def pick(array, index, axis):
    return lax.dynamic_index_in_dim(array, index, axis, keepdims=False)


def over_core(partials):
    core = lax.axis_index("core")
    with jax.named_scope("reduce_core"):
        away = jnp.concatenate([pick(part, 1 - core, 1) for part in partials])
        kept = jnp.concatenate([pick(part, core, 1) for part in partials])
        return kept + lax.ppermute(away, "core", ring(NC, 1))


def over_x(summed):
    x = lax.axis_index("x")
    with jax.named_scope("reduce_x"):
        total = pick(summed, x, 1)
        for shift in (1, 3, 2):
            total += lax.ppermute(pick(summed, (x + shift) % NX, 1), "x", ring(NX, shift))
        return total


def over_z(summed):
    with jax.named_scope("reduce_z"):
        outgoing = summed.transpose(1, 0, 2)
        return jnp.sum(lax.all_to_all(outgoing, "z", 0, 0, tiled=True), axis=0)


def per_device(amplitudes, integrals, slot_block, rest, occ_energy, vir_energy):
    nblocks = amplitudes.shape[1]
    cap = integrals.shape[0]
    n = integrals.shape[2]
    picker = (slot_block[:, None] == jnp.arange(nblocks, dtype=jnp.int32)[None, :]).astype(
        jnp.bfloat16
    )
    picker = picker.reshape(-1, cap, nblocks)
    step = amplitudes.shape[0] // 2

    own = lax.optimization_barrier(route(amplitudes[:step], picker))
    after, before = neighbours(own)
    low, high = opposite(after, before)
    later = route(amplitudes[step:], picker)
    later, low, high = lax.optimization_barrier((later, low, high))
    after_later, before_later = neighbours(later)
    parts = [contract(rows, integrals) for rows in (own, after, low, high, before)]
    first = over_core(parts)
    first, after_later, before_later = lax.optimization_barrier((first, after_later, before_later))

    low_later, high_later = opposite(after_later, before_later)
    first = over_z(over_x(first))
    sides = [contract(rows, integrals) for rows in (later, after_later, before_later)]
    sides = over_core(sides)
    first, sides, low_later, high_later = lax.optimization_barrier(
        (first, sides, low_later, high_later)
    )
    sides = over_x(sides)
    across = [contract(rows, integrals) for rows in (low_later, high_later)]
    across = over_x(over_core(across))
    second = over_z(jnp.concatenate([sides[: 2 * step], across, sides[2 * step :]]))
    first = first.reshape(NY, step, n)
    second = second.reshape(NY, step, n)

    relative = jnp.concatenate([first, second], axis=1)
    k = lax.axis_index("y")
    doubled = jnp.concatenate([relative, relative], axis=0)
    ladder = lax.dynamic_slice_in_dim(doubled, (NY - k) % NY, NY, 0).reshape(rest.shape)
    denominator = vir_energy[None, :] - occ_energy[:, None]
    return ((rest.astype(jnp.float32) + ladder) / denominator).astype(jnp.bfloat16)


def solution(mesh):
    grid = Mesh(mesh.devices.reshape(NZ, NX, NC, NY), ("z", "x", "core", "y"))
    tile = ("z", "x", "core")
    in_specs = (
        P(tile + ("y",), None, None),
        P(tile, None, "y"),
        P(),
        P(tile, "y"),
        P(tile),
        P("y"),
    )
    return jax.shard_map(
        per_device, mesh=grid, in_specs=in_specs, out_specs=P(tile, "y"), check_vma=False
    )
```

time: 203 us -> 230 us (1.13); the launches traced: 203 us -> 226 us
  matrix products: 30 us -> 43.4 us
  starting transfers between devices: 43.1 us -> 56.3 us
  waiting for transfers between devices: 118 us -> 105 us
  local copies, waits for them, and re-layouts: 9.86 us -> 14.5 us
  other arithmetic: 1.27 us -> 5.77 us
    all_to_all x2, waiting for transfers between devices: 47.4 us -> 15.7 us  [over_z(): return jnp.sum(lax.all_to_all(outgoing, 'z', 0, 0, tiled=True), axis=0)]
    ppermute x10 -> x20, waiting for transfers between devices: 19 us -> 38.6 us  [the longest x2 15.3 us: neighbours(): lax.ppermute(own, 'y', ring(NY, -1))]
    ppermute x10 -> x20, starting transfers between devices: 13.5 us -> 27.5 us  [the longest x9 14.3 us: over_x(): lax.ppermute(pick(summed, (x + shift) % NX, 1), 'x', ring(NX, shift))]
    dot_general x10, matrix products: 26 us -> 38.3 us  [contract(): jnp.einsum('rsme,sen->rmn', rows, integrals, preferred_element_type=jnp.f...]
    slice x4 -> x6, local copies, waits for them, and re-layouts: 1.18 us -> 5.37 us  [the longest x2 3.43 us: opposite(): low = lax.ppermute(before[:half], 'y', ring(NY, 1))]
    add x0 -> x5, other arithmetic: none -> 2.88 us  [the longest x3 2.81 us: over_core(): return kept + lax.ppermute(away, 'core', ring(NC, 1))]
    unnamed x22, local copies, waits for them, and re-layouts: 1.14 us -> 3.87 us
  transfers between devices with their start and end apart: 14 -> 24, of which waited for: 8 -> 15; matrix products, arithmetic and copies ran while one was open for 17% -> 15% of each run, Pallas kernels for 0% -> 0%
where the time goes in v2:
time: 230 us; the launch traced here: 226 us
  waiting for transfers between devices  105 us (46%)
  starting transfers between devices  56.3 us (24%)
  matrix products  43.4 us (19%)
  local copies, waits for them, and re-layouts  14.5 us (6%)
  other arithmetic  5.77 us (3%)
    all_to_all x2, waiting for transfers between devices, route(): routed = lax.all_to_all(outgoing, ('z', 'x', 'core'), 0, 0, tiled=True)  51.2 us
    dot_general x10, matrix products, contract(): jnp.einsum('rsme,sen->rmn', rows, integrals, preferred_element_type=jnp.f...  38.3 us
    all_to_all x2, starting transfers between devices, route(): routed = lax.all_to_all(outgoing, ('z', 'x', 'core'), 0, 0, tiled=True)  17.7 us
    all_to_all x2, waiting for transfers between devices, over_z(): return jnp.sum(lax.all_to_all(outgoing, 'z', 0, 0, tiled=True), axis=0)  15.7 us
    ppermute x2, waiting for transfers between devices, neighbours(): lax.ppermute(own, 'y', ring(NY, -1))  15.3 us
    ppermute x9, starting transfers between devices, over_x(): lax.ppermute(pick(summed, (x + shift) % NX, 1), 'x', ring(NX, shift))  14.3 us
    ppermute x9, waiting for transfers between devices, over_x(): lax.ppermute(pick(summed, (x + shift) % NX, 1), 'x', ring(NX, shift))  13.8 us
    all_to_all x2, starting transfers between devices, over_z(): return jnp.sum(lax.all_to_all(outgoing, 'z', 0, 0, tiled=True), axis=0)  11.2 us
  transfers between devices with their start and end apart: 24, of which 15 were waited for; matrix products, arithmetic and copies ran while one was open for 15% of the time, Pallas kernels for 0%

profile of v2, /device:TPU:2, one launch (start us, length us, event | category | flops | bytes accessed | tf_op | source)
XLA Modules:
  0.0 225.8 jit_solution(4029720002147416428)
XLA Ops:
  0.8 2.5 %fusion.20 = bf16[64,2,8,512]{3,2,1,0:T(8,128)(2,1)} fusion(bf16[4,256,512]{2,1,0:T(8,128)(2,1)} %param.6, s32[64,8]{1,0:T(8,128)S(1)} %eq.27), kind=kOutput, calls=%fused_computation.22 | convolution fusion | flops 269090816 | bytes 1574912 | tf_op jit(solution)/shard_map/pick/tsg,rgb->trsb/dot_general | solution.py:17
  3.3 12.0 %all-to-all-start = ((bf16[64,2,8,512]{3,2,1,0:T(8,128)(2,1)}), bf16[64,2,8,512]{3,2,1,0:T(8,128)(2,1)S(1)}, u32[]{:S(2)}, u32[]{:S(2)}) async-start(bf16[64,2,8,512]{3,2,1,0:T(8,128)(2,1)} %fusion.20), calls=%async_computation | async-start | bytes 2097152 | tf_op jit(solution)/shard_map/route/all_to_all | solution.py:22
  15.3 2.5 %fusion.21 = bf16[64,2,8,512]{3,2,1,0:T(8,128)(2,1)} fusion(bf16[4,256,512]{2,1,0:T(8,128)(2,1)} %param.6, s32[64,8]{1,0:T(8,128)S(1)} %eq.27), kind=kOutput, calls=%fused_computation.23 | convolution fusion | flops 269090816 | bytes 1574912 | tf_op jit(solution)/shard_map/pick/tsg,rgb->trsb/dot_general | solution.py:17
  17.9 26.3 %all-to-all-done = bf16[64,2,8,512]{3,2,1,0:T(8,128)(2,1)S(1)} async-done(((bf16[64,2,8,512]{3,2,1,0:T(8,128)(2,1)}), bf16[64,2,8,512]{3,2,1,0:T(8,128)(2,1)S(1)}, u32[]{:S(2)}, u32[]{:S(2)}) %all-to-all-start) | async-done | bytes 1048608 | tf_op jit(solution)/shard_map/route/all_to_all | solution.py:22
  44.1 5.7 %all-to-all-start.1 = ((bf16[64,2,8,512]{3,2,1,0:T(8,128)(2,1)}), bf16[64,2,8,512]{3,2,1,0:T(8,128)(2,1)S(1)}, u32[]{:S(2)}, u32[]{:S(2)}) async-start(bf16[64,2,8,512]{3,2,1,0:T(8,128)(2,1)} %fusion.21), calls=%async_computation.1 | async-start | bytes 2097152 | tf_op jit(solution)/shard_map/route/all_to_all | solution.py:22
  53.7 24.9 %all-to-all-done.1 = bf16[64,2,8,512]{3,2,1,0:T(8,128)(2,1)S(1)} async-done(((bf16[64,2,8,512]{3,2,1,0:T(8,128)(2,1)}), bf16[64,2,8,512]{3,2,1,0:T(8,128)(2,1)S(1)}, u32[]{:S(2)}, u32[]{:S(2)}) %all-to-all-start.1) | async-done | bytes 1048608 | tf_op jit(solution)/shard_map/route/all_to_all | solution.py:22
  78.7 4.6 %fusion.18 = f32[2,64,1024,1]{2,1,3,0:T(8,128)S(1)} fusion(bf16[2,8,64,512]{3,2,1,0:T(8,128)(2,1)S(1)} %bitcast.222, bf16[8,512,1024]{2,1,0:T(8,128)(2,1)} %param.7), kind=kOutput, calls=%fused_computation.18 | convolution fusion | flops 1073741824 | bytes 9961472 | tf_op jit(solution)/shard_map/rsme,sen->rmn/dot_general | solution.py:39
  88.4 1.9 collective-permute-start.3
  90.4 5.0 %fusion.16 = f32[2,64,1024,1]{2,1,3,0:T(8,128)S(1)} fusion(bf16[2,8,64,512]{3,2,1,0:T(8,128)(2,1)} %collective-permute-done, bf16[8,512,1024]{2,1,0:T(8,128)(2,1)} %param.7), kind=kOutput, calls=%fused_computation.16 | convolution fusion | flops 1073741824 | bytes 9961472 | tf_op jit(solution)/shard_map/rsme,sen->rmn/dot_general | solution.py:39
  96.1 2.5 %fusion.14 = f32[2,64,1024,1]{2,1,3,0:T(8,128)S(1)} fusion(bf16[2,8,64,512]{3,2,1,0:T(8,128)(2,1)} %collective-permute-done.1, bf16[8,512,1024]{2,1,0:T(8,128)(2,1)S(1)} %bitcast.214), kind=kOutput, calls=%fused_computation.14 | convolution fusion | flops 1073741824 | bytes 9961472 | tf_op jit(solution)/shard_map/rsme,sen->rmn/dot_general | solution.py:39
  107.4 2.9 %collective-permute-start.5 = (bf16[2,8,64,512]{3,1,2,0:T(8,128)(2,1)S(1)}, bf16[2,8,64,512]{3,1,2,0:T(8,128)(2,1)S(1)}, u32[]{:S(2)}, u32[]{:S(2)}) collective-permute-start(bf16[2,8,64,512]{3,1,2,0:T(8,128)(2,1)S(1)} %bitcast.217), channel_id=1, source_target_pairs={{0,3},{1,0},{2,1},{3,2},{4,7},{5,4},{6,5},{7,6},{8,11},{9,8},{10,9... | collective-permute-start | bytes 3145736 | tf_op jit(solution)/shard_map/ppermute | solution.py:28
  110.4 5.1 %fusion.12 = f32[2,64,1024,1]{2,1,3,0:T(8,128)S(1)} fusion(bf16[8,512,1024]{2,1,0:T(8,128)(2,1)} %param.7, bf16[2,8,64,512]{3,1,2,0:T(8,128)(2,1)S(1)} %bitcast.219), kind=kOutput, calls=%fused_computation.12 | convolution fusion | flops 1073741824 | bytes 9961472 | tf_op jit(solution)/shard_map/rsme,sen->rmn/dot_general | solution.py:39
  117.2 15.3 %collective-permute-done.5 = bf16[2,8,64,512]{3,1,2,0:T(8,128)(2,1)S(1)} collective-permute-done((bf16[2,8,64,512]{3,1,2,0:T(8,128)(2,1)S(1)}, bf16[2,8,64,512]{3,1,2,0:T(8,128)(2,1)S(1)}, u32[]{:S(2)}, u32[]{:S(2)}) %collective-permute-start.5) | collective-permute-done | bytes 1048608 | tf_op jit(solution)/shard_map/ppermute | solution.py:28
  132.5 3.5 %collective-permute-done.6 = bf16[2,8,64,512]{3,1,2,0:T(8,128)(2,1)} collective-permute-done((bf16[2,8,64,512]{3,1,2,0:T(8,128)(2,1)S(1)}, bf16[2,8,64,512]{3,1,2,0:T(8,128)(2,1)}, u32[]{:S(2)}, u32[]{:S(2)}) %collective-permute-start.6) | collective-permute-done | bytes 1048608 | tf_op jit(solution)/shard_map/ppermute | solution.py:28
  136.0 5.1 %fusion.10 = f32[2,64,1024,1]{2,1,3,0:T(8,128)S(1)} fusion(bf16[8,512,1024]{2,1,0:T(8,128)(2,1)} %param.7, bf16[2,8,64,512]{3,1,2,0:T(8,128)(2,1)S(1)} %collective-permute-done.5), kind=kOutput, calls=%fused_computation.10 | convolution fusion | flops 1073741824 | bytes 9961472 | tf_op jit(solution)/shard_map/rsme,sen->rmn/dot_general | solution.py:39
  141.1 3.0 %fusion.8 = f32[2,64,1024,1]{2,1,3,0:T(8,128)S(1)} fusion(bf16[8,512,1024]{2,1,0:T(8,128)(2,1)S(1)} %bitcast.216, bf16[2,8,64,512]{3,1,2,0:T(8,128)(2,1)} %collective-permute-done.6), kind=kOutput, calls=%fused_computation.8 | convolution fusion | flops 1073741824 | bytes 9961472 | tf_op jit(solution)/shard_map/rsme,sen->rmn/dot_general | solution.py:39
  149.7 4.8 %collective-permute-done.7 = f32[8,8,1024]{2,1,0:T(8,128)S(1)} collective-permute-done((f32[8,8,1024]{2,1,0:T(8,128)}, f32[8,8,1024]{2,1,0:T(8,128)S(1)}, u32[]{:S(2)}, u32[]{:S(2)}) %collective-permute-start.7) | collective-permute-done | bytes 262176 | tf_op jit(solution)/shard_map/reduce_x/ppermute | solution.py:60
  155.9 2.8 %collective-permute-done.9 = f32[8,8,1024]{2,1,0:T(8,128)} collective-permute-done((f32[8,8,1024]{2,1,0:T(8,128)}, f32[8,8,1024]{2,1,0:T(8,128)}, u32[]{:S(2)}, u32[]{:S(2)}) %collective-permute-start.9) | collective-permute-done | bytes 262176 | tf_op jit(solution)/shard_map/reduce_x/ppermute | solution.py:60
  160.7 4.3 %all-to-all-start.2 = ((f32[8,8,1024]{2,1,0:T(8,128)}), f32[8,8,1024]{2,1,0:T(8,128)S(1)}, u32[]{:S(2)}, u32[]{:S(2)}) async-start(f32[8,8,1024]{2,1,0:T(8,128)} %copy.67), calls=%async_computation.2 | async-start | bytes 524288 | tf_op jit(solution)/shard_map/reduce_z/all_to_all | solution.py:67
  165.0 1.9 slice.28
  167.7 3.2 %collective-permute-start.12 = (bf16[1,8,64,512]{3,1,2,0:T(8,128)(2,1)}, bf16[1,8,64,512]{3,1,2,0:T(8,128)(2,1)S(1)}, u32[]{:S(2)}, u32[]{:S(2)}) collective-permute-start(bf16[1,8,64,512]{3,1,2,0:T(8,128)(2,1)} %slice.29), channel_id=1, source_target_pairs={{0,3},{1,0},{2,1},{3,2},{4,7},{5,4},{6,5},{7,6},{8,11},{9,8},{10,9... | collective-permute-start | bytes 1572872 | tf_op jit(solution)/shard_map/ppermute | solution.py:34
  170.9 4.5 %all-to-all-done.2 = f32[8,8,1024]{2,1,0:T(8,128)S(1)} async-done(((f32[8,8,1024]{2,1,0:T(8,128)}), f32[8,8,1024]{2,1,0:T(8,128)S(1)}, u32[]{:S(2)}, u32[]{:S(2)}) %all-to-all-start.2) | async-done | bytes 262176 | tf_op jit(solution)/shard_map/reduce_z/all_to_all | solution.py:67
  176.7 3.4 %collective-permute-done.11 = bf16[1,8,64,512]{3,1,2,0:T(8,128)(2,1)S(1)} collective-permute-done((bf16[1,8,64,512]{3,1,2,0:T(8,128)(2,1)}, bf16[1,8,64,512]{3,1,2,0:T(8,128)(2,1)S(1)}, u32[]{:S(2)}, u32[]{:S(2)}) %collective-permute-start.11) | collective-permute-done | bytes 524320 | tf_op jit(solution)/shard_map/ppermute | solution.py:33
  180.1 4.9 %fusion.22 = f32[2,4,8,1024]{3,2,1,0:T(8,128)S(1)} fusion(bf16[8,512,1024]{2,1,0:T(8,128)(2,1)} %param.7, bf16[2,4,8,512,8]{3,4,2,1,0:T(8,128)(2,1)S(1)} %bitcast.234), kind=kOutput, calls=%fused_computation.24 | convolution fusion | flops 536870912 | bytes 9175040 | tf_op jit(solution)/shard_map/rsme,sen->rmn/dot_general | solution.py:39
  185.1 4.9 %fusion.25 = f32[2,4,8,1024]{3,2,1,0:T(8,128)S(1)} fusion(bf16[8,512,1024]{2,1,0:T(8,128)(2,1)} %param.7, bf16[2,4,8,512,8]{3,4,2,1,0:T(8,128)(2,1)S(1)} %bitcast.233), kind=kOutput, calls=%fused_computation.25 | convolution fusion | flops 536870912 | bytes 9175040 | tf_op jit(solution)/shard_map/rsme,sen->rmn/dot_general | solution.py:39
  190.3 2.0 collective-permute-start.14
  193.9 2.4 %collective-permute-start.17 = (f32[2,8,1024]{2,1,0:T(8,128)S(1)}, f32[2,8,1024]{2,1,0:T(8,128)S(1)}, u32[]{:S(2)}, u32[]{:S(2)}) collective-permute-start(f32[2,8,1024]{2,1,0:T(8,128)S(1)} %get-tuple-element.43), channel_id=1, source_target_pairs={{0,8},{8,16},{16,24},{24,0},{1,9},{9,17},{17,25},{25,1},{2,10},{10... | collective-permute-start | bytes 196616 | tf_op jit(solution)/shard_map/reduce_x/ppermute | solution.py:60
  196.3 1.7 collective-permute-done.13
  198.0 4.7 %collective-permute-start.19 = (f32[2,8,1024]{2,1,0:T(8,128)S(1)}, f32[2,8,1024]{2,1,0:T(8,128)S(1)}, u32[]{:S(2)}, u32[]{:S(2)}) collective-permute-start(f32[2,8,1024]{2,1,0:T(8,128)S(1)} %get-tuple-element.44), channel_id=1, source_target_pairs={{0,16},{8,24},{16,0},{24,8},{1,17},{9,25},{17,1},{25,9},{2,18},{10... | collective-permute-start | bytes 196616 | tf_op jit(solution)/shard_map/reduce_x/ppermute | solution.py:60
  203.9 2.0 collective-permute-done.19
  206.8 6.9 %all-to-all-start.3 = ((f32[8,8,1024]{2,1,0:T(8,128)}), f32[8,8,1024]{2,1,0:T(8,128)S(1)}, u32[]{:S(2)}, u32[]{:S(2)}) async-start(f32[8,8,1024]{2,1,0:T(8,128)} %copy.79), calls=%async_computation.3 | async-start | bytes 524288 | tf_op jit(solution)/shard_map/reduce_z/all_to_all | solution.py:67
  213.8 11.1 %all-to-all-done.3 = f32[8,8,1024]{2,1,0:T(8,128)S(1)} async-done(((f32[8,8,1024]{2,1,0:T(8,128)}), f32[8,8,1024]{2,1,0:T(8,128)S(1)}, u32[]{:S(2)}, u32[]{:S(2)}) %all-to-all-start.3) | async-done | bytes 262176 | tf_op jit(solution)/shard_map/reduce_z/all_to_all | solution.py:67
  (89 shorter events, 36.9 us)
Async XLA Ops:
  3.3 40.8 %all-to-all-start = ((bf16[64,2,8,512]{3,2,1,0:T(8,128)(2,1)}), bf16[64,2,8,512]{3,2,1,0:T(8,128)(2,1)S(1)}, u32[]{:S(2)}, u32[]{:S(2)}) async-start(bf16[64,2,8,512]{3,2,1,0:T(8,128)(2,1)} %fusion.20), calls=%async_computation | async-start | bytes 2097152 | tf_op jit(solution)/shard_map/route/all_to_all | solution.py:22
  44.1 34.5 %all-to-all-start.1 = ((bf16[64,2,8,512]{3,2,1,0:T(8,128)(2,1)}), bf16[64,2,8,512]{3,2,1,0:T(8,128)(2,1)S(1)}, u32[]{:S(2)}, u32[]{:S(2)}) async-start(bf16[64,2,8,512]{3,2,1,0:T(8,128)(2,1)} %fusion.21), calls=%async_computation.1 | async-start | bytes 2097152 | tf_op jit(solution)/shard_map/route/all_to_all | solution.py:22
  50.4 33.7 %collective-permute-start.1 = (bf16[2,8,64,512]{3,2,1,0:T(8,128)(2,1)S(1)}, bf16[2,8,64,512]{3,2,1,0:T(8,128)(2,1)}, u32[]{:S(2)}, u32[]{:S(2)}) collective-permute-start(bf16[2,8,64,512]{3,2,1,0:T(8,128)(2,1)S(1)} %bitcast.220), channel_id=1, source_target_pairs={{0,1},{1,2},{2,3},{3,0},{4,5},{5,6},{6,7},{7,4},{8,9},{9,10},{10,1... | collective-permute-start | bytes 3145736 | tf_op jit(solution)/shard_map/ppermute | solution.py:28
  52.0 35.3 %collective-permute-start = (bf16[2,8,64,512]{3,2,1,0:T(8,128)(2,1)S(1)}, bf16[2,8,64,512]{3,2,1,0:T(8,128)(2,1)}, u32[]{:S(2)}, u32[]{:S(2)}) collective-permute-start(bf16[2,8,64,512]{3,2,1,0:T(8,128)(2,1)S(1)} %bitcast.221), channel_id=1, source_target_pairs={{0,3},{1,0},{2,1},{3,2},{4,7},{5,4},{6,5},{7,6},{8,11},{9,8},{10,9... | collective-permute-start | bytes 3145736 | tf_op jit(solution)/shard_map/ppermute | solution.py:28
  83.3 12.7 %slice-start = ((s8[8388608]{0:T(1024)(128)(4,1)}), s8[4194304]{0:T(1024)(128)(4,1)S(1)}, s32[]{:S(2)}) async-start(s8[8388608]{0:T(1024)(128)(4,1)} %bitcast.213), calls=%async_computation.4 | async-start | bytes 8388608
  85.7 14.0 %collective-permute-start.2 = (bf16[1,8,64,512]{3,2,1,0:T(8,128)(2,1)S(1)}, bf16[1,8,64,512]{3,2,1,0:T(8,128)(2,1)S(1)}, u32[]{:S(2)}, u32[]{:S(2)}) collective-permute-start(bf16[1,8,64,512]{3,2,1,0:T(8,128)(2,1)S(1)} %slice.32), channel_id=1, source_target_pairs={{0,1},{1,2},{2,3},{3,0},{4,5},{5,6},{6,7},{7,4},{8,9},{9,10},{10,1... | collective-permute-start | bytes 1572872 | tf_op jit(solution)/shard_map/ppermute | solution.py:33
  88.4 7.6 %slice-start.1 = ((s8[8388608]{0:T(1024)(128)(4,1)}), s8[4194304]{0:T(1024)(128)(4,1)S(1)}, s32[]{:S(2)}) async-start(s8[8388608]{0:T(1024)(128)(4,1)} %bitcast.213), calls=%async_computation.5 | async-start | bytes 8388608
  88.4 12.7 %collective-permute-start.3 = (bf16[1,8,64,512]{3,2,1,0:T(8,128)(2,1)S(1)}, bf16[1,8,64,512]{3,2,1,0:T(8,128)(2,1)S(1)}, u32[]{:S(2)}, u32[]{:S(2)}) collective-permute-start(bf16[1,8,64,512]{3,2,1,0:T(8,128)(2,1)S(1)} %slice.33), channel_id=1, source_target_pairs={{0,3},{1,0},{2,1},{3,2},{4,7},{5,4},{6,5},{7,6},{8,11},{9,8},{10,9... | collective-permute-start | bytes 1572872 | tf_op jit(solution)/shard_map/ppermute | solution.py:34
  106.4 9.2 %collective-permute-start.4 = (f32[8,4,8,1024]{3,2,1,0:T(8,128)}, f32[8,4,8,1024]{3,2,1,0:T(8,128)}, u32[]{:S(2)}, u32[]{:S(2)}) collective-permute-start(f32[8,4,8,1024]{3,2,1,0:T(8,128)} %get-tuple-element.37), channel_id=1, source_target_pairs={{0,4},{4,0},{1,5},{5,1},{2,6},{6,2},{3,7},{7,3},{8,12},{12,8},{9,1... | collective-permute-start | bytes 3145736 | tf_op jit(solution)/shard_map/reduce_core/ppermute | solution.py:52
  107.4 25.1 %collective-permute-start.5 = (bf16[2,8,64,512]{3,1,2,0:T(8,128)(2,1)S(1)}, bf16[2,8,64,512]{3,1,2,0:T(8,128)(2,1)S(1)}, u32[]{:S(2)}, u32[]{:S(2)}) collective-permute-start(bf16[2,8,64,512]{3,1,2,0:T(8,128)(2,1)S(1)} %bitcast.217), channel_id=1, source_target_pairs={{0,3},{1,0},{2,1},{3,2},{4,7},{5,4},{6,5},{7,6},{8,11},{9,8},{10,9... | collective-permute-start | bytes 3145736 | tf_op jit(solution)/shard_map/ppermute | solution.py:28
  110.4 25.6 %collective-permute-start.6 = (bf16[2,8,64,512]{3,1,2,0:T(8,128)(2,1)S(1)}, bf16[2,8,64,512]{3,1,2,0:T(8,128)(2,1)}, u32[]{:S(2)}, u32[]{:S(2)}) collective-permute-start(bf16[2,8,64,512]{3,1,2,0:T(8,128)(2,1)S(1)} %bitcast.218), channel_id=1, source_target_pairs={{0,1},{1,2},{2,3},{3,0},{4,5},{5,6},{6,7},{7,4},{8,9},{9,10},{10,1... | collective-permute-start | bytes 3145736 | tf_op jit(solution)/shard_map/ppermute | solution.py:28
  110.4 5.2 %copy-start.1 = (f32[8,4,8,1024]{3,2,1,0:T(8,128)S(1)}, f32[8,4,8,1024]{3,2,1,0:T(8,128)}, u32[]{:S(2)}) copy-start(f32[8,4,8,1024]{3,2,1,0:T(8,128)} %copy-done) | copy-start | bytes 3145732
  115.5 25.5 %slice-start.2 = ((s8[8388608]{0:T(1024)(128)(4,1)}), s8[4194304]{0:T(1024)(128)(4,1)S(1)}, s32[]{:S(2)}) async-start(s8[8388608]{0:T(1024)(128)(4,1)} %bitcast.215), calls=%async_computation.6 | async-start | bytes 8388608
  117.2 23.9 %slice-start.3 = ((s8[8388608]{0:T(1024)(128)(4,1)}), s8[4194304]{0:T(1024)(128)(4,1)S(1)}, s32[]{:S(2)}) async-start(s8[8388608]{0:T(1024)(128)(4,1)} %bitcast.215), calls=%async_computation.7 | async-start | bytes 8388608
  145.0 9.4 %collective-permute-start.7 = (f32[8,8,1024]{2,1,0:T(8,128)}, f32[8,8,1024]{2,1,0:T(8,128)S(1)}, u32[]{:S(2)}, u32[]{:S(2)}) collective-permute-start(f32[8,8,1024]{2,1,0:T(8,128)} %get-tuple-element.25), channel_id=1, source_target_pairs={{0,8},{8,16},{16,24},{24,0},{1,9},{9,17},{17,25},{25,1},{2,10},{10... | collective-permute-start | bytes 786440 | tf_op jit(solution)/shard_map/reduce_x/ppermute | solution.py:60
  146.4 9.5 %collective-permute-start.8 = (f32[8,8,1024]{2,1,0:T(8,128)}, f32[8,8,1024]{2,1,0:T(8,128)}, u32[]{:S(2)}, u32[]{:S(2)}) collective-permute-start(f32[8,8,1024]{2,1,0:T(8,128)} %get-tuple-element.27), channel_id=1, source_target_pairs={{0,24},{8,0},{16,8},{24,16},{1,25},{9,1},{17,9},{25,17},{2,26},{10... | collective-permute-start | bytes 786440 | tf_op jit(solution)/shard_map/reduce_x/ppermute | solution.py:60
  147.0 11.7 %collective-permute-start.9 = (f32[8,8,1024]{2,1,0:T(8,128)}, f32[8,8,1024]{2,1,0:T(8,128)}, u32[]{:S(2)}, u32[]{:S(2)}) collective-permute-start(f32[8,8,1024]{2,1,0:T(8,128)} %get-tuple-element.26), channel_id=1, source_target_pairs={{0,16},{8,24},{16,0},{24,8},{1,17},{9,25},{17,1},{25,9},{2,18},{10... | collective-permute-start | bytes 786440 | tf_op jit(solution)/shard_map/reduce_x/ppermute | solution.py:60
  149.7 25.8 %collective-permute-start.10 = (f32[6,4,8,1024]{3,2,1,0:T(8,128)}, f32[6,4,8,1024]{3,2,1,0:T(8,128)}, u32[]{:S(2)}, u32[]{:S(2)}) collective-permute-start(f32[6,4,8,1024]{3,2,1,0:T(8,128)} %pad_maximum_fusion), channel_id=1, source_target_pairs={{0,4},{4,0},{1,5},{5,1},{2,6},{6,2},{3,7},{7,3},{8,12},{12,8},{9,1... | collective-permute-start | bytes 2359304 | tf_op jit(solution)/shard_map/reduce_core/ppermute | solution.py:52
  160.7 14.7 %all-to-all-start.2 = ((f32[8,8,1024]{2,1,0:T(8,128)}), f32[8,8,1024]{2,1,0:T(8,128)S(1)}, u32[]{:S(2)}, u32[]{:S(2)}) async-start(f32[8,8,1024]{2,1,0:T(8,128)} %copy.67), calls=%async_computation.2 | async-start | bytes 524288 | tf_op jit(solution)/shard_map/reduce_z/all_to_all | solution.py:67
  167.7 12.4 %collective-permute-start.11 = (bf16[1,8,64,512]{3,1,2,0:T(8,128)(2,1)}, bf16[1,8,64,512]{3,1,2,0:T(8,128)(2,1)S(1)}, u32[]{:S(2)}, u32[]{:S(2)}) collective-permute-start(bf16[1,8,64,512]{3,1,2,0:T(8,128)(2,1)} %slice.28), channel_id=1, source_target_pairs={{0,1},{1,2},{2,3},{3,0},{4,5},{5,6},{6,7},{7,4},{8,9},{9,10},{10,1... | collective-permute-start | bytes 1572872 | tf_op jit(solution)/shard_map/ppermute | solution.py:33
  167.7 12.4 %collective-permute-start.12 = (bf16[1,8,64,512]{3,1,2,0:T(8,128)(2,1)}, bf16[1,8,64,512]{3,1,2,0:T(8,128)(2,1)S(1)}, u32[]{:S(2)}, u32[]{:S(2)}) collective-permute-start(bf16[1,8,64,512]{3,1,2,0:T(8,128)(2,1)} %slice.29), channel_id=1, source_target_pairs={{0,3},{1,0},{2,1},{3,2},{4,7},{5,4},{6,5},{7,6},{8,11},{9,8},{10,9... | collective-permute-start | bytes 1572872 | tf_op jit(solution)/shard_map/ppermute | solution.py:34
  185.1 40.0 %copy-start.2 = (bf16[16,1024]{1,0:T(8,128)(2,1)S(1)}, bf16[16,1024]{1,0:T(8,128)(2,1)}, u32[]{:S(2)}) copy-start(bf16[16,1024]{1,0:T(8,128)(2,1)} %param.9) | copy-start | bytes 98308
  185.1 40.0 %copy-start.3 = (f32[1024]{0:T(1024)S(1)}, f32[1024]{0:T(1024)}, u32[]{:S(2)}) copy-start(f32[1024]{0:T(1024)} %param.11) | copy-start | bytes 12292
  185.1 40.0 %copy-start.4 = (f32[16]{0:T(128)S(1)}, f32[16]{0:T(128)}, u32[]{:S(2)}) copy-start(f32[16]{0:T(128)} %param.10) | copy-start | bytes 196
  190.1 3.7 %collective-permute-start.16 = (f32[2,4,8,1024]{3,2,1,0:T(8,128)S(1)}, f32[2,4,8,1024]{3,2,1,0:T(8,128)S(1)}, u32[]{:S(2)}, u32[]{:S(2)}) collective-permute-start(f32[2,4,8,1024]{3,2,1,0:T(8,128)S(1)} %pad_maximum_fusion.1), channel_id=1, source_target_pairs={{0,4},{4,0},{1,5},{5,1},{2,6},{6,2},{3,7},{7,3},{8,12},{12,8},{9,1... | collective-permute-start | bytes 786440 | tf_op jit(solution)/shard_map/reduce_core/ppermute | solution.py:52
  190.3 7.8 %collective-permute-start.13 = (f32[6,8,1024]{2,1,0:T(8,128)S(1)}, f32[6,8,1024]{2,1,0:T(8,128)S(1)}, u32[]{:S(2)}, u32[]{:S(2)}) collective-permute-start(f32[6,8,1024]{2,1,0:T(8,128)S(1)} %get-tuple-element.28), channel_id=1, source_target_pairs={{0,8},{8,16},{16,24},{24,0},{1,9},{9,17},{17,25},{25,1},{2,10},{10... | collective-permute-start | bytes 589832 | tf_op jit(solution)/shard_map/reduce_x/ppermute | solution.py:60
  190.3 12.4 %collective-permute-start.14 = (f32[6,8,1024]{2,1,0:T(8,128)S(1)}, f32[6,8,1024]{2,1,0:T(8,128)S(1)}, u32[]{:S(2)}, u32[]{:S(2)}) collective-permute-start(f32[6,8,1024]{2,1,0:T(8,128)S(1)} %get-tuple-element.30), channel_id=1, source_target_pairs={{0,24},{8,0},{16,8},{24,16},{1,25},{9,1},{17,9},{25,17},{2,26},{10... | collective-permute-start | bytes 589832 | tf_op jit(solution)/shard_map/reduce_x/ppermute | solution.py:60
  192.4 11.4 %collective-permute-start.15 = (f32[6,8,1024]{2,1,0:T(8,128)S(1)}, f32[6,8,1024]{2,1,0:T(8,128)S(1)}, u32[]{:S(2)}, u32[]{:S(2)}) collective-permute-start(f32[6,8,1024]{2,1,0:T(8,128)S(1)} %get-tuple-element.29), channel_id=1, source_target_pairs={{0,16},{8,24},{16,0},{24,8},{1,17},{9,25},{17,1},{25,9},{2,18},{10... | collective-permute-start | bytes 589832 | tf_op jit(solution)/shard_map/reduce_x/ppermute | solution.py:60
  193.9 10.0 %collective-permute-start.17 = (f32[2,8,1024]{2,1,0:T(8,128)S(1)}, f32[2,8,1024]{2,1,0:T(8,128)S(1)}, u32[]{:S(2)}, u32[]{:S(2)}) collective-permute-start(f32[2,8,1024]{2,1,0:T(8,128)S(1)} %get-tuple-element.43), channel_id=1, source_target_pairs={{0,8},{8,16},{16,24},{24,0},{1,9},{9,17},{17,25},{25,1},{2,10},{10... | collective-permute-start | bytes 196616 | tf_op jit(solution)/shard_map/reduce_x/ppermute | solution.py:60
  196.3 7.6 %collective-permute-start.18 = (f32[2,8,1024]{2,1,0:T(8,128)S(1)}, f32[2,8,1024]{2,1,0:T(8,128)S(1)}, u32[]{:S(2)}, u32[]{:S(2)}) collective-permute-start(f32[2,8,1024]{2,1,0:T(8,128)S(1)} %get-tuple-element.45), channel_id=1, source_target_pairs={{0,24},{8,0},{16,8},{24,16},{1,25},{9,1},{17,9},{25,17},{2,26},{10... | collective-permute-start | bytes 196616 | tf_op jit(solution)/shard_map/reduce_x/ppermute | solution.py:60
  198.0 7.9 %collective-permute-start.19 = (f32[2,8,1024]{2,1,0:T(8,128)S(1)}, f32[2,8,1024]{2,1,0:T(8,128)S(1)}, u32[]{:S(2)}, u32[]{:S(2)}) collective-permute-start(f32[2,8,1024]{2,1,0:T(8,128)S(1)} %get-tuple-element.44), channel_id=1, source_target_pairs={{0,16},{8,24},{16,0},{24,8},{1,17},{9,25},{17,1},{25,9},{2,18},{10... | collective-permute-start | bytes 196616 | tf_op jit(solution)/shard_map/reduce_x/ppermute | solution.py:60
  206.8 18.1 %all-to-all-start.3 = ((f32[8,8,1024]{2,1,0:T(8,128)}), f32[8,8,1024]{2,1,0:T(8,128)S(1)}, u32[]{:S(2)}, u32[]{:S(2)}) async-start(f32[8,8,1024]{2,1,0:T(8,128)} %copy.79), calls=%async_computation.3 | async-start | bytes 524288 | tf_op jit(solution)/shard_map/reduce_z/all_to_all | solution.py:67
  (1 other events, 1.0 us)

commit v3 on v1

v3 whole, which is shorter than its diff:
```python
import jax
import jax.numpy as jnp
from jax import lax
from jax.experimental import pallas as pl
from jax.experimental.pallas import tpu as pltpu
from jax.sharding import Mesh, PartitionSpec as P

NZ, NX, NC, NY = 8, 4, 2, 4
LANES = 128


def ring(size, shift):
    return [(i, (i + shift) % size) for i in range(size)]


def after_that(earlier, *values):
    return lax.optimization_barrier((earlier,) + values)[1:]


def gather_rows(amp_rows, picker):
    with jax.named_scope("pick"):
        return jnp.einsum(
            "tsg,rgb->trsb", picker, amp_rows, preferred_element_type=jnp.float32
        ).astype(jnp.bfloat16)


def route(outgoing):
    tiles, rows, cap, width = outgoing.shape
    with jax.named_scope("route"):
        routed = lax.all_to_all(outgoing, ("z", "x", "core"), 0, 0, tiled=True)
    routed = routed.reshape(NZ, NX, NC, rows, cap, width)
    routed = routed.transpose(3, 4, 2, 1, 0, 5).reshape(rows, cap, tiles, width)
    return lax.optimization_barrier(routed)


def neighbours(own):
    return lax.ppermute(own, "y", ring(NY, -1)), lax.ppermute(own, "y", ring(NY, 1))


def opposite(after, before):
    half = after.shape[0] // 2
    low = lax.ppermute(before[:half], "y", ring(NY, 1))
    high = lax.ppermute(after[half:], "y", ring(NY, -1))
    return low, high


def product(parts, integrals):
    cap, width, n = integrals.shape
    tiles = parts[0].shape[2]
    total = sum(part.shape[0] for part in parts)
    group = 2

    def body(*refs):
        *row_refs, integral_ref, out_ref = refs
        value = None
        for j in range(group):
            rows = jnp.concatenate([ref[:, j] for ref in row_refs]).reshape(total * tiles, width)
            term = jnp.dot(rows, integral_ref[j], preferred_element_type=jnp.float32)
            value = term if value is None else value + term
        value = value.reshape(total, tiles, n)

        @pl.when(pl.program_id(0) == 0)
        def _():
            out_ref[...] = value

        @pl.when(pl.program_id(0) > 0)
        def _():
            out_ref[...] += value

    return pl.pallas_call(
        body,
        grid=(cap // group,),
        out_shape=jax.ShapeDtypeStruct((total, tiles, n), jnp.float32),
        in_specs=[
            pl.BlockSpec((part.shape[0], group, tiles, width), lambda i: (0, i, 0, 0))
            for part in parts
        ]
        + [pl.BlockSpec((group, width, n), lambda i: (i, 0, 0))],
        out_specs=pl.BlockSpec((total, tiles, n), lambda i: (0, 0, 0)),
        compiler_params=pltpu.CompilerParams(vmem_limit_bytes=56 << 20),
        cost_estimate=pl.CostEstimate(
            flops=2 * total * tiles * cap * width * n,
            bytes_accessed=2 * cap * width * (n + total * tiles) + 4 * total * tiles * n,
            transcendentals=0,
        ),
        name="product",
    )(*parts, integrals)


def pick(array, index, axis):
    return lax.dynamic_index_in_dim(array, index, axis, keepdims=False)


def over_core(partial):
    core = lax.axis_index("core")
    rows, _, n = partial.shape
    partial = partial.reshape(rows, NC, NX, NZ, n)
    with jax.named_scope("reduce_core"):
        away = lax.ppermute(pick(partial, 1 - core, 1), "core", ring(NC, 1))
        summed = pick(partial, core, 1) + away
        summed = summed.reshape(rows, NX, NZ, n // LANES, LANES)
        return summed.transpose(2, 1, 0, 3, 4).reshape(NZ * NX, -1, LANES)


def over_zx(outgoing):
    with jax.named_scope("reduce_zx"):
        return jnp.sum(lax.all_to_all(outgoing, ("z", "x"), 0, 0, tiled=True), axis=0)


def per_device(amplitudes, integrals, slot_block, rest, occ_energy, vir_energy):
    nblocks = amplitudes.shape[1]
    cap = integrals.shape[0]
    n = integrals.shape[2]
    picker = (slot_block[:, None] == jnp.arange(nblocks, dtype=jnp.int32)[None, :]).astype(
        jnp.bfloat16
    )
    picker = picker.reshape(-1, cap, nblocks)
    step = amplitudes.shape[0] // 2

    outgoing = gather_rows(amplitudes[:step], picker)
    outgoing_later = gather_rows(amplitudes[step:], picker)
    own = route(outgoing)
    (outgoing_later,) = after_that(own, outgoing_later)
    after, before = neighbours(own)
    later = route(outgoing_later)
    low, high = opposite(*after_that(later, after, before))
    early = product([own, after, before, later], integrals)
    early = over_core(*after_that((low, high), early))
    after_later, before_later = neighbours(later)
    low_later, high_later = opposite(after_later, before_later)
    early = over_zx(early)
    low, high, low_later, high_later = after_that(early, low, high, low_later, high_later)
    late = [low, high, after_later, low_later, high_later, before_later]
    late = over_zx(over_core(product(late, integrals)))

    early = early.reshape(4, step, n)
    late = late.reshape(4, step, n)
    own, after, before, later = (early[i] for i in range(4))
    across, after_later, across_later, before_later = (late[i] for i in range(4))
    relative = jnp.concatenate(
        [own, later, after, after_later, across, across_later, before, before_later]
    ).reshape(NY, 2 * step, n)
    k = lax.axis_index("y")
    doubled = jnp.concatenate([relative, relative], axis=0)
    ladder = lax.dynamic_slice_in_dim(doubled, (NY - k) % NY, NY, 0).reshape(rest.shape)
    denominator = vir_energy[None, :] - occ_energy[:, None]
    return ((rest.astype(jnp.float32) + ladder) / denominator).astype(jnp.bfloat16)


def solution(mesh):
    grid = Mesh(mesh.devices.reshape(NZ, NX, NC, NY), ("z", "x", "core", "y"))
    tile = ("z", "x", "core")
    in_specs = (
        P(tile + ("y",), None, None),
        P(tile, None, "y"),
        P(),
        P(tile, "y"),
        P(tile),
        P("y"),
    )
    return jax.shard_map(
        per_device, mesh=grid, in_specs=in_specs, out_specs=P(tile, "y"), check_vma=False
    )
```

time: 203 us -> 208 us (1.025)
  matrix products: 30 us -> 3.99 us
  Pallas kernels: 0 us -> 19.2 us
  starting transfers between devices: 43.1 us -> 49.5 us
    dot_general x12 -> x2, matrix products: 30 us -> 3.99 us  [gather_rows(): jnp.einsum('tsg,rgb->trsb', picker, amp_rows, preferred_element_type=jnp....]
    ppermute x10, waiting for transfers between devices: 19 us -> 39.2 us  [the longest x2 22.7 us: neighbours(): lax.ppermute(own, 'y', ring(NY, 1))]
    pallas_call x0 -> x2, Pallas kernels: none -> 19.2 us  [product(): pl.pallas_call(body, grid=(cap // group,), out_shape=jax.ShapeDtypeStruct...]
    all_to_all x2, waiting for transfers between devices: 47.4 us -> 28.3 us  [over_zx(): lax.all_to_all(outgoing, ('z', 'x'), 0, 0, tiled=True)]
    all_to_all x2, starting transfers between devices: 11.9 us -> 18.4 us  [over_zx(): lax.all_to_all(outgoing, ('z', 'x'), 0, 0, tiled=True)]
    transpose x4 -> x0, local copies, waits for them, and re-layouts: 5.34 us -> none  [the longest x2 3.21 us: reduce_tiles(): outgoing = summed.transpose(2, 1, 0, 3).reshape(NZ * NX, rows, n)]
    reshape x2 -> x5, local copies, waits for them, and re-layouts: 0.05 us -> 4.58 us  [the longest x2 2.42 us: over_core(): summed = summed.reshape(rows, NX, NZ, n // LANES, LANES)]
    squeeze x2 -> x10, local copies, waits for them, and re-layouts: 0.16 us -> 2.86 us  [the longest x2 2.77 us: pick(): return lax.dynamic_index_in_dim(array, index, axis, keepdims=False)]
  transfers between devices with their start and end apart: 14 -> 14, of which waited for: 8 -> 10; matrix products, arithmetic and copies ran while one was open for 17% -> 2% of each run, Pallas kernels for 0% -> 5%
where the time goes in v3:
time: 208 us; the launch traced here: 207 us
  waiting for transfers between devices  120 us (58%)
  starting transfers between devices  49.5 us (24%)
  Pallas kernels  19.2 us (9%)
  local copies, waits for them, and re-layouts  11.5 us (6%)
  matrix products  3.99 us (2%)
  other arithmetic  2.43 us (1%)
    all_to_all x2, waiting for transfers between devices, route(): routed = lax.all_to_all(outgoing, ('z', 'x', 'core'), 0, 0, tiled=True)  53 us
    all_to_all x2, waiting for transfers between devices, over_zx(): lax.all_to_all(outgoing, ('z', 'x'), 0, 0, tiled=True)  28.3 us
    ppermute x2, waiting for transfers between devices, neighbours(): lax.ppermute(own, 'y', ring(NY, 1))  22.7 us
    pallas_call x2, Pallas kernels, product(): pl.pallas_call(body, grid=(cap // group,), out_shape=jax.ShapeDtypeStruct...  19.2 us
    all_to_all x2, starting transfers between devices, over_zx(): lax.all_to_all(outgoing, ('z', 'x'), 0, 0, tiled=True)  18.4 us
    all_to_all x2, starting transfers between devices, route(): routed = lax.all_to_all(outgoing, ('z', 'x', 'core'), 0, 0, tiled=True)  17.7 us
    ppermute x2, waiting for transfers between devices, opposite(): low = lax.ppermute(before[:half], 'y', ring(NY, 1))  10.7 us
    ppermute x2, starting transfers between devices, neighbours(): lax.ppermute(own, 'y', ring(NY, -1))  6.31 us
  transfers between devices with their start and end apart: 14, of which 10 were waited for; matrix products, arithmetic and copies ran while one was open for 2% of the time, Pallas kernels for 5%

profile of v3, /device:TPU:2, one launch (start us, length us, event | category | flops | bytes accessed | tf_op | source)
XLA Modules:
  0.0 207.4 jit_solution(13319667473849663000)
XLA Ops:
  0.0 0.9 eq.18
  0.9 2.5 %fusion = bf16[64,2,8,512]{3,2,1,0:T(8,128)(2,1)} fusion(bf16[4,256,512]{2,1,0:T(8,128)(2,1)} %param.6, s32[64,8]{1,0:T(8,128)S(1)} %eq.18), kind=kOutput, calls=%fused_computation.2 | convolution fusion | flops 269090816 | bytes 1574912 | tf_op jit(solution)/shard_map/pick/tsg,rgb->trsb/dot_general | solution.py:22
  3.3 12.0 %all-to-all-start = ((bf16[64,2,8,512]{3,2,1,0:T(8,128)(2,1)}), bf16[64,2,8,512]{3,2,1,0:T(8,128)(2,1)S(1)}, u32[]{:S(2)}, u32[]{:S(2)}) async-start(bf16[64,2,8,512]{3,2,1,0:T(8,128)(2,1)} %fusion), calls=%async_computation | async-start | bytes 2097152 | tf_op jit(solution)/shard_map/route/all_to_all | solution.py:30
  15.4 1.5 fusion.1
  16.9 27.3 %all-to-all-done = bf16[64,2,8,512]{3,2,1,0:T(8,128)(2,1)S(1)} async-done(((bf16[64,2,8,512]{3,2,1,0:T(8,128)(2,1)}), bf16[64,2,8,512]{3,2,1,0:T(8,128)(2,1)S(1)}, u32[]{:S(2)}, u32[]{:S(2)}) %all-to-all-start) | async-done | bytes 1048608 | tf_op jit(solution)/shard_map/route/all_to_all | solution.py:30
  44.2 0.6 copy.11
  44.8 5.7 %all-to-all-start.1 = ((bf16[64,2,8,512]{3,2,1,0:T(8,128)(2,1)}), bf16[64,2,8,512]{3,2,1,0:T(8,128)(2,1)S(1)}, u32[]{:S(2)}, u32[]{:S(2)}) async-start(bf16[64,2,8,512]{3,2,1,0:T(8,128)(2,1)} %fusion.1), calls=%async_computation.1 | async-start | bytes 2097152 | tf_op jit(solution)/shard_map/route/all_to_all | solution.py:30
  50.4 3.1 %collective-permute-start = (bf16[2,8,64,512]{3,2,1,0:T(8,128)(2,1)S(1)}, bf16[2,8,64,512]{3,2,1,0:T(8,128)(2,1)S(1)}, u32[]{:S(2)}, u32[]{:S(2)}) collective-permute-start(bf16[2,8,64,512]{3,2,1,0:T(8,128)(2,1)S(1)} %bitcast.65), channel_id=1, source_target_pairs={{0,3},{1,0},{2,1},{3,2},{4,7},{5,4},{6,5},{7,6},{8,11},{9,8},{10,9... | collective-permute-start | bytes 3145736 | tf_op jit(solution)/shard_map/ppermute | solution.py:37
  53.5 25.7 %all-to-all-done.1 = bf16[64,2,8,512]{3,2,1,0:T(8,128)(2,1)S(1)} async-done(((bf16[64,2,8,512]{3,2,1,0:T(8,128)(2,1)}), bf16[64,2,8,512]{3,2,1,0:T(8,128)(2,1)S(1)}, u32[]{:S(2)}, u32[]{:S(2)}) %all-to-all-start.1) | async-done | bytes 1048608 | tf_op jit(solution)/shard_map/route/all_to_all | solution.py:30
  79.2 1.6 copy.12
  80.8 1.5 slice.52
  82.3 1.7 collective-permute-start.2
  84.0 1.7 collective-permute-start.3
  85.7 9.6 %product.2 = f32[8,64,1024]{2,1,0:T(8,128)} custom-call(bf16[2,8,64,512]{3,2,1,0:T(8,128)(2,1)} %bitcast.67, bf16[2,8,64,512]{3,2,1,0:T(8,128)(2,1)} %copy-done.5, bf16[2,8,64,512]{3,2,1,0:T(8,128)(2,1)} %collective-permute-done.1.refs_2_, bf16[2,8,64,512]{3,2,1,0:T(8,128)(2,1)} %bitcast.62, bf16[8,512,1024]{2,1,0:T(8,128)(2,1)} %refs_6_.1), custom_call_target="tpu_custom_call" | custom-call | flops 4294967296 | bytes 14680064 | tf_op jit(solution)/shard_map/product/pallas_call | solution.py:70
  95.3 1.1 collective-permute-done.2.refs_0_
  96.5 1.3 dynamic-slice_bitcast_fusion.1
  98.0 2.8 %collective-permute-done.4 = f32[8,4,8,1024]{3,2,1,0:T(8,128)} collective-permute-done((f32[8,4,8,1024]{3,2,1,0:T(8,128)S(1)}, f32[8,4,8,1024]{3,2,1,0:T(8,128)}, u32[]{:S(2)}, u32[]{:S(2)}) %collective-permute-start.4) | collective-permute-done | bytes 1048608 | tf_op jit(solution)/shard_map/reduce_core/ppermute | solution.py:99
  100.7 1.4 fusion.3
  102.1 1.2 copy.15
  103.3 8.4 %all-to-all-start.2 = ((f32[32,64,128]{2,1,0:T(8,128)}), f32[32,64,128]{2,1,0:T(8,128)S(1)}, u32[]{:S(2)}, u32[]{:S(2)}) async-start(f32[32,64,128]{2,1,0:T(8,128)} %bitcast.18), calls=%async_computation.2 | async-start | bytes 2097152 | tf_op jit(solution)/shard_map/reduce_zx/all_to_all | solution.py:107
  111.9 3.2 %collective-permute-start.7 = (bf16[2,8,64,512]{3,2,1,0:T(8,128)(2,1)S(1)}, bf16[2,8,64,512]{3,2,1,0:T(8,128)(2,1)S(1)}, u32[]{:S(2)}, u32[]{:S(2)}) collective-permute-start(bf16[2,8,64,512]{3,2,1,0:T(8,128)(2,1)S(1)} %bitcast.64), channel_id=1, source_target_pairs={{0,3},{1,0},{2,1},{3,2},{4,7},{5,4},{6,5},{7,6},{8,11},{9,8},{10,9... | collective-permute-start | bytes 3145736 | tf_op jit(solution)/shard_map/ppermute | solution.py:37
  115.1 22.7 %collective-permute-done.5.refs_5_ = bf16[2,8,64,512]{3,2,1,0:T(8,128)(2,1)S(1)} collective-permute-done((bf16[2,8,64,512]{3,2,1,0:T(8,128)(2,1)S(1)}, bf16[2,8,64,512]{3,2,1,0:T(8,128)(2,1)S(1)}, u32[]{:S(2)}, u32[]{:S(2)}) %collective-permute-start.5) | collective-permute-done | bytes 1048608 | tf_op jit(solution)/shard_map/ppermute | solution.py:37
  138.2 0.6 copy-done.6
  139.1 3.2 %collective-permute-start.8 = (bf16[1,8,64,512]{3,2,1,0:T(8,128)(2,1)S(1)}, bf16[1,8,64,512]{3,2,1,0:T(8,128)(2,1)}, u32[]{:S(2)}, u32[]{:S(2)}) collective-permute-start(bf16[1,8,64,512]{3,2,1,0:T(8,128)(2,1)S(1)} %slice.68), channel_id=1, source_target_pairs={{0,3},{1,0},{2,1},{3,2},{4,7},{5,4},{6,5},{7,6},{8,11},{9,8},{10,9... | collective-permute-start | bytes 1572872 | tf_op jit(solution)/shard_map/ppermute | solution.py:43
  142.4 9.5 %collective-permute-done.6.refs_3_ = bf16[1,8,64,512]{3,2,1,0:T(8,128)(2,1)S(1)} collective-permute-done((bf16[1,8,64,512]{3,2,1,0:T(8,128)(2,1)S(1)}, bf16[1,8,64,512]{3,2,1,0:T(8,128)(2,1)S(1)}, u32[]{:S(2)}, u32[]{:S(2)}) %collective-permute-start.6) | collective-permute-done | bytes 524320 | tf_op jit(solution)/shard_map/ppermute | solution.py:42
  152.8 9.6 %product.3 = f32[8,64,1024]{2,1,0:T(8,128)} custom-call(bf16[1,8,64,512]{3,2,1,0:T(8,128)(2,1)} %collective-permute-done.2.refs_0_, bf16[1,8,64,512]{3,2,1,0:T(8,128)(2,1)} %collective-permute-done.3.refs_1_, bf16[2,8,64,512]{3,2,1,0:T(8,128)(2,1)} %copy-done.7, bf16[1,8,64,512]{3,2,1,0:T(8,128)(2,1)} %copy-done.11, ...), custom_call_target="tpu_custom_call" | custom-call | flops 4294967296 | bytes 14680064 | tf_op jit(solution)/shard_map/product/pallas_call | solution.py:70
  162.4 1.5 dynamic-slice_bitcast_fusion
  164.0 2.6 %collective-permute-done.9 = f32[8,4,8,1024]{3,2,1,0:T(8,128)S(1)} collective-permute-done((f32[8,4,8,1024]{3,2,1,0:T(8,128)S(1)}, f32[8,4,8,1024]{3,2,1,0:T(8,128)S(1)}, u32[]{:S(2)}, u32[]{:S(2)}) %collective-permute-start.9) | collective-permute-done | bytes 1048608 | tf_op jit(solution)/shard_map/reduce_core/ppermute | solution.py:99
  166.8 1.2 copy.18
  168.0 9.9 %all-to-all-start.3 = ((f32[32,64,128]{2,1,0:T(8,128)}), f32[32,64,128]{2,1,0:T(8,128)S(1)}, u32[]{:S(2)}, u32[]{:S(2)}) async-start(f32[32,64,128]{2,1,0:T(8,128)} %bitcast.24), calls=%async_computation.3 | async-start | bytes 2097152 | tf_op jit(solution)/shard_map/reduce_zx/all_to_all | solution.py:107
  178.0 28.3 %all-to-all-done.3 = f32[32,64,128]{2,1,0:T(8,128)S(1)} async-done(((f32[32,64,128]{2,1,0:T(8,128)}), f32[32,64,128]{2,1,0:T(8,128)S(1)}, u32[]{:S(2)}, u32[]{:S(2)}) %all-to-all-start.3) | async-done | bytes 1048608 | tf_op jit(solution)/shard_map/reduce_zx/all_to_all | solution.py:107
  206.7 0.7 divide_convert_fusion
  (54 shorter events, 2.6 us)
Async XLA Ops:
  0.0 15.4 %copy-start.2 = (bf16[4,256,512]{2,1,0:T(8,128)(2,1)S(1)}, bf16[4,256,512]{2,1,0:T(8,128)(2,1)}, u32[]{:S(2)}) copy-start(bf16[4,256,512]{2,1,0:T(8,128)(2,1)} %param.6) | copy-start | bytes 3145732
  3.3 40.8 %all-to-all-start = ((bf16[64,2,8,512]{3,2,1,0:T(8,128)(2,1)}), bf16[64,2,8,512]{3,2,1,0:T(8,128)(2,1)S(1)}, u32[]{:S(2)}, u32[]{:S(2)}) async-start(bf16[64,2,8,512]{3,2,1,0:T(8,128)(2,1)} %fusion), calls=%async_computation | async-start | bytes 2097152 | tf_op jit(solution)/shard_map/route/all_to_all | solution.py:30
  44.8 36.0 %copy-start.4 = (bf16[8,4,2,2,8,512]{5,0,1,2,4,3:T(8,128)(2,1)}, bf16[8,4,2,2,8,512]{5,0,1,2,4,3:T(8,128)(2,1)S(1)}, u32[]{:S(2)}) copy-start(bf16[8,4,2,2,8,512]{5,0,1,2,4,3:T(8,128)(2,1)S(1)} %copy.11) | copy-start | bytes 3145732
  44.8 34.5 %all-to-all-start.1 = ((bf16[64,2,8,512]{3,2,1,0:T(8,128)(2,1)}), bf16[64,2,8,512]{3,2,1,0:T(8,128)(2,1)S(1)}, u32[]{:S(2)}, u32[]{:S(2)}) async-start(bf16[64,2,8,512]{3,2,1,0:T(8,128)(2,1)} %fusion.1), calls=%async_computation.1 | async-start | bytes 2097152 | tf_op jit(solution)/shard_map/route/all_to_all | solution.py:30
  50.4 30.4 %collective-permute-start = (bf16[2,8,64,512]{3,2,1,0:T(8,128)(2,1)S(1)}, bf16[2,8,64,512]{3,2,1,0:T(8,128)(2,1)S(1)}, u32[]{:S(2)}, u32[]{:S(2)}) collective-permute-start(bf16[2,8,64,512]{3,2,1,0:T(8,128)(2,1)S(1)} %bitcast.65), channel_id=1, source_target_pairs={{0,3},{1,0},{2,1},{3,2},{4,7},{5,4},{6,5},{7,6},{8,11},{9,8},{10,9... | collective-permute-start | bytes 3145736 | tf_op jit(solution)/shard_map/ppermute | solution.py:37
  53.5 27.3 %collective-permute-start.1 = (bf16[2,8,64,512]{3,2,1,0:T(8,128)(2,1)S(1)}, bf16[2,8,64,512]{3,2,1,0:T(8,128)(2,1)}, u32[]{:S(2)}, u32[]{:S(2)}) collective-permute-start(bf16[2,8,64,512]{3,2,1,0:T(8,128)(2,1)S(1)} %bitcast.66), channel_id=1, source_target_pairs={{0,1},{1,2},{2,3},{3,0},{4,5},{5,6},{6,7},{7,4},{8,9},{9,10},{10,1... | collective-permute-start | bytes 3145736 | tf_op jit(solution)/shard_map/ppermute | solution.py:37
  80.8 4.9 %copy-start.5 = (bf16[2,8,64,512]{3,2,1,0:T(8,128)(2,1)}, bf16[2,8,64,512]{3,2,1,0:T(8,128)(2,1)S(1)}, u32[]{:S(2)}) copy-start(bf16[2,8,64,512]{3,2,1,0:T(8,128)(2,1)S(1)} %collective-permute-done.refs_1_) | copy-start | bytes 3145732
  82.3 14.1 %collective-permute-start.2 = (bf16[1,8,64,512]{3,2,1,0:T(8,128)(2,1)S(1)}, bf16[1,8,64,512]{3,2,1,0:T(8,128)(2,1)}, u32[]{:S(2)}, u32[]{:S(2)}) collective-permute-start(bf16[1,8,64,512]{3,2,1,0:T(8,128)(2,1)S(1)} %slice.52), channel_id=1, source_target_pairs={{0,1},{1,2},{2,3},{3,0},{4,5},{5,6},{6,7},{7,4},{8,9},{9,10},{10,1... | collective-permute-start | bytes 1572872 | tf_op jit(solution)/shard_map/ppermute | solution.py:42
  84.0 12.6 %collective-permute-start.3 = (bf16[1,8,64,512]{3,2,1,0:T(8,128)(2,1)S(1)}, bf16[1,8,64,512]{3,2,1,0:T(8,128)(2,1)}, u32[]{:S(2)}, u32[]{:S(2)}) collective-permute-start(bf16[1,8,64,512]{3,2,1,0:T(8,128)(2,1)S(1)} %slice.53), channel_id=1, source_target_pairs={{0,3},{1,0},{2,1},{3,2},{4,7},{5,4},{6,5},{7,6},{8,11},{9,8},{10,9... | collective-permute-start | bytes 1572872 | tf_op jit(solution)/shard_map/ppermute | solution.py:43
  95.3 5.5 %copy-start = (f32[8,64,1024]{2,1,0:T(8,128)S(1)}, f32[8,64,1024]{2,1,0:T(8,128)}, u32[]{:S(2)}) copy-start(f32[8,64,1024]{2,1,0:T(8,128)} %product.2) | copy-start | bytes 6291460
  97.8 2.9 %collective-permute-start.4 = (f32[8,4,8,1024]{3,2,1,0:T(8,128)S(1)}, f32[8,4,8,1024]{3,2,1,0:T(8,128)}, u32[]{:S(2)}, u32[]{:S(2)}) collective-permute-start(f32[8,4,8,1024]{3,2,1,0:T(8,128)S(1)} %dynamic-slice_bitcast_fusion.1), channel_id=1, source_target_pairs={{0,4},{4,0},{1,5},{5,1},{2,6},{6,2},{3,7},{7,3},{8,12},{12,8},{9,1... | collective-permute-start | bytes 3145736 | tf_op jit(solution)/shard_map/reduce_core/ppermute | solution.py:99
  102.1 9.7 %copy-start.3 = (bf16[8,4,2,2,8,512]{5,0,1,2,4,3:T(8,128)(2,1)S(1)}, bf16[8,4,2,2,8,512]{5,0,1,2,4,3:T(8,128)(2,1)}, u32[]{:S(2)}) copy-start(bf16[8,4,2,2,8,512]{5,0,1,2,4,3:T(8,128)(2,1)} %copy.12) | copy-start | bytes 3145732
  103.3 39.0 %all-to-all-start.2 = ((f32[32,64,128]{2,1,0:T(8,128)}), f32[32,64,128]{2,1,0:T(8,128)S(1)}, u32[]{:S(2)}, u32[]{:S(2)}) async-start(f32[32,64,128]{2,1,0:T(8,128)} %bitcast.18), calls=%async_computation.2 | async-start | bytes 2097152 | tf_op jit(solution)/shard_map/reduce_zx/all_to_all | solution.py:107
  111.8 26.0 %collective-permute-start.5 = (bf16[2,8,64,512]{3,2,1,0:T(8,128)(2,1)S(1)}, bf16[2,8,64,512]{3,2,1,0:T(8,128)(2,1)S(1)}, u32[]{:S(2)}, u32[]{:S(2)}) collective-permute-start(bf16[2,8,64,512]{3,2,1,0:T(8,128)(2,1)S(1)} %bitcast.63), channel_id=1, source_target_pairs={{0,1},{1,2},{2,3},{3,0},{4,5},{5,6},{6,7},{7,4},{8,9},{9,10},{10,1... | collective-permute-start | bytes 3145736 | tf_op jit(solution)/shard_map/ppermute | solution.py:37
  111.9 26.3 %collective-permute-start.7 = (bf16[2,8,64,512]{3,2,1,0:T(8,128)(2,1)S(1)}, bf16[2,8,64,512]{3,2,1,0:T(8,128)(2,1)S(1)}, u32[]{:S(2)}, u32[]{:S(2)}) collective-permute-start(bf16[2,8,64,512]{3,2,1,0:T(8,128)(2,1)S(1)} %bitcast.64), channel_id=1, source_target_pairs={{0,3},{1,0},{2,1},{3,2},{4,7},{5,4},{6,5},{7,6},{8,11},{9,8},{10,9... | collective-permute-start | bytes 3145736 | tf_op jit(solution)/shard_map/ppermute | solution.py:37
  137.8 1.0 copy-start.6
  137.9 14.1 %collective-permute-start.6 = (bf16[1,8,64,512]{3,2,1,0:T(8,128)(2,1)S(1)}, bf16[1,8,64,512]{3,2,1,0:T(8,128)(2,1)S(1)}, u32[]{:S(2)}, u32[]{:S(2)}) collective-permute-start(bf16[1,8,64,512]{3,2,1,0:T(8,128)(2,1)S(1)} %slice.67), channel_id=1, source_target_pairs={{0,1},{1,2},{2,3},{3,0},{4,5},{5,6},{6,7},{7,4},{8,9},{9,10},{10,1... | collective-permute-start | bytes 1572872 | tf_op jit(solution)/shard_map/ppermute | solution.py:42
  138.1 1.0 copy-start.7
  139.1 13.1 %collective-permute-start.8 = (bf16[1,8,64,512]{3,2,1,0:T(8,128)(2,1)S(1)}, bf16[1,8,64,512]{3,2,1,0:T(8,128)(2,1)}, u32[]{:S(2)}, u32[]{:S(2)}) collective-permute-start(bf16[1,8,64,512]{3,2,1,0:T(8,128)(2,1)S(1)} %slice.68), channel_id=1, source_target_pairs={{0,3},{1,0},{2,1},{3,2},{4,7},{5,4},{6,5},{7,6},{8,11},{9,8},{10,9... | collective-permute-start | bytes 1572872 | tf_op jit(solution)/shard_map/ppermute | solution.py:43
  152.0 0.8 copy-start.11
  162.4 4.2 %copy-start.1 = (f32[8,64,1024]{2,1,0:T(8,128)S(1)}, f32[8,64,1024]{2,1,0:T(8,128)}, u32[]{:S(2)}) copy-start(f32[8,64,1024]{2,1,0:T(8,128)} %product.3) | copy-start | bytes 6291460
  163.9 2.7 %collective-permute-start.9 = (f32[8,4,8,1024]{3,2,1,0:T(8,128)S(1)}, f32[8,4,8,1024]{3,2,1,0:T(8,128)S(1)}, u32[]{:S(2)}, u32[]{:S(2)}) collective-permute-start(f32[8,4,8,1024]{3,2,1,0:T(8,128)S(1)} %dynamic-slice_bitcast_fusion), channel_id=1, source_target_pairs={{0,4},{4,0},{1,5},{5,1},{2,6},{6,2},{3,7},{7,3},{8,12},{12,8},{9,1... | collective-permute-start | bytes 3145736 | tf_op jit(solution)/shard_map/reduce_core/ppermute | solution.py:99
  168.0 38.6 %copy-start.8 = (bf16[16,1024]{1,0:T(8,128)(2,1)S(1)}, bf16[16,1024]{1,0:T(8,128)(2,1)}, u32[]{:S(2)}) copy-start(bf16[16,1024]{1,0:T(8,128)(2,1)} %param.9) | copy-start | bytes 98308
  168.0 38.6 %copy-start.9 = (f32[1024]{0:T(1024)S(1)}, f32[1024]{0:T(1024)}, u32[]{:S(2)}) copy-start(f32[1024]{0:T(1024)} %param.11) | copy-start | bytes 12292
  168.0 38.6 %copy-start.10 = (f32[16]{0:T(128)S(1)}, f32[16]{0:T(128)}, u32[]{:S(2)}) copy-start(f32[16]{0:T(128)} %param.10) | copy-start | bytes 196
  168.0 38.3 %all-to-all-start.3 = ((f32[32,64,128]{2,1,0:T(8,128)}), f32[32,64,128]{2,1,0:T(8,128)S(1)}, u32[]{:S(2)}, u32[]{:S(2)}) async-start(f32[32,64,128]{2,1,0:T(8,128)} %bitcast.24), calls=%async_computation.3 | async-start | bytes 2097152 | tf_op jit(solution)/shard_map/reduce_zx/all_to_all | solution.py:107

commit v4 on v3

--- a/solution.py
+++ b/solution.py
@@ -6,7 +6,6 @@
 from jax.sharding import Mesh, PartitionSpec as P
 
 NZ, NX, NC, NY = 8, 4, 2, 4
-LANES = 128
 
 
 def ring(size, shift):
@@ -44,14 +43,34 @@
     return low, high
 
 
-def product(parts, integrals):
+def product(parts, gathered, integrals):
     cap, width, n = integrals.shape
+    group = 4
     tiles = parts[0].shape[2]
+    near = tiles // NC
+    place = jnp.stack([lax.axis_index("core"), lax.axis_index("y")]).astype(jnp.int32)
+    operands = list(parts)
+    specs = [
+        pl.BlockSpec((part.shape[0], group, tiles, width), lambda i, place: (0, i, 0, 0))
+        for part in parts
+    ]
     total = sum(part.shape[0] for part in parts)
-    group = 2
+    if gathered is not None:
+        rows = gathered.shape[1]
+        for shift in (1, 2, 3):
+            operands.append(gathered)
+            specs.append(
+                pl.BlockSpec(
+                    (None, rows, group, tiles, width),
+                    lambda i, place, shift=shift: ((place[1] + shift) % NY, 0, i, 0, 0),
+                )
+            )
+            total += rows
+    steps = cap // group
 
-    def body(*refs):
-        *row_refs, integral_ref, out_ref = refs
+    def body(place_ref, *refs):
+        *row_refs, integral_ref, kept_ref, away_ref, sum_ref = refs
+        step = pl.program_id(0)
         value = None
         for j in range(group):
             rows = jnp.concatenate([ref[:, j] for ref in row_refs]).reshape(total * tiles, width)
@@ -59,24 +78,43 @@
             value = term if value is None else value + term
         value = value.reshape(total, tiles, n)
 
-        @pl.when(pl.program_id(0) == 0)
+        @pl.when(step == 0)
         def _():
-            out_ref[...] = value
+            sum_ref[...] = value
 
-        @pl.when(pl.program_id(0) > 0)
+        @pl.when(jnp.logical_and(step > 0, step < steps - 1))
         def _():
-            out_ref[...] += value
+            sum_ref[...] += value
 
+        @pl.when(step == steps - 1)
+        def _():
+            sums = sum_ref[...] + value
+
+            def put(first_ref, second_ref):
+                for r in range(total):
+                    first_ref[:, r, :] = sums[r, :near]
+                    second_ref[:, r, :] = sums[r, near:]
+
+            @pl.when(place_ref[0] == 0)
+            def _():
+                put(kept_ref, away_ref)
+
+            @pl.when(place_ref[0] == 1)
+            def _():
+                put(away_ref, kept_ref)
+
+    out = jax.ShapeDtypeStruct((near, total, n), jnp.float32)
+    out_spec = pl.BlockSpec((near, total, n), lambda i, place: (0, 0, 0))
     return pl.pallas_call(
         body,
-        grid=(cap // group,),
-        out_shape=jax.ShapeDtypeStruct((total, tiles, n), jnp.float32),
-        in_specs=[
-            pl.BlockSpec((part.shape[0], group, tiles, width), lambda i: (0, i, 0, 0))
-            for part in parts
-        ]
-        + [pl.BlockSpec((group, width, n), lambda i: (i, 0, 0))],
-        out_specs=pl.BlockSpec((total, tiles, n), lambda i: (0, 0, 0)),
+        grid_spec=pltpu.PrefetchScalarGridSpec(
+            num_scalar_prefetch=1,
+            grid=(steps,),
+            in_specs=specs + [pl.BlockSpec((group, width, n), lambda i, place: (i, 0, 0))],
+            out_specs=[out_spec, out_spec],
+            scratch_shapes=[pltpu.VMEM((total, tiles, n), jnp.float32)],
+        ),
+        out_shape=[out, out],
         compiler_params=pltpu.CompilerParams(vmem_limit_bytes=56 << 20),
         cost_estimate=pl.CostEstimate(
             flops=2 * total * tiles * cap * width * n,
@@ -84,27 +122,18 @@
             transcendentals=0,
         ),
         name="product",
-    )(*parts, integrals)
+    )(place, *operands, integrals)
 
 
-def pick(array, index, axis):
-    return lax.dynamic_index_in_dim(array, index, axis, keepdims=False)
+def over_core(sums):
+    kept, away = sums
+    with jax.named_scope("reduce_core"):
+        return kept + lax.ppermute(away, "core", ring(NC, 1))
 
 
-def over_core(partial):
-    core = lax.axis_index("core")
-    rows, _, n = partial.shape
-    partial = partial.reshape(rows, NC, NX, NZ, n)
-    with jax.named_scope("reduce_core"):
-        away = lax.ppermute(pick(partial, 1 - core, 1), "core", ring(NC, 1))
-        summed = pick(partial, core, 1) + away
-        summed = summed.reshape(rows, NX, NZ, n // LANES, LANES)
-        return summed.transpose(2, 1, 0, 3, 4).reshape(NZ * NX, -1, LANES)
-
-
-def over_zx(outgoing):
-    with jax.named_scope("reduce_zx"):
-        return jnp.sum(lax.all_to_all(outgoing, ("z", "x"), 0, 0, tiled=True), axis=0)
+def over_xz(outgoing):
+    with jax.named_scope("reduce_xz"):
+        return jnp.sum(lax.all_to_all(outgoing, ("x", "z"), 0, 0, tiled=True), axis=0)
 
 
 def per_device(amplitudes, integrals, slot_block, rest, occ_energy, vir_energy):
@@ -123,15 +152,14 @@
     (outgoing_later,) = after_that(own, outgoing_later)
     after, before = neighbours(own)
     later = route(outgoing_later)
+    (later,) = after_that((after, before), later)
+    with jax.named_scope("replicate_later"):
+        gathered = lax.all_gather(later, "y", axis=0, tiled=False)
     low, high = opposite(*after_that(later, after, before))
-    early = product([own, after, before, later], integrals)
-    early = over_core(*after_that((low, high), early))
-    after_later, before_later = neighbours(later)
-    low_later, high_later = opposite(after_later, before_later)
-    early = over_zx(early)
-    low, high, low_later, high_later = after_that(early, low, high, low_later, high_later)
-    late = [low, high, after_later, low_later, high_later, before_later]
-    late = over_zx(over_core(product(late, integrals)))
+    early = over_core(product([own, after, before, later], None, integrals))
+    low, high = after_that(early, low, high)
+    early = over_xz(early)
+    late = over_xz(over_core(product([low, high], gathered, integrals)))
 
     early = early.reshape(4, step, n)
     late = late.reshape(4, step, n)

time: 208 us -> 210 us (level)
  between operations: 0.3 us -> 13.6 us
  local copies, waits for them, and re-layouts: 11.5 us -> 4.51 us
  starting transfers between devices: 49.5 us -> 43.1 us
  waiting for transfers between devices: 120 us -> 114 us
  other arithmetic: 2.43 us -> 6.29 us
    ppermute x2 -> x1, waiting for transfers between devices: 22.7 us -> 0.01 us  [neighbours(): lax.ppermute(own, 'y', ring(NY, 1))]
    ppermute x2 -> x1, waiting for transfers between devices: 10.7 us -> 23.2 us  [opposite(): low = lax.ppermute(before[:half], 'y', ring(NY, 1))]
    all_gather x0 -> x1, waiting for transfers between devices: none -> 6.64 us  [per_device(): gathered = lax.all_gather(later, 'y', axis=0, tiled=False)]
    add x0 -> x2, other arithmetic: none -> 4.7 us  [over_core(): return kept + lax.ppermute(away, 'core', ring(NC, 1))]
    ppermute x2 -> x1, starting transfers between devices: 6.31 us -> 3.09 us  [neighbours(): lax.ppermute(own, 'y', ring(NY, -1))]
    squeeze x10 -> x0, local copies, waits for them, and re-layouts: 2.86 us -> none  [the longest x2 2.77 us: pick(): return lax.dynamic_index_in_dim(array, index, axis, keepdims=False)]
    reshape x2 -> x0, local copies, waits for them, and re-layouts: 2.42 us -> none  [over_core(): summed = summed.reshape(rows, NX, NZ, n // LANES, LANES)]
    ppermute x2 -> x1, starting transfers between devices: 4.95 us -> 3.47 us  [opposite(): high = lax.ppermute(after[half:], 'y', ring(NY, -1))]
  transfers between devices with their start and end apart: 14 -> 11, of which waited for: 10 -> 7; matrix products, arithmetic and copies ran while one was open for 2% -> 5% of each run, Pallas kernels for 5% -> 10%
where the time goes in v4:
time: 210 us; the launch traced here: 207 us
  waiting for transfers between devices  114 us (54%)
  starting transfers between devices  43.1 us (21%)
  Pallas kernels  21 us (10%)
  between operations  13.6 us (6%)
  other arithmetic  6.29 us (3%)
  matrix products  5.01 us (2%)
  local copies, waits for them, and re-layouts  4.51 us (2%)
    all_to_all x2, waiting for transfers between devices, route(): routed = lax.all_to_all(outgoing, ('z', 'x', 'core'), 0, 0, tiled=True)  51.9 us
    all_to_all x2, waiting for transfers between devices, over_xz(): lax.all_to_all(outgoing, ('x', 'z'), 0, 0, tiled=True)  26.3 us
    ppermute x1, waiting for transfers between devices, opposite(): low = lax.ppermute(before[:half], 'y', ring(NY, 1))  23.2 us
    pallas_call x2, Pallas kernels, product(): pl.pallas_call(body, grid_spec=pltpu.PrefetchScalarGridSpec(num_scalar_pr...  21 us
    all_to_all x2, starting transfers between devices, over_xz(): lax.all_to_all(outgoing, ('x', 'z'), 0, 0, tiled=True)  18.6 us
    all_to_all x2, starting transfers between devices, route(): routed = lax.all_to_all(outgoing, ('z', 'x', 'core'), 0, 0, tiled=True)  17.7 us
    all_gather x1, waiting for transfers between devices, per_device(): gathered = lax.all_gather(later, 'y', axis=0, tiled=False)  6.64 us
    ppermute x2, waiting for transfers between devices, over_core(): return kept + lax.ppermute(away, 'core', ring(NC, 1))  5.72 us
  transfers between devices with their start and end apart: 11, of which 7 were waited for; matrix products, arithmetic and copies ran while one was open for 5% of the time, Pallas kernels for 10%

profile of v4, /device:TPU:2, one launch (start us, length us, event | category | flops | bytes accessed | tf_op | source)
XLA Modules:
  0.0 207.3 jit_solution(6319289786821603123)
XLA Ops:
  6.5 0.8 eq.18
  7.3 2.5 %fusion = bf16[64,2,8,512]{3,2,1,0:T(8,128)(2,1)} fusion(bf16[4,256,512]{2,1,0:T(8,128)(2,1)} %param.6, s32[64,8]{1,0:T(8,128)S(1)} %eq.18), kind=kOutput, calls=%fused_computation.2 | convolution fusion | flops 269090816 | bytes 1574912 | tf_op jit(solution)/shard_map/pick/tsg,rgb->trsb/dot_general | solution.py:21
  9.8 12.0 %all-to-all-start = ((bf16[64,2,8,512]{3,2,1,0:T(8,128)(2,1)}), bf16[64,2,8,512]{3,2,1,0:T(8,128)(2,1)S(1)}, u32[]{:S(2)}, u32[]{:S(2)}) async-start(bf16[64,2,8,512]{3,2,1,0:T(8,128)(2,1)} %fusion), calls=%async_computation | async-start | bytes 2097152 | tf_op jit(solution)/shard_map/route/all_to_all | solution.py:29
  21.8 2.5 %fusion.1 = bf16[64,2,8,512]{3,2,1,0:T(8,128)(2,1)} fusion(bf16[4,256,512]{2,1,0:T(8,128)(2,1)} %param.6, s32[64,8]{1,0:T(8,128)S(1)} %eq.18), kind=kOutput, calls=%fused_computation.3 | convolution fusion | flops 269090816 | bytes 1574912 | tf_op jit(solution)/shard_map/pick/tsg,rgb->trsb/dot_general | solution.py:21
  24.4 26.3 %all-to-all-done = bf16[64,2,8,512]{3,2,1,0:T(8,128)(2,1)S(1)} async-done(((bf16[64,2,8,512]{3,2,1,0:T(8,128)(2,1)}), bf16[64,2,8,512]{3,2,1,0:T(8,128)(2,1)S(1)}, u32[]{:S(2)}, u32[]{:S(2)}) %all-to-all-start) | async-done | bytes 1048608 | tf_op jit(solution)/shard_map/route/all_to_all | solution.py:29
  50.6 0.6 copy.11
  51.2 5.7 %all-to-all-start.1 = ((bf16[64,2,8,512]{3,2,1,0:T(8,128)(2,1)}), bf16[64,2,8,512]{3,2,1,0:T(8,128)(2,1)S(1)}, u32[]{:S(2)}, u32[]{:S(2)}) async-start(bf16[64,2,8,512]{3,2,1,0:T(8,128)(2,1)} %fusion.1), calls=%async_computation.1 | async-start | bytes 2097152 | tf_op jit(solution)/shard_map/route/all_to_all | solution.py:29
  56.9 0.0 all-gather.3.cloned.1.call-start
  56.9 3.1 %collective-permute-start = (bf16[2,8,64,512]{3,2,1,0:T(8,128)(2,1)S(1)}, bf16[2,8,64,512]{3,2,1,0:T(8,128)(2,1)S(1)}, u32[]{:S(2)}, u32[]{:S(2)}) collective-permute-start(bf16[2,8,64,512]{3,2,1,0:T(8,128)(2,1)S(1)} %bitcast.34), channel_id=1, source_target_pairs={{0,3},{1,0},{2,1},{3,2},{4,7},{5,4},{6,5},{7,6},{8,11},{9,8},{10,9... | collective-permute-start | bytes 3145736 | tf_op jit(solution)/shard_map/ppermute | solution.py:36
  60.0 25.6 %all-to-all-done.1 = bf16[64,2,8,512]{3,2,1,0:T(8,128)(2,1)S(1)} async-done(((bf16[64,2,8,512]{3,2,1,0:T(8,128)(2,1)}), bf16[64,2,8,512]{3,2,1,0:T(8,128)(2,1)S(1)}, u32[]{:S(2)}, u32[]{:S(2)}) %all-to-all-start.1) | async-done | bytes 1048608 | tf_op jit(solution)/shard_map/route/all_to_all | solution.py:29
  85.7 1.6 copy.12
  87.3 0.7 pad_add_fusion.place_ref
  88.0 0.3 copy-done.3
  88.3 10.5 %product.2 = (f32[32,8,1024]{2,1,0:T(8,128)}, f32[32,8,1024]{2,1,0:T(8,128)}) custom-call(s32[2]{0:T(128)} %pad_add_fusion.place_ref, bf16[2,8,64,512]{3,2,1,0:T(8,128)(2,1)} %bitcast.36, bf16[2,8,64,512]{3,2,1,0:T(8,128)(2,1)} %copy-done.3, bf16[2,8,64,512]{3,2,1,0:T(8,128)(2,1)} %collective-permute-done.1.refs_2_, bf16[2,8,64,512]{3,2,1,0:T(8,128)(2,1)} %bitcast.31, ...), custom_call_target="tpu_custom_call" | custom-call | flops 4294967296 | bytes 14680064 | tf_op jit(solution)/shard_map/product/pallas_call | solution.py:108
  98.8 2.9 %collective-permute-done.2 = f32[32,8,1024]{2,1,0:T(8,128)S(1)} collective-permute-done((f32[32,8,1024]{2,1,0:T(8,128)}, f32[32,8,1024]{2,1,0:T(8,128)S(1)}, u32[]{:S(2)}, u32[]{:S(2)}) %collective-permute-start.2) | collective-permute-done | bytes 1048608 | tf_op jit(solution)/shard_map/reduce_core/ppermute | solution.py:131
  101.7 2.3 %add.16 = f32[32,8,1024]{2,1,0:T(8,128)} add(f32[32,8,1024]{2,1,0:T(8,128)} %get-tuple-element.17, f32[32,8,1024]{2,1,0:T(8,128)S(1)} %collective-permute-done.2) | non-fusion elementwise | flops 262144 | bytes 3145728 | tf_op jit(solution)/shard_map/reduce_core/add | solution.py:131
  104.0 8.5 %all-to-all-start.2 = ((f32[32,8,1024]{2,1,0:T(8,128)}), f32[32,8,1024]{2,1,0:T(8,128)S(1)}, u32[]{:S(2)}, u32[]{:S(2)}) async-start(f32[32,8,1024]{2,1,0:T(8,128)} %add.16), calls=%async_computation.2 | async-start | bytes 2097152 | tf_op jit(solution)/shard_map/reduce_xz/all_to_all | solution.py:136
  112.5 1.1 slice.49
  113.6 0.1 collective-permute-start.3
  113.8 3.5 %collective-permute-start.4 = (bf16[1,8,64,512]{3,2,1,0:T(8,128)(2,1)S(1)}, bf16[1,8,64,512]{3,2,1,0:T(8,128)(2,1)S(1)}, u32[]{:S(2)}, u32[]{:S(2)}) collective-permute-start(bf16[1,8,64,512]{3,2,1,0:T(8,128)(2,1)S(1)} %slice.50), channel_id=1, source_target_pairs={{0,3},{1,0},{2,1},{3,2},{4,7},{5,4},{6,5},{7,6},{8,11},{9,8},{10,9... | collective-permute-start | bytes 1572872 | tf_op jit(solution)/shard_map/ppermute | solution.py:42
  117.2 23.2 %collective-permute-done.3.refs_0_ = bf16[1,8,64,512]{3,2,1,0:T(8,128)(2,1)S(1)} collective-permute-done((bf16[1,8,64,512]{3,2,1,0:T(8,128)(2,1)S(1)}, bf16[1,8,64,512]{3,2,1,0:T(8,128)(2,1)S(1)}, u32[]{:S(2)}, u32[]{:S(2)}) %collective-permute-start.3) | collective-permute-done | bytes 524320 | tf_op jit(solution)/shard_map/ppermute | solution.py:41
  140.5 6.6 %all-gather.3.cloned.1.call-done = bf16[8,8,64,512]{3,2,1,0:T(8,128)(2,1)} async-done(((bf16[2,8,64,512]{3,2,1,0:T(8,128)(2,1)}), bf16[8,8,64,512]{3,2,1,0:T(8,128)(2,1)}) %all-gather.3.cloned.1.call-update) | async-done | bytes 4194320 | tf_op jit(solution)/shard_map/replicate_later/all_gather | solution.py:157
  147.1 10.5 %product.3 = (f32[32,8,1024]{2,1,0:T(8,128)}, f32[32,8,1024]{2,1,0:T(8,128)}) custom-call(s32[2]{0:T(128)} %pad_add_fusion.place_ref, bf16[1,8,64,512]{3,2,1,0:T(8,128)(2,1)} %copy-done.1, bf16[1,8,64,512]{3,2,1,0:T(8,128)(2,1)} %copy-done.2, bf16[4,2,8,64,512]{4,3,2,1,0:T(8,128)(2,1)} %bitcast.27, bf16[4,2,8,64,512]{4,3,2,1,0:T(8,128)(2,1)} %bitcast.28, ...), custom_call_target="tpu_custom_call" | custom-call | flops 4294967296 | bytes 14680064 | tf_op jit(solution)/shard_map/product/pallas_call | solution.py:108
  157.6 0.1 collective-permute-start.5
  157.7 2.9 %collective-permute-done.5 = f32[32,8,1024]{2,1,0:T(8,128)S(1)} collective-permute-done((f32[32,8,1024]{2,1,0:T(8,128)}, f32[32,8,1024]{2,1,0:T(8,128)S(1)}, u32[]{:S(2)}, u32[]{:S(2)}) %collective-permute-start.5) | collective-permute-done | bytes 1048608 | tf_op jit(solution)/shard_map/reduce_core/ppermute | solution.py:131
  160.6 2.4 %add.17 = f32[32,8,1024]{2,1,0:T(8,128)} add(f32[32,8,1024]{2,1,0:T(8,128)} %get-tuple-element.23, f32[32,8,1024]{2,1,0:T(8,128)S(1)} %collective-permute-done.5) | non-fusion elementwise | flops 262144 | bytes 3145728 | tf_op jit(solution)/shard_map/reduce_core/add | solution.py:131
  162.9 10.1 %all-to-all-start.3 = ((f32[32,8,1024]{2,1,0:T(8,128)}), f32[32,8,1024]{2,1,0:T(8,128)S(1)}, u32[]{:S(2)}, u32[]{:S(2)}) async-start(f32[32,8,1024]{2,1,0:T(8,128)} %add.17), calls=%async_computation.3 | async-start | bytes 2097152 | tf_op jit(solution)/shard_map/reduce_xz/all_to_all | solution.py:136
  173.1 0.1 reduce_sum.18
  173.2 26.3 %all-to-all-done.3 = f32[32,8,1024]{2,1,0:T(8,128)S(1)} async-done(((f32[32,8,1024]{2,1,0:T(8,128)}), f32[32,8,1024]{2,1,0:T(8,128)S(1)}, u32[]{:S(2)}, u32[]{:S(2)}) %all-to-all-start.3) | async-done | bytes 1048608 | tf_op jit(solution)/shard_map/reduce_xz/all_to_all | solution.py:136
  199.5 0.1 reduce_sum.19
  199.6 0.1 concatenate.6
  199.8 0.7 divide_convert_fusion
  (28 shorter events, 0.2 us)
Async XLA Ops:
  9.8 40.8 %all-to-all-start = ((bf16[64,2,8,512]{3,2,1,0:T(8,128)(2,1)}), bf16[64,2,8,512]{3,2,1,0:T(8,128)(2,1)S(1)}, u32[]{:S(2)}, u32[]{:S(2)}) async-start(bf16[64,2,8,512]{3,2,1,0:T(8,128)(2,1)} %fusion), calls=%async_computation | async-start | bytes 2097152 | tf_op jit(solution)/shard_map/route/all_to_all | solution.py:29
  51.2 36.8 %copy-start = (bf16[8,4,2,2,8,512]{5,0,1,2,4,3:T(8,128)(2,1)}, bf16[8,4,2,2,8,512]{5,0,1,2,4,3:T(8,128)(2,1)S(1)}, u32[]{:S(2)}) copy-start(bf16[8,4,2,2,8,512]{5,0,1,2,4,3:T(8,128)(2,1)S(1)} %copy.11) | copy-start | bytes 3145732
  51.2 34.5 %all-to-all-start.1 = ((bf16[64,2,8,512]{3,2,1,0:T(8,128)(2,1)}), bf16[64,2,8,512]{3,2,1,0:T(8,128)(2,1)S(1)}, u32[]{:S(2)}, u32[]{:S(2)}) async-start(bf16[64,2,8,512]{3,2,1,0:T(8,128)(2,1)} %fusion.1), calls=%async_computation.1 | async-start | bytes 2097152 | tf_op jit(solution)/shard_map/route/all_to_all | solution.py:29
  56.9 90.2 %all-gather.3.cloned.1.call-start = ((), (), s32[]{:S(2)}) async-start(), calls=%async_computation.4 | async-start | bytes 5242880 | tf_op jit(solution)/shard_map/replicate_later/all_gather | solution.py:157
  56.9 30.3 %collective-permute-start = (bf16[2,8,64,512]{3,2,1,0:T(8,128)(2,1)S(1)}, bf16[2,8,64,512]{3,2,1,0:T(8,128)(2,1)S(1)}, u32[]{:S(2)}, u32[]{:S(2)}) collective-permute-start(bf16[2,8,64,512]{3,2,1,0:T(8,128)(2,1)S(1)} %bitcast.34), channel_id=1, source_target_pairs={{0,3},{1,0},{2,1},{3,2},{4,7},{5,4},{6,5},{7,6},{8,11},{9,8},{10,9... | collective-permute-start | bytes 3145736 | tf_op jit(solution)/shard_map/ppermute | solution.py:36
  60.0 27.2 %collective-permute-start.1 = (bf16[2,8,64,512]{3,2,1,0:T(8,128)(2,1)S(1)}, bf16[2,8,64,512]{3,2,1,0:T(8,128)(2,1)}, u32[]{:S(2)}, u32[]{:S(2)}) collective-permute-start(bf16[2,8,64,512]{3,2,1,0:T(8,128)(2,1)S(1)} %bitcast.35), channel_id=1, source_target_pairs={{0,1},{1,2},{2,3},{3,0},{4,5},{5,6},{6,7},{7,4},{8,9},{9,10},{10,1... | collective-permute-start | bytes 3145736 | tf_op jit(solution)/shard_map/ppermute | solution.py:36
  87.2 1.1 copy-start.3
  98.8 14.9 %copy-start.4 = (bf16[2,8,64,512]{3,2,1,0:T(8,128)(2,1)S(1)}, bf16[2,8,64,512]{3,2,1,0:T(8,128)(2,1)}, u32[]{:S(2)}) copy-start(bf16[2,8,64,512]{3,2,1,0:T(8,128)(2,1)} %copy-done.3) | copy-start | bytes 3145732
  98.8 2.9 %collective-permute-start.2 = (f32[32,8,1024]{2,1,0:T(8,128)}, f32[32,8,1024]{2,1,0:T(8,128)S(1)}, u32[]{:S(2)}, u32[]{:S(2)}) collective-permute-start(f32[32,8,1024]{2,1,0:T(8,128)} %get-tuple-element.18), channel_id=1, source_target_pairs={{0,4},{4,0},{1,5},{5,1},{2,6},{6,2},{3,7},{7,3},{8,12},{12,8},{9,1... | collective-permute-start | bytes 3145736 | tf_op jit(solution)/shard_map/reduce_core/ppermute | solution.py:131
  104.0 58.9 %all-to-all-start.2 = ((f32[32,8,1024]{2,1,0:T(8,128)}), f32[32,8,1024]{2,1,0:T(8,128)S(1)}, u32[]{:S(2)}, u32[]{:S(2)}) async-start(f32[32,8,1024]{2,1,0:T(8,128)} %add.16), calls=%async_computation.2 | async-start | bytes 2097152 | tf_op jit(solution)/shard_map/reduce_xz/all_to_all | solution.py:136
  113.6 26.8 %collective-permute-start.3 = (bf16[1,8,64,512]{3,2,1,0:T(8,128)(2,1)S(1)}, bf16[1,8,64,512]{3,2,1,0:T(8,128)(2,1)S(1)}, u32[]{:S(2)}, u32[]{:S(2)}) collective-permute-start(bf16[1,8,64,512]{3,2,1,0:T(8,128)(2,1)S(1)} %slice.49), channel_id=1, source_target_pairs={{0,1},{1,2},{2,3},{3,0},{4,5},{5,6},{6,7},{7,4},{8,9},{9,10},{10,1... | collective-permute-start | bytes 1572872 | tf_op jit(solution)/shard_map/ppermute | solution.py:41
  113.8 26.7 %collective-permute-start.4 = (bf16[1,8,64,512]{3,2,1,0:T(8,128)(2,1)S(1)}, bf16[1,8,64,512]{3,2,1,0:T(8,128)(2,1)S(1)}, u32[]{:S(2)}, u32[]{:S(2)}) collective-permute-start(bf16[1,8,64,512]{3,2,1,0:T(8,128)(2,1)S(1)} %slice.50), channel_id=1, source_target_pairs={{0,3},{1,0},{2,1},{3,2},{4,7},{5,4},{6,5},{7,6},{8,11},{9,8},{10,9... | collective-permute-start | bytes 1572872 | tf_op jit(solution)/shard_map/ppermute | solution.py:42
  140.4 6.7 %copy-start.1 = (bf16[1,8,64,512]{3,2,1,0:T(8,128)(2,1)}, bf16[1,8,64,512]{3,2,1,0:T(8,128)(2,1)S(1)}, u32[]{:S(2)}) copy-start(bf16[1,8,64,512]{3,2,1,0:T(8,128)(2,1)S(1)} %collective-permute-done.3.refs_0_) | copy-start | bytes 1572868
  140.4 6.6 %copy-start.2 = (bf16[1,8,64,512]{3,2,1,0:T(8,128)(2,1)}, bf16[1,8,64,512]{3,2,1,0:T(8,128)(2,1)S(1)}, u32[]{:S(2)}) copy-start(bf16[1,8,64,512]{3,2,1,0:T(8,128)(2,1)S(1)} %collective-permute-done.4.refs_1_) | copy-start | bytes 1572868
  157.6 42.2 %copy-start.5 = (bf16[16,1024]{1,0:T(8,128)(2,1)S(1)}, bf16[16,1024]{1,0:T(8,128)(2,1)}, u32[]{:S(2)}) copy-start(bf16[16,1024]{1,0:T(8,128)(2,1)} %param.9) | copy-start | bytes 98308
  157.6 42.2 %copy-start.6 = (f32[1024]{0:T(1024)S(1)}, f32[1024]{0:T(1024)}, u32[]{:S(2)}) copy-start(f32[1024]{0:T(1024)} %param.11) | copy-start | bytes 12292
  157.6 42.2 %copy-start.7 = (f32[16]{0:T(128)S(1)}, f32[16]{0:T(128)}, u32[]{:S(2)}) copy-start(f32[16]{0:T(128)} %param.10) | copy-start | bytes 196
  157.6 3.0 %collective-permute-start.5 = (f32[32,8,1024]{2,1,0:T(8,128)}, f32[32,8,1024]{2,1,0:T(8,128)S(1)}, u32[]{:S(2)}, u32[]{:S(2)}) collective-permute-start(f32[32,8,1024]{2,1,0:T(8,128)} %get-tuple-element.24), channel_id=1, source_target_pairs={{0,4},{4,0},{1,5},{5,1},{2,6},{6,2},{3,7},{7,3},{8,12},{12,8},{9,1... | collective-permute-start | bytes 3145736 | tf_op jit(solution)/shard_map/reduce_core/ppermute | solution.py:131
  162.9 36.6 %all-to-all-start.3 = ((f32[32,8,1024]{2,1,0:T(8,128)}), f32[32,8,1024]{2,1,0:T(8,128)S(1)}, u32[]{:S(2)}, u32[]{:S(2)}) async-start(f32[32,8,1024]{2,1,0:T(8,128)} %add.17), calls=%async_computation.3 | async-start | bytes 2097152 | tf_op jit(solution)/shard_map/reduce_xz/all_to_all | solution.py:136
Sparse Core Ops, SparseCore 0:
  87.4 59.6 all-gather.2

commit v5 on v4

--- a/solution.py
+++ b/solution.py
@@ -6,6 +6,7 @@
 from jax.sharding import Mesh, PartitionSpec as P
 
 NZ, NX, NC, NY = 8, 4, 2, 4
+ROWS = 8
 
 
 def ring(size, shift):
@@ -43,33 +44,19 @@
     return low, high
 
 
-def product(parts, gathered, integrals):
+def product(parts, integrals, base=None):
     cap, width, n = integrals.shape
     group = 4
     tiles = parts[0].shape[2]
     near = tiles // NC
-    place = jnp.stack([lax.axis_index("core"), lax.axis_index("y")]).astype(jnp.int32)
-    operands = list(parts)
-    specs = [
-        pl.BlockSpec((part.shape[0], group, tiles, width), lambda i, place: (0, i, 0, 0))
-        for part in parts
-    ]
+    place = lax.axis_index("core").astype(jnp.int32).reshape(1)
     total = sum(part.shape[0] for part in parts)
-    if gathered is not None:
-        rows = gathered.shape[1]
-        for shift in (1, 2, 3):
-            operands.append(gathered)
-            specs.append(
-                pl.BlockSpec(
-                    (None, rows, group, tiles, width),
-                    lambda i, place, shift=shift: ((place[1] + shift) % NY, 0, i, 0, 0),
-                )
-            )
-            total += rows
+    offset = ROWS - total if base is not None else 0
     steps = cap // group
 
     def body(place_ref, *refs):
-        *row_refs, integral_ref, kept_ref, away_ref, sum_ref = refs
+        *refs, integral_ref, kept_ref, away_ref, sum_ref = refs
+        base_refs, row_refs = refs[: len(refs) - len(parts)], refs[len(refs) - len(parts) :]
         step = pl.program_id(0)
         value = None
         for j in range(group):
@@ -89,11 +76,13 @@
         @pl.when(step == steps - 1)
         def _():
             sums = sum_ref[...] + value
+            for base_ref, out_ref in zip(base_refs, (kept_ref, away_ref)):
+                out_ref[...] = base_ref[...]
 
             def put(first_ref, second_ref):
                 for r in range(total):
-                    first_ref[:, r, :] = sums[r, :near]
-                    second_ref[:, r, :] = sums[r, near:]
+                    first_ref[:, offset + r, :] = sums[r, :near]
+                    second_ref[:, offset + r, :] = sums[r, near:]
 
             @pl.when(place_ref[0] == 0)
             def _():
@@ -103,14 +92,21 @@
             def _():
                 put(away_ref, kept_ref)
 
-    out = jax.ShapeDtypeStruct((near, total, n), jnp.float32)
-    out_spec = pl.BlockSpec((near, total, n), lambda i, place: (0, 0, 0))
+    out = jax.ShapeDtypeStruct((near, ROWS, n), jnp.float32)
+    out_spec = pl.BlockSpec((near, ROWS, n), lambda i, place: (0, 0, 0))
+    row_specs = [
+        pl.BlockSpec((part.shape[0], group, tiles, width), lambda i, place: (0, i, 0, 0))
+        for part in parts
+    ]
+    base = [] if base is None else list(base)
     return pl.pallas_call(
         body,
         grid_spec=pltpu.PrefetchScalarGridSpec(
             num_scalar_prefetch=1,
             grid=(steps,),
-            in_specs=specs + [pl.BlockSpec((group, width, n), lambda i, place: (i, 0, 0))],
+            in_specs=[out_spec] * len(base)
+            + row_specs
+            + [pl.BlockSpec((group, width, n), lambda i, place: (i, 0, 0))],
             out_specs=[out_spec, out_spec],
             scratch_shapes=[pltpu.VMEM((total, tiles, n), jnp.float32)],
         ),
@@ -122,7 +118,7 @@
             transcendentals=0,
         ),
         name="product",
-    )(place, *operands, integrals)
+    )(place, *base, *parts, integrals)
 
 
 def over_core(sums):
@@ -153,18 +149,21 @@
     after, before = neighbours(own)
     later = route(outgoing_later)
     (later,) = after_that((after, before), later)
-    with jax.named_scope("replicate_later"):
-        gathered = lax.all_gather(later, "y", axis=0, tiled=False)
     low, high = opposite(*after_that(later, after, before))
-    early = over_core(product([own, after, before, later], None, integrals))
-    low, high = after_that(early, low, high)
+    after_later, before_later = neighbours(later)
+    low_later, high_later = opposite(after_later, before_later)
+    kept, away = product([own, after, before, later], integrals)
+    low, high, away = lax.optimization_barrier((low, high, away))
+    early = over_core((kept, away))
     early = over_xz(early)
-    late = over_xz(over_core(product([low, high], gathered, integrals)))
+    late = product([low, high, after_later, before_later], integrals)
+    late = product([low_later, high_later], integrals, late)
+    late = over_xz(over_core(late))
 
     early = early.reshape(4, step, n)
     late = late.reshape(4, step, n)
     own, after, before, later = (early[i] for i in range(4))
-    across, after_later, across_later, before_later = (late[i] for i in range(4))
+    across, after_later, before_later, across_later = (late[i] for i in range(4))
     relative = jnp.concatenate(
         [own, later, after, after_later, across, across_later, before, before_later]
     ).reshape(NY, 2 * step, n)

time: 210 us -> 192 us (0.914)
  waiting for transfers between devices: 114 us -> 98.2 us
  between operations: 13.6 us -> 0.2 us
  starting transfers between devices: 43.1 us -> 48.1 us
  Pallas kernels: 21 us -> 24.9 us
  local copies, waits for them, and re-layouts: 4.51 us -> 7.45 us
    ppermute x1 -> x2, waiting for transfers between devices: 23.2 us -> 2.87 us  [opposite(): low = lax.ppermute(before[:half], 'y', ring(NY, 1))]
    ppermute x1 -> x2, waiting for transfers between devices: 0.01 us -> 12.6 us  [neighbours(): lax.ppermute(own, 'y', ring(NY, 1))]
    all_gather x1 -> x0, waiting for transfers between devices: 6.64 us -> none  [per_device(): gathered = lax.all_gather(later, 'y', axis=0, tiled=False)]
    pallas_call x2 -> x3, Pallas kernels: 21 us -> 24.9 us  [product(): pl.pallas_call(body, grid_spec=pltpu.PrefetchScalarGridSpec(num_scalar_pr...]
    ppermute x2, waiting for transfers between devices: 5.72 us -> 2.87 us  [over_core(): return kept + lax.ppermute(away, 'core', ring(NC, 1))]
    ppermute x1 -> x2, starting transfers between devices: 3.09 us -> 4.79 us  [neighbours(): lax.ppermute(own, 'y', ring(NY, -1))]
    ppermute x1 -> x2, starting transfers between devices: 3.47 us -> 4.73 us  [opposite(): high = lax.ppermute(after[half:], 'y', ring(NY, -1))]
  transfers between devices with their start and end apart: 11 -> 14, of which waited for: 7 -> 9; matrix products, arithmetic and copies ran while one was open for 5% -> 5% of each run, Pallas kernels for 10% -> 13%
where the time goes in v5:
time: 192 us; the launch traced here: 188 us
  waiting for transfers between devices  98.2 us (51%)
  starting transfers between devices  48.1 us (25%)
  Pallas kernels  24.9 us (13%)
  local copies, waits for them, and re-layouts  7.45 us (4%)
  other arithmetic  5.55 us (3%)
  matrix products  3.95 us (2%)
    all_to_all x2, waiting for transfers between devices, route(): routed = lax.all_to_all(outgoing, ('z', 'x', 'core'), 0, 0, tiled=True)  53 us
    all_to_all x2, waiting for transfers between devices, over_xz(): lax.all_to_all(outgoing, ('x', 'z'), 0, 0, tiled=True)  26.3 us
    pallas_call x3, Pallas kernels, product(): pl.pallas_call(body, grid_spec=pltpu.PrefetchScalarGridSpec(num_scalar_pr...  24.9 us
    all_to_all x2, starting transfers between devices, route(): routed = lax.all_to_all(outgoing, ('z', 'x', 'core'), 0, 0, tiled=True)  17.7 us
    all_to_all x2, starting transfers between devices, over_xz(): lax.all_to_all(outgoing, ('x', 'z'), 0, 0, tiled=True)  17.3 us
    ppermute x2, waiting for transfers between devices, neighbours(): lax.ppermute(own, 'y', ring(NY, 1))  12.6 us
    ppermute x2, starting transfers between devices, neighbours(): lax.ppermute(own, 'y', ring(NY, -1))  4.79 us
    ppermute x2, starting transfers between devices, opposite(): high = lax.ppermute(after[half:], 'y', ring(NY, -1))  4.73 us
  transfers between devices with their start and end apart: 14, of which 9 were waited for; matrix products, arithmetic and copies ran while one was open for 5% of the time, Pallas kernels for 13%

profile of v5, /device:TPU:2, one launch (start us, length us, event | category | flops | bytes accessed | tf_op | source)
XLA Modules:
  0.0 188.3 jit_solution(17701989327237183401)
XLA Ops:
  0.0 0.9 eq.18
  0.9 2.5 %fusion = bf16[64,2,8,512]{3,2,1,0:T(8,128)(2,1)} fusion(bf16[4,256,512]{2,1,0:T(8,128)(2,1)} %param.6, s32[64,8]{1,0:T(8,128)S(1)} %eq.18), kind=kOutput, calls=%fused_computation.2 | convolution fusion | flops 269090816 | bytes 1574912 | tf_op jit(solution)/shard_map/pick/tsg,rgb->trsb/dot_general | solution.py:22
  3.3 12.0 %all-to-all-start = ((bf16[64,2,8,512]{3,2,1,0:T(8,128)(2,1)}), bf16[64,2,8,512]{3,2,1,0:T(8,128)(2,1)S(1)}, u32[]{:S(2)}, u32[]{:S(2)}) async-start(bf16[64,2,8,512]{3,2,1,0:T(8,128)(2,1)} %fusion), calls=%async_computation | async-start | bytes 2097152 | tf_op jit(solution)/shard_map/route/all_to_all | solution.py:30
  15.4 1.5 fusion.1
  16.9 27.3 %all-to-all-done = bf16[64,2,8,512]{3,2,1,0:T(8,128)(2,1)S(1)} async-done(((bf16[64,2,8,512]{3,2,1,0:T(8,128)(2,1)}), bf16[64,2,8,512]{3,2,1,0:T(8,128)(2,1)S(1)}, u32[]{:S(2)}, u32[]{:S(2)}) %all-to-all-start) | async-done | bytes 1048608 | tf_op jit(solution)/shard_map/route/all_to_all | solution.py:30
  44.2 0.6 copy.9
  44.8 5.7 %all-to-all-start.1 = ((bf16[64,2,8,512]{3,2,1,0:T(8,128)(2,1)}), bf16[64,2,8,512]{3,2,1,0:T(8,128)(2,1)S(1)}, u32[]{:S(2)}, u32[]{:S(2)}) async-start(bf16[64,2,8,512]{3,2,1,0:T(8,128)(2,1)} %fusion.1), calls=%async_computation.1 | async-start | bytes 2097152 | tf_op jit(solution)/shard_map/route/all_to_all | solution.py:30
  50.4 3.1 %collective-permute-start = (bf16[2,8,64,512]{3,2,1,0:T(8,128)(2,1)S(1)}, bf16[2,8,64,512]{3,2,1,0:T(8,128)(2,1)S(1)}, u32[]{:S(2)}, u32[]{:S(2)}) collective-permute-start(bf16[2,8,64,512]{3,2,1,0:T(8,128)(2,1)S(1)} %bitcast.30), channel_id=1, source_target_pairs={{0,3},{1,0},{2,1},{3,2},{4,7},{5,4},{6,5},{7,6},{8,11},{9,8},{10,9... | collective-permute-start | bytes 3145736 | tf_op jit(solution)/shard_map/ppermute | solution.py:37
  53.5 25.7 %all-to-all-done.1 = bf16[64,2,8,512]{3,2,1,0:T(8,128)(2,1)S(1)} async-done(((bf16[64,2,8,512]{3,2,1,0:T(8,128)(2,1)}), bf16[64,2,8,512]{3,2,1,0:T(8,128)(2,1)S(1)}, u32[]{:S(2)}, u32[]{:S(2)}) %all-to-all-start.1) | async-done | bytes 1048608 | tf_op jit(solution)/shard_map/route/all_to_all | solution.py:30
  79.2 1.6 copy.10
  80.8 1.5 slice.52
  82.3 1.7 collective-permute-start.2
  84.0 1.7 collective-permute-start.3
  85.7 9.8 %product.3 = (f32[32,8,1024]{2,1,0:T(8,128)}, f32[32,8,1024]{2,1,0:T(8,128)}) custom-call(s32[1]{0:T(128)} %bitcast.place_ref, bf16[2,8,64,512]{3,2,1,0:T(8,128)(2,1)} %bitcast.32, bf16[2,8,64,512]{3,2,1,0:T(8,128)(2,1)} %copy-done.5, bf16[2,8,64,512]{3,2,1,0:T(8,128)(2,1)} %collective-permute-done.1.refs_2_, bf16[2,8,64,512]{3,2,1,0:T(8,128)(2,1)} %bitcast.27, ...), custom_call_target="tpu_custom_call" | custom-call | flops 4294967296 | bytes 14680064 | tf_op jit(solution)/shard_map/product/pallas_call | solution.py:102
  95.5 0.8 collective-permute-done.2.refs_0_
  96.4 0.7 copy-done.10
  97.3 1.5 collective-permute-start.6
  98.8 1.7 collective-permute-start.5
  100.5 2.4 %add.16 = f32[32,8,1024]{2,1,0:T(8,128)} add(f32[32,8,1024]{2,1,0:T(8,128)} %get-tuple-element.20, f32[32,8,1024]{2,1,0:T(8,128)S(1)} %collective-permute-done.4) | non-fusion elementwise | flops 262144 | bytes 3145728 | tf_op jit(solution)/shard_map/reduce_core/add | solution.py:127
  102.9 8.6 %all-to-all-start.2 = ((f32[32,8,1024]{2,1,0:T(8,128)}), f32[32,8,1024]{2,1,0:T(8,128)S(1)}, u32[]{:S(2)}, u32[]{:S(2)}) async-start(f32[32,8,1024]{2,1,0:T(8,128)} %add.16), calls=%async_computation.2 | async-start | bytes 2097152 | tf_op jit(solution)/shard_map/reduce_xz/all_to_all | solution.py:132
  111.5 12.6 %collective-permute-done.6.refs_3_ = bf16[2,8,64,512]{3,2,1,0:T(8,128)(2,1)S(1)} collective-permute-done((bf16[2,8,64,512]{3,2,1,0:T(8,128)(2,1)S(1)}, bf16[2,8,64,512]{3,2,1,0:T(8,128)(2,1)S(1)}, u32[]{:S(2)}, u32[]{:S(2)}) %collective-permute-start.6) | collective-permute-done | bytes 1048608 | tf_op jit(solution)/shard_map/ppermute | solution.py:37
  124.5 1.1 slice.68
  125.6 3.0 %collective-permute-start.8 = (bf16[1,8,64,512]{3,2,1,0:T(8,128)(2,1)S(1)}, bf16[1,8,64,512]{3,2,1,0:T(8,128)(2,1)S(1)}, u32[]{:S(2)}, u32[]{:S(2)}) collective-permute-start(bf16[1,8,64,512]{3,2,1,0:T(8,128)(2,1)S(1)} %slice.68), channel_id=1, source_target_pairs={{0,3},{1,0},{2,1},{3,2},{4,7},{5,4},{6,5},{7,6},{8,11},{9,8},{10,9... | collective-permute-start | bytes 1572872 | tf_op jit(solution)/shard_map/ppermute | solution.py:43
  128.6 8.3 %product.4 = (f32[32,8,1024]{2,1,0:T(8,128)}, f32[32,8,1024]{2,1,0:T(8,128)}) custom-call(s32[1]{0:T(128)} %bitcast.place_ref, bf16[1,8,64,512]{3,2,1,0:T(8,128)(2,1)} %copy-done.10, bf16[1,8,64,512]{3,2,1,0:T(8,128)(2,1)} %copy-done.11, bf16[2,8,64,512]{3,2,1,0:T(8,128)(2,1)} %collective-permute-done.5.refs_2_, bf16[2,8,64,512]{3,2,1,0:T(8,128)(2,1)} %copy-done.6, ...), custom_call_target="tpu_custom_call" | custom-call | flops 3221225472 | bytes 13107200 | tf_op jit(solution)/shard_map/product/pallas_call | solution.py:102
  136.9 2.1 %collective-permute-done.7.refs_2_ = bf16[1,8,64,512]{3,2,1,0:T(8,128)(2,1)S(1)} collective-permute-done((bf16[1,8,64,512]{3,2,1,0:T(8,128)(2,1)S(1)}, bf16[1,8,64,512]{3,2,1,0:T(8,128)(2,1)S(1)}, u32[]{:S(2)}, u32[]{:S(2)}) %collective-permute-start.7) | collective-permute-done | bytes 524320 | tf_op jit(solution)/shard_map/ppermute | solution.py:42
  139.8 0.4 copy-done.4
  140.2 6.8 %product.5 = (f32[32,8,1024]{2,1,0:T(8,128)}, f32[32,8,1024]{2,1,0:T(8,128)}) custom-call(s32[1]{0:T(128)} %bitcast.place_ref, f32[32,8,1024]{2,1,0:T(8,128)} %get-tuple-element.27.refs_0_, f32[32,8,1024]{2,1,0:T(8,128)} %get-tuple-element.28.refs_1_, bf16[1,8,64,512]{3,2,1,0:T(8,128)(2,1)} %copy-done.3, bf16[1,8,64,512]{3,2,1,0:T(8,128)(2,1)} %copy-done.4, ...), custom_call_target="tpu_custom_call" | custom-call | flops 1073741824 | bytes 9961472 | tf_op jit(solution)/shard_map/product/pallas_call | solution.py:102
  147.0 2.9 %collective-permute-done.9 = f32[32,8,1024]{2,1,0:T(8,128)S(1)} collective-permute-done((f32[32,8,1024]{2,1,0:T(8,128)}, f32[32,8,1024]{2,1,0:T(8,128)S(1)}, u32[]{:S(2)}, u32[]{:S(2)}) %collective-permute-start.9) | collective-permute-done | bytes 1048608 | tf_op jit(solution)/shard_map/reduce_core/ppermute | solution.py:127
  149.9 2.3 %add.17 = f32[32,8,1024]{2,1,0:T(8,128)} add(f32[32,8,1024]{2,1,0:T(8,128)} %get-tuple-element.29, f32[32,8,1024]{2,1,0:T(8,128)S(1)} %collective-permute-done.9) | non-fusion elementwise | flops 262144 | bytes 3145728 | tf_op jit(solution)/shard_map/reduce_core/add | solution.py:127
  152.2 8.7 %all-to-all-start.3 = ((f32[32,8,1024]{2,1,0:T(8,128)}), f32[32,8,1024]{2,1,0:T(8,128)S(1)}, u32[]{:S(2)}, u32[]{:S(2)}) async-start(f32[32,8,1024]{2,1,0:T(8,128)} %add.17), calls=%async_computation.3 | async-start | bytes 2097152 | tf_op jit(solution)/shard_map/reduce_xz/all_to_all | solution.py:132
  161.1 26.3 %all-to-all-done.3 = f32[32,8,1024]{2,1,0:T(8,128)S(1)} async-done(((f32[32,8,1024]{2,1,0:T(8,128)}), f32[32,8,1024]{2,1,0:T(8,128)S(1)}, u32[]{:S(2)}, u32[]{:S(2)}) %all-to-all-start.3) | async-done | bytes 1048608 | tf_op jit(solution)/shard_map/reduce_xz/all_to_all | solution.py:132
  187.6 0.7 divide_convert_fusion
  (43 shorter events, 2.0 us)
Async XLA Ops:
  0.0 15.4 %copy-start = (bf16[4,256,512]{2,1,0:T(8,128)(2,1)S(1)}, bf16[4,256,512]{2,1,0:T(8,128)(2,1)}, u32[]{:S(2)}) copy-start(bf16[4,256,512]{2,1,0:T(8,128)(2,1)} %param.6) | copy-start | bytes 3145732
  3.3 40.8 %all-to-all-start = ((bf16[64,2,8,512]{3,2,1,0:T(8,128)(2,1)}), bf16[64,2,8,512]{3,2,1,0:T(8,128)(2,1)S(1)}, u32[]{:S(2)}, u32[]{:S(2)}) async-start(bf16[64,2,8,512]{3,2,1,0:T(8,128)(2,1)} %fusion), calls=%async_computation | async-start | bytes 2097152 | tf_op jit(solution)/shard_map/route/all_to_all | solution.py:30
  44.7 36.0 %copy-start.2 = (bf16[8,4,2,2,8,512]{5,0,1,2,4,3:T(8,128)(2,1)}, bf16[8,4,2,2,8,512]{5,0,1,2,4,3:T(8,128)(2,1)S(1)}, u32[]{:S(2)}) copy-start(bf16[8,4,2,2,8,512]{5,0,1,2,4,3:T(8,128)(2,1)S(1)} %copy.9) | copy-start | bytes 3145732
  44.8 34.5 %all-to-all-start.1 = ((bf16[64,2,8,512]{3,2,1,0:T(8,128)(2,1)}), bf16[64,2,8,512]{3,2,1,0:T(8,128)(2,1)S(1)}, u32[]{:S(2)}, u32[]{:S(2)}) async-start(bf16[64,2,8,512]{3,2,1,0:T(8,128)(2,1)} %fusion.1), calls=%async_computation.1 | async-start | bytes 2097152 | tf_op jit(solution)/shard_map/route/all_to_all | solution.py:30
  50.4 30.4 %collective-permute-start = (bf16[2,8,64,512]{3,2,1,0:T(8,128)(2,1)S(1)}, bf16[2,8,64,512]{3,2,1,0:T(8,128)(2,1)S(1)}, u32[]{:S(2)}, u32[]{:S(2)}) collective-permute-start(bf16[2,8,64,512]{3,2,1,0:T(8,128)(2,1)S(1)} %bitcast.30), channel_id=1, source_target_pairs={{0,3},{1,0},{2,1},{3,2},{4,7},{5,4},{6,5},{7,6},{8,11},{9,8},{10,9... | collective-permute-start | bytes 3145736 | tf_op jit(solution)/shard_map/ppermute | solution.py:37
  53.5 27.3 %collective-permute-start.1 = (bf16[2,8,64,512]{3,2,1,0:T(8,128)(2,1)S(1)}, bf16[2,8,64,512]{3,2,1,0:T(8,128)(2,1)}, u32[]{:S(2)}, u32[]{:S(2)}) collective-permute-start(bf16[2,8,64,512]{3,2,1,0:T(8,128)(2,1)S(1)} %bitcast.31), channel_id=1, source_target_pairs={{0,1},{1,2},{2,3},{3,0},{4,5},{5,6},{6,7},{7,4},{8,9},{9,10},{10,1... | collective-permute-start | bytes 3145736 | tf_op jit(solution)/shard_map/ppermute | solution.py:37
  80.8 4.9 %copy-start.5 = (bf16[2,8,64,512]{3,2,1,0:T(8,128)(2,1)}, bf16[2,8,64,512]{3,2,1,0:T(8,128)(2,1)S(1)}, u32[]{:S(2)}) copy-start(bf16[2,8,64,512]{3,2,1,0:T(8,128)(2,1)S(1)} %collective-permute-done.refs_1_) | copy-start | bytes 3145732
  82.3 14.0 %collective-permute-start.2 = (bf16[1,8,64,512]{3,2,1,0:T(8,128)(2,1)S(1)}, bf16[1,8,64,512]{3,2,1,0:T(8,128)(2,1)S(1)}, u32[]{:S(2)}, u32[]{:S(2)}) collective-permute-start(bf16[1,8,64,512]{3,2,1,0:T(8,128)(2,1)S(1)} %slice.52), channel_id=1, source_target_pairs={{0,1},{1,2},{2,3},{3,0},{4,5},{5,6},{6,7},{7,4},{8,9},{9,10},{10,1... | collective-permute-start | bytes 1572872 | tf_op jit(solution)/shard_map/ppermute | solution.py:42
  84.0 12.5 %collective-permute-start.3 = (bf16[1,8,64,512]{3,2,1,0:T(8,128)(2,1)S(1)}, bf16[1,8,64,512]{3,2,1,0:T(8,128)(2,1)S(1)}, u32[]{:S(2)}, u32[]{:S(2)}) collective-permute-start(bf16[1,8,64,512]{3,2,1,0:T(8,128)(2,1)S(1)} %slice.53), channel_id=1, source_target_pairs={{0,3},{1,0},{2,1},{3,2},{4,7},{5,4},{6,5},{7,6},{8,11},{9,8},{10,9... | collective-permute-start | bytes 1572872 | tf_op jit(solution)/shard_map/ppermute | solution.py:43
  85.7 11.6 %copy-start.1 = (bf16[8,4,2,2,8,512]{5,0,1,2,4,3:T(8,128)(2,1)S(1)}, bf16[8,4,2,2,8,512]{5,0,1,2,4,3:T(8,128)(2,1)}, u32[]{:S(2)}) copy-start(bf16[8,4,2,2,8,512]{5,0,1,2,4,3:T(8,128)(2,1)} %copy.10) | copy-start | bytes 3145732
  96.3 0.8 copy-start.10
  96.4 0.8 copy-start.11
  97.3 3.2 %collective-permute-start.4 = (f32[32,8,1024]{2,1,0:T(8,128)}, f32[32,8,1024]{2,1,0:T(8,128)S(1)}, u32[]{:S(2)}, u32[]{:S(2)}) collective-permute-start(f32[32,8,1024]{2,1,0:T(8,128)} %get-tuple-element.24), channel_id=1, source_target_pairs={{0,4},{4,0},{1,5},{5,1},{2,6},{6,2},{3,7},{7,3},{8,12},{12,8},{9,1... | collective-permute-start | bytes 3145736 | tf_op jit(solution)/shard_map/reduce_core/ppermute | solution.py:127
  97.3 26.8 %collective-permute-start.6 = (bf16[2,8,64,512]{3,2,1,0:T(8,128)(2,1)S(1)}, bf16[2,8,64,512]{3,2,1,0:T(8,128)(2,1)S(1)}, u32[]{:S(2)}, u32[]{:S(2)}) collective-permute-start(bf16[2,8,64,512]{3,2,1,0:T(8,128)(2,1)S(1)} %bitcast.28), channel_id=1, source_target_pairs={{0,1},{1,2},{2,3},{3,0},{4,5},{5,6},{6,7},{7,4},{8,9},{9,10},{10,1... | collective-permute-start | bytes 3145736 | tf_op jit(solution)/shard_map/ppermute | solution.py:37
  98.8 25.7 %collective-permute-start.5 = (bf16[2,8,64,512]{3,2,1,0:T(8,128)(2,1)S(1)}, bf16[2,8,64,512]{3,2,1,0:T(8,128)(2,1)}, u32[]{:S(2)}, u32[]{:S(2)}) collective-permute-start(bf16[2,8,64,512]{3,2,1,0:T(8,128)(2,1)S(1)} %bitcast.29), channel_id=1, source_target_pairs={{0,3},{1,0},{2,1},{3,2},{4,7},{5,4},{6,5},{7,6},{8,11},{9,8},{10,9... | collective-permute-start | bytes 3145736 | tf_op jit(solution)/shard_map/ppermute | solution.py:37
  102.9 49.3 %all-to-all-start.2 = ((f32[32,8,1024]{2,1,0:T(8,128)}), f32[32,8,1024]{2,1,0:T(8,128)S(1)}, u32[]{:S(2)}, u32[]{:S(2)}) async-start(f32[32,8,1024]{2,1,0:T(8,128)} %add.16), calls=%async_computation.2 | async-start | bytes 2097152 | tf_op jit(solution)/shard_map/reduce_xz/all_to_all | solution.py:132
  124.1 4.5 %copy-start.6 = (bf16[2,8,64,512]{3,2,1,0:T(8,128)(2,1)}, bf16[2,8,64,512]{3,2,1,0:T(8,128)(2,1)S(1)}, u32[]{:S(2)}) copy-start(bf16[2,8,64,512]{3,2,1,0:T(8,128)(2,1)S(1)} %collective-permute-done.6.refs_3_) | copy-start | bytes 3145732
  124.1 14.8 %collective-permute-start.7 = (bf16[1,8,64,512]{3,2,1,0:T(8,128)(2,1)S(1)}, bf16[1,8,64,512]{3,2,1,0:T(8,128)(2,1)S(1)}, u32[]{:S(2)}, u32[]{:S(2)}) collective-permute-start(bf16[1,8,64,512]{3,2,1,0:T(8,128)(2,1)S(1)} %slice.67), channel_id=1, source_target_pairs={{0,1},{1,2},{2,3},{3,0},{4,5},{5,6},{6,7},{7,4},{8,9},{9,10},{10,1... | collective-permute-start | bytes 1572872 | tf_op jit(solution)/shard_map/ppermute | solution.py:42
  125.6 13.8 %collective-permute-start.8 = (bf16[1,8,64,512]{3,2,1,0:T(8,128)(2,1)S(1)}, bf16[1,8,64,512]{3,2,1,0:T(8,128)(2,1)S(1)}, u32[]{:S(2)}, u32[]{:S(2)}) collective-permute-start(bf16[1,8,64,512]{3,2,1,0:T(8,128)(2,1)S(1)} %slice.68), channel_id=1, source_target_pairs={{0,3},{1,0},{2,1},{3,2},{4,7},{5,4},{6,5},{7,6},{8,11},{9,8},{10,9... | collective-permute-start | bytes 1572872 | tf_op jit(solution)/shard_map/ppermute | solution.py:43
  139.0 0.8 copy-start.3
  139.4 0.8 copy-start.4
  147.0 2.9 %collective-permute-start.9 = (f32[32,8,1024]{2,1,0:T(8,128)}, f32[32,8,1024]{2,1,0:T(8,128)S(1)}, u32[]{:S(2)}, u32[]{:S(2)}) collective-permute-start(f32[32,8,1024]{2,1,0:T(8,128)} %get-tuple-element.30), channel_id=1, source_target_pairs={{0,4},{4,0},{1,5},{5,1},{2,6},{6,2},{3,7},{7,3},{8,12},{12,8},{9,1... | collective-permute-start | bytes 3145736 | tf_op jit(solution)/shard_map/reduce_core/ppermute | solution.py:127
  152.2 35.4 %copy-start.7 = (bf16[16,1024]{1,0:T(8,128)(2,1)S(1)}, bf16[16,1024]{1,0:T(8,128)(2,1)}, u32[]{:S(2)}) copy-start(bf16[16,1024]{1,0:T(8,128)(2,1)} %param.9) | copy-start | bytes 98308
  152.2 35.4 %copy-start.8 = (f32[1024]{0:T(1024)S(1)}, f32[1024]{0:T(1024)}, u32[]{:S(2)}) copy-start(f32[1024]{0:T(1024)} %param.11) | copy-start | bytes 12292
  152.2 35.4 %copy-start.9 = (f32[16]{0:T(128)S(1)}, f32[16]{0:T(128)}, u32[]{:S(2)}) copy-start(f32[16]{0:T(128)} %param.10) | copy-start | bytes 196
  152.2 35.1 %all-to-all-start.3 = ((f32[32,8,1024]{2,1,0:T(8,128)}), f32[32,8,1024]{2,1,0:T(8,128)S(1)}, u32[]{:S(2)}, u32[]{:S(2)}) async-start(f32[32,8,1024]{2,1,0:T(8,128)} %add.17), calls=%async_computation.3 | async-start | bytes 2097152 | tf_op jit(solution)/shard_map/reduce_xz/all_to_all | solution.py:132

commit v6 on v5

--- a/solution.py
+++ b/solution.py
@@ -6,7 +6,6 @@
 from jax.sharding import Mesh, PartitionSpec as P
 
 NZ, NX, NC, NY = 8, 4, 2, 4
-ROWS = 8
 
 
 def ring(size, shift):
@@ -29,34 +28,32 @@
     with jax.named_scope("route"):
         routed = lax.all_to_all(outgoing, ("z", "x", "core"), 0, 0, tiled=True)
     routed = routed.reshape(NZ, NX, NC, rows, cap, width)
-    routed = routed.transpose(3, 4, 2, 1, 0, 5).reshape(rows, cap, tiles, width)
+    routed = [
+        routed[:, :, :, r].transpose(3, 2, 1, 0, 4).reshape(1, cap, tiles, width)
+        for r in range(rows)
+    ]
     return lax.optimization_barrier(routed)
 
 
-def neighbours(own):
-    return lax.ppermute(own, "y", ring(NY, -1)), lax.ppermute(own, "y", ring(NY, 1))
-
-
-def opposite(after, before):
-    half = after.shape[0] // 2
-    low = lax.ppermute(before[:half], "y", ring(NY, 1))
-    high = lax.ppermute(after[half:], "y", ring(NY, -1))
-    return low, high
-
-
-def product(parts, integrals, base=None):
+def forward(row):
+    return lax.ppermute(row, "y", ring(NY, 1))
+
+
+def backward(row):
+    return lax.ppermute(row, "y", ring(NY, -1))
+
+
+def product(parts, integrals):
     cap, width, n = integrals.shape
     group = 4
     tiles = parts[0].shape[2]
     near = tiles // NC
     place = lax.axis_index("core").astype(jnp.int32).reshape(1)
     total = sum(part.shape[0] for part in parts)
-    offset = ROWS - total if base is not None else 0
     steps = cap // group
 
     def body(place_ref, *refs):
-        *refs, integral_ref, kept_ref, away_ref, sum_ref = refs
-        base_refs, row_refs = refs[: len(refs) - len(parts)], refs[len(refs) - len(parts) :]
+        *row_refs, integral_ref, kept_ref, away_ref, sum_ref = refs
         step = pl.program_id(0)
         value = None
         for j in range(group):
@@ -76,13 +73,11 @@
         @pl.when(step == steps - 1)
         def _():
             sums = sum_ref[...] + value
-            for base_ref, out_ref in zip(base_refs, (kept_ref, away_ref)):
-                out_ref[...] = base_ref[...]
 
             def put(first_ref, second_ref):
                 for r in range(total):
-                    first_ref[:, offset + r, :] = sums[r, :near]
-                    second_ref[:, offset + r, :] = sums[r, near:]
+                    first_ref[:, r, :] = sums[r, :near]
+                    second_ref[:, r, :] = sums[r, near:]
 
             @pl.when(place_ref[0] == 0)
             def _():
@@ -92,20 +87,18 @@
             def _():
                 put(away_ref, kept_ref)
 
-    out = jax.ShapeDtypeStruct((near, ROWS, n), jnp.float32)
-    out_spec = pl.BlockSpec((near, ROWS, n), lambda i, place: (0, 0, 0))
+    out = jax.ShapeDtypeStruct((near, total, n), jnp.float32)
+    out_spec = pl.BlockSpec((near, total, n), lambda i, place: (0, 0, 0))
     row_specs = [
         pl.BlockSpec((part.shape[0], group, tiles, width), lambda i, place: (0, i, 0, 0))
         for part in parts
     ]
-    base = [] if base is None else list(base)
     return pl.pallas_call(
         body,
         grid_spec=pltpu.PrefetchScalarGridSpec(
             num_scalar_prefetch=1,
             grid=(steps,),
-            in_specs=[out_spec] * len(base)
-            + row_specs
+            in_specs=row_specs
             + [pl.BlockSpec((group, width, n), lambda i, place: (i, 0, 0))],
             out_specs=[out_spec, out_spec],
             scratch_shapes=[pltpu.VMEM((total, tiles, n), jnp.float32)],
@@ -118,7 +111,7 @@
             transcendentals=0,
         ),
         name="product",
-    )(place, *base, *parts, integrals)
+    )(place, *parts, integrals)
 
 
 def over_core(sums):
@@ -130,6 +123,19 @@
 def over_xz(outgoing):
     with jax.named_scope("reduce_xz"):
         return jnp.sum(lax.all_to_all(outgoing, ("x", "z"), 0, 0, tiled=True), axis=0)
+
+
+def over_x_then_z(outgoing, earlier):
+    x = lax.axis_index("x")
+    outgoing = outgoing.reshape(NX, NZ, *outgoing.shape[1:])
+    with jax.named_scope("reduce_x"):
+        total = lax.dynamic_index_in_dim(outgoing, x, 0, keepdims=False)
+        for shift in (1, 3, 2):
+            away = lax.dynamic_index_in_dim(outgoing, (x + shift) % NX, 0, keepdims=False)
+            total += lax.ppermute(away, "x", ring(NX, shift))
+    with jax.named_scope("reduce_z"):
+        (total,) = after_that(earlier, total)
+        return jnp.sum(lax.all_to_all(total, "z", 0, 0, tiled=True), axis=0)
 
 
 def per_device(amplitudes, integrals, slot_block, rest, occ_energy, vir_energy):
@@ -146,19 +152,24 @@
     outgoing_later = gather_rows(amplitudes[step:], picker)
     own = route(outgoing)
     (outgoing_later,) = after_that(own, outgoing_later)
-    after, before = neighbours(own)
+    after = [backward(row) for row in own]
+    before = [forward(row) for row in own]
     later = route(outgoing_later)
     (later,) = after_that((after, before), later)
-    low, high = opposite(*after_that(later, after, before))
-    after_later, before_later = neighbours(later)
-    low_later, high_later = opposite(after_later, before_later)
-    kept, away = product([own, after, before, later], integrals)
-    low, high, away = lax.optimization_barrier((low, high, away))
+    across = [forward(before[0]), backward(after[1])]
+    before_later = [forward(later[0])]
+    after_later = [backward(later[1])]
+    kept, away = product([*own, *after, *before, *later], integrals)
+    (away,) = after_that((across, before_later, after_later), away)
     early = over_core((kept, away))
+    (across,) = after_that(early, across)
     early = over_xz(early)
-    late = product([low, high, after_later, before_later], integrals)
-    late = product([low_later, high_later], integrals, late)
-    late = over_xz(over_core(late))
+
+    across_later = [forward(before_later[0]), backward(after_later[0])]
+    before_later = [before_later[0], forward(later[1])]
+    after_later = [backward(later[0]), after_later[0]]
+    late = product([*across, *after_later, *before_later, *across_later], integrals)
+    late = over_x_then_z(over_core(late), early)
 
     early = early.reshape(4, step, n)
     late = late.reshape(4, step, n)

time: 192 us -> 182 us (0.948); the launches traced: 188 us -> 181 us
  starting transfers between devices: 48.1 us -> 56.8 us
  waiting for transfers between devices: 98.2 us -> 91.5 us
  Pallas kernels: 24.9 us -> 19.6 us
  local copies, waits for them, and re-layouts: 7.45 us -> 2.6 us
    all_to_all x2 -> x1, waiting for transfers between devices: 26.3 us -> 0.01 us  [over_xz(): lax.all_to_all(outgoing, ('x', 'z'), 0, 0, tiled=True)]
    ppermute x8 -> x15, waiting for transfers between devices: 16 us -> 40 us  [the longest x6 28.4 us: forward(): return lax.ppermute(row, 'y', ring(NY, 1))]
    all_to_all x2, waiting for transfers between devices: 53 us -> 36.7 us  [route(): routed = lax.all_to_all(outgoing, ('z', 'x', 'core'), 0, 0, tiled=True)]
    all_to_all x0 -> x1, waiting for transfers between devices: none -> 12 us  [over_x_then_z(): return jnp.sum(lax.all_to_all(total, 'z', 0, 0, tiled=True), axis=0)]
    ppermute x8 -> x15, starting transfers between devices: 13.1 us -> 22.4 us  [the longest x6 13.7 us: backward(): return lax.ppermute(row, 'y', ring(NY, -1))]
    all_to_all x2 -> x1, starting transfers between devices: 17.3 us -> 9.9 us  [over_xz(): lax.all_to_all(outgoing, ('x', 'z'), 0, 0, tiled=True)]
    all_to_all x0 -> x1, starting transfers between devices: none -> 6.78 us  [over_x_then_z(): return jnp.sum(lax.all_to_all(total, 'z', 0, 0, tiled=True), axis=0)]
    pallas_call x3 -> x2, Pallas kernels: 24.9 us -> 19.6 us  [product(): pl.pallas_call(body, grid_spec=pltpu.PrefetchScalarGridSpec(num_scalar_pr...]
  transfers between devices with their start and end apart: 14 -> 21, of which waited for: 9 -> 11; matrix products, arithmetic and copies ran while one was open for 5% -> 4% of each run, Pallas kernels for 13% -> 11%
where the time goes in v6:
time: 182 us; the launch traced here: 181 us
  waiting for transfers between devices  91.5 us (50%)
  starting transfers between devices  56.8 us (31%)
  Pallas kernels  19.6 us (11%)
  other arithmetic  6.22 us (3%)
  matrix products  3.96 us (2%)
  local copies, waits for them, and re-layouts  2.6 us (1%)
    all_to_all x2, waiting for transfers between devices, route(): routed = lax.all_to_all(outgoing, ('z', 'x', 'core'), 0, 0, tiled=True)  36.7 us
    ppermute x6, waiting for transfers between devices, forward(): return lax.ppermute(row, 'y', ring(NY, 1))  28.4 us
    pallas_call x2, Pallas kernels, product(): pl.pallas_call(body, grid_spec=pltpu.PrefetchScalarGridSpec(num_scalar_pr...  19.6 us
    all_to_all x2, starting transfers between devices, route(): routed = lax.all_to_all(outgoing, ('z', 'x', 'core'), 0, 0, tiled=True)  17.7 us
    ppermute x6, starting transfers between devices, backward(): return lax.ppermute(row, 'y', ring(NY, -1))  13.7 us
    all_to_all x1, waiting for transfers between devices, over_x_then_z(): return jnp.sum(lax.all_to_all(total, 'z', 0, 0, tiled=True), axis=0)  12 us
    ppermute x3, waiting for transfers between devices, over_x_then_z(): total += lax.ppermute(away, 'x', ring(NX, shift))  11.5 us
    all_to_all x1, starting transfers between devices, over_xz(): lax.all_to_all(outgoing, ('x', 'z'), 0, 0, tiled=True)  9.9 us
  transfers between devices with their start and end apart: 21, of which 11 were waited for; matrix products, arithmetic and copies ran while one was open for 4% of the time, Pallas kernels for 11%

profile of v6, /device:TPU:2, one launch (start us, length us, event | category | flops | bytes accessed | tf_op | source)
XLA Modules:
  0.0 181.0 jit_solution(12490049356093874319)
XLA Ops:
  0.0 0.9 eq.21
  0.9 2.5 %fusion = bf16[64,2,8,512]{3,2,1,0:T(8,128)(2,1)} fusion(bf16[4,256,512]{2,1,0:T(8,128)(2,1)} %param.6, s32[64,8]{1,0:T(8,128)S(1)} %eq.21), kind=kOutput, calls=%fused_computation.2 | convolution fusion | flops 269090816 | bytes 1574912 | tf_op jit(solution)/shard_map/pick/tsg,rgb->trsb/dot_general | solution.py:21
  3.4 12.0 %all-to-all-start = ((bf16[64,2,8,512]{3,2,1,0:T(8,128)(2,1)}), bf16[64,2,8,512]{3,2,1,0:T(8,128)(2,1)S(1)}, u32[]{:S(2)}, u32[]{:S(2)}) async-start(bf16[64,2,8,512]{3,2,1,0:T(8,128)(2,1)} %fusion), calls=%async_computation | async-start | bytes 2097152 | tf_op jit(solution)/shard_map/route/all_to_all | solution.py:29
  15.4 1.5 fusion.1
  16.9 27.3 %all-to-all-done = bf16[64,2,8,512]{3,2,1,0:T(8,128)(2,1)S(1)} async-done(((bf16[64,2,8,512]{3,2,1,0:T(8,128)(2,1)}), bf16[64,2,8,512]{3,2,1,0:T(8,128)(2,1)S(1)}, u32[]{:S(2)}, u32[]{:S(2)}) %all-to-all-start) | async-done | bytes 1048608 | tf_op jit(solution)/shard_map/route/all_to_all | solution.py:29
  45.0 5.7 %all-to-all-start.1 = ((bf16[64,2,8,512]{3,2,1,0:T(8,128)(2,1)}), bf16[64,2,8,512]{3,2,1,0:T(8,128)(2,1)S(1)}, u32[]{:S(2)}, u32[]{:S(2)}) async-start(bf16[64,2,8,512]{3,2,1,0:T(8,128)(2,1)} %fusion.1), calls=%async_computation.1 | async-start | bytes 2097152 | tf_op jit(solution)/shard_map/route/all_to_all | solution.py:29
  50.6 1.7 collective-permute-start.2
  52.3 1.7 collective-permute-start.1
  54.0 1.8 collective-permute-start
  56.0 10.8 %collective-permute-done.2.refs_4_ = bf16[1,8,64,512]{3,2,1,0:T(8,128)(2,1)} collective-permute-done((bf16[1,8,64,512]{3,2,1,0:T(8,128)(2,1)S(1)}, bf16[1,8,64,512]{3,2,1,0:T(8,128)(2,1)}, u32[]{:S(2)}, u32[]{:S(2)}) %collective-permute-start.2) | collective-permute-done | bytes 524320 | tf_op jit(solution)/shard_map/ppermute | solution.py:39
  67.2 2.9 %collective-permute-start.5 = (bf16[1,8,64,512]{3,2,1,0:T(8,128)(2,1)}, bf16[1,8,64,512]{3,2,1,0:T(8,128)(2,1)S(1)}, u32[]{:S(2)}, u32[]{:S(2)}) collective-permute-start(bf16[1,8,64,512]{3,2,1,0:T(8,128)(2,1)} %collective-permute-done.1.refs_3_), channel_id=1, source_target_pairs={{0,3},{1,0},{2,1},{3,2},{4,7},{5,4},{6,5},{7,6},{8,11},{9,8},{10,9... | collective-permute-start | bytes 1572872 | tf_op jit(solution)/shard_map/ppermute | solution.py:43
  70.1 9.4 %all-to-all-done.1 = bf16[64,2,8,512]{3,2,1,0:T(8,128)(2,1)S(1)} async-done(((bf16[64,2,8,512]{3,2,1,0:T(8,128)(2,1)}), bf16[64,2,8,512]{3,2,1,0:T(8,128)(2,1)S(1)}, u32[]{:S(2)}, u32[]{:S(2)}) %all-to-all-start.1) | async-done | bytes 1048608 | tf_op jit(solution)/shard_map/route/all_to_all | solution.py:29
  80.2 1.7 collective-permute-start.6
  81.9 1.7 collective-permute-start.7
  83.6 9.8 %product.2 = (f32[32,8,1024]{2,1,0:T(8,128)}, f32[32,8,1024]{2,1,0:T(8,128)}) custom-call(s32[1]{0:T(128)} %bitcast.place_ref, bf16[1,8,64,512]{3,2,1,0:T(8,128)(2,1)} %bitcast.64, bf16[1,8,64,512]{3,2,1,0:T(8,128)(2,1)} %bitcast.67, bf16[1,8,64,512]{3,2,1,0:T(8,128)(2,1)} %collective-permute-done.refs_2_, ...), custom_call_target="tpu_custom_call" | custom-call | flops 4294967296 | bytes 14680064 | tf_op jit(solution)/shard_map/product/pallas_call | solution.py:96
  93.4 6.3 %collective-permute-done.6.refs_4_ = bf16[1,8,64,512]{3,2,1,0:T(8,128)(2,1)} collective-permute-done((bf16[1,8,64,512]{3,2,1,0:T(8,128)(2,1)S(1)}, bf16[1,8,64,512]{3,2,1,0:T(8,128)(2,1)}, u32[]{:S(2)}, u32[]{:S(2)}) %collective-permute-start.6) | collective-permute-done | bytes 524320 | tf_op jit(solution)/shard_map/ppermute | solution.py:39
  99.8 3.0 %collective-permute-start.9 = (bf16[1,8,64,512]{3,2,1,0:T(8,128)(2,1)}, bf16[1,8,64,512]{3,2,1,0:T(8,128)(2,1)S(1)}, u32[]{:S(2)}, u32[]{:S(2)}) collective-permute-start(bf16[1,8,64,512]{3,2,1,0:T(8,128)(2,1)} %bitcast.61), channel_id=1, source_target_pairs={{0,3},{1,0},{2,1},{3,2},{4,7},{5,4},{6,5},{7,6},{8,11},{9,8},{10,9... | collective-permute-start | bytes 1572872 | tf_op jit(solution)/shard_map/ppermute | solution.py:43
  103.4 2.7 %collective-permute-start.12 = (bf16[1,8,64,512]{3,2,1,0:T(8,128)(2,1)}, bf16[1,8,64,512]{3,2,1,0:T(8,128)(2,1)}, u32[]{:S(2)}, u32[]{:S(2)}) collective-permute-start(bf16[1,8,64,512]{3,2,1,0:T(8,128)(2,1)} %collective-permute-done.7.refs_3_), channel_id=1, source_target_pairs={{0,3},{1,0},{2,1},{3,2},{4,7},{5,4},{6,5},{7,6},{8,11},{9,8},{10,9... | collective-permute-start | bytes 1572872 | tf_op jit(solution)/shard_map/ppermute | solution.py:43
  106.1 2.3 %add.56 = f32[32,8,1024]{2,1,0:T(8,128)} add(f32[32,8,1024]{2,1,0:T(8,128)} %get-tuple-element.27, f32[32,8,1024]{2,1,0:T(8,128)S(1)} %collective-permute-done.8) | non-fusion elementwise | flops 262144 | bytes 3145728 | tf_op jit(solution)/shard_map/reduce_core/add | solution.py:120
  108.4 9.9 %all-to-all-start.2 = ((f32[32,8,1024]{2,1,0:T(8,128)}), f32[32,8,1024]{2,1,0:T(8,128)S(1)}, u32[]{:S(2)}, u32[]{:S(2)}) async-start(f32[32,8,1024]{2,1,0:T(8,128)} %add.56), calls=%async_computation.2 | async-start | bytes 2097152 | tf_op jit(solution)/shard_map/reduce_xz/all_to_all | solution.py:125
  119.0 10.6 %collective-permute-done.11.refs_6_ = bf16[1,8,64,512]{3,2,1,0:T(8,128)(2,1)} collective-permute-done((bf16[1,8,64,512]{3,2,1,0:T(8,128)(2,1)}, bf16[1,8,64,512]{3,2,1,0:T(8,128)(2,1)}, u32[]{:S(2)}, u32[]{:S(2)}) %collective-permute-start.11) | collective-permute-done | bytes 524320 | tf_op jit(solution)/shard_map/ppermute | solution.py:39
  129.7 9.8 %product.3 = (f32[32,8,1024]{2,1,0:T(8,128)}, f32[32,8,1024]{2,1,0:T(8,128)}) custom-call(s32[1]{0:T(128)} %bitcast.place_ref, bf16[1,8,64,512]{3,2,1,0:T(8,128)(2,1)} %copy-done.8, bf16[1,8,64,512]{3,2,1,0:T(8,128)(2,1)} %copy-done.9, bf16[1,8,64,512]{3,2,1,0:T(8,128)(2,1)} %copy-done.10, bf16[1,8,64,512]{3,2,1,0:T(8,128)(2,1)} %collective-permute-done.7.refs_3_, ...), custom_call_target="tpu_custom_call" | custom-call | flops 4294967296 | bytes 14680064 | tf_op jit(solution)/shard_map/product/pallas_call | solution.py:96
  139.5 2.8 %collective-permute-done.13 = f32[32,8,1024]{2,1,0:T(8,128)S(1)} collective-permute-done((f32[32,8,1024]{2,1,0:T(8,128)}, f32[32,8,1024]{2,1,0:T(8,128)S(1)}, u32[]{:S(2)}, u32[]{:S(2)}) %collective-permute-start.13) | collective-permute-done | bytes 1048608 | tf_op jit(solution)/shard_map/reduce_core/ppermute | solution.py:120
  142.3 1.4 add.57
  143.8 2.2 %collective-permute-start.16 = (f32[8,8,1024]{2,1,0:T(8,128)S(1)}, f32[8,8,1024]{2,1,0:T(8,128)S(1)}, u32[]{:S(2)}, u32[]{:S(2)}) collective-permute-start(f32[8,8,1024]{2,1,0:T(8,128)S(1)} %get-tuple-element.36), channel_id=1, source_target_pairs={{0,16},{8,24},{16,0},{24,8},{1,17},{9,25},{17,1},{25,9},{2,18},{10... | collective-permute-start | bytes 786440 | tf_op jit(solution)/shard_map/reduce_x/ppermute | solution.py:135
  146.0 1.5 collective-permute-start.15
  148.0 6.6 %collective-permute-done.16 = f32[8,8,1024]{2,1,0:T(8,128)S(1)} collective-permute-done((f32[8,8,1024]{2,1,0:T(8,128)S(1)}, f32[8,8,1024]{2,1,0:T(8,128)S(1)}, u32[]{:S(2)}, u32[]{:S(2)}) %collective-permute-start.16) | collective-permute-done | bytes 262176 | tf_op jit(solution)/shard_map/reduce_x/ppermute | solution.py:135
  154.6 4.8 %collective-permute-done.15 = f32[8,8,1024]{2,1,0:T(8,128)S(1)} collective-permute-done((f32[8,8,1024]{2,1,0:T(8,128)S(1)}, f32[8,8,1024]{2,1,0:T(8,128)S(1)}, u32[]{:S(2)}, u32[]{:S(2)}) %collective-permute-start.15) | collective-permute-done | bytes 262176 | tf_op jit(solution)/shard_map/reduce_x/ppermute | solution.py:135
  159.5 1.7 fusion.10
  161.3 6.8 %all-to-all-start.3 = ((f32[8,8,1024]{2,1,0:T(8,128)}), f32[8,8,1024]{2,1,0:T(8,128)S(1)}, u32[]{:S(2)}, u32[]{:S(2)}) async-start(f32[8,8,1024]{2,1,0:T(8,128)} %fusion.10), calls=%async_computation.3 | async-start | bytes 524288 | tf_op jit(solution)/shard_map/reduce_z/all_to_all | solution.py:138
  168.1 12.0 %all-to-all-done.3 = f32[8,8,1024]{2,1,0:T(8,128)S(1)} async-done(((f32[8,8,1024]{2,1,0:T(8,128)}), f32[8,8,1024]{2,1,0:T(8,128)S(1)}, u32[]{:S(2)}, u32[]{:S(2)}) %all-to-all-start.3) | async-done | bytes 262176 | tf_op jit(solution)/shard_map/reduce_z/all_to_all | solution.py:138
  180.3 0.7 divide_convert_fusion
  (58 shorter events, 4.5 us)
Async XLA Ops:
  0.0 15.4 %copy-start = (bf16[4,256,512]{2,1,0:T(8,128)(2,1)S(1)}, bf16[4,256,512]{2,1,0:T(8,128)(2,1)}, u32[]{:S(2)}) copy-start(bf16[4,256,512]{2,1,0:T(8,128)(2,1)} %param.6) | copy-start | bytes 3145732
  3.4 40.8 %all-to-all-start = ((bf16[64,2,8,512]{3,2,1,0:T(8,128)(2,1)}), bf16[64,2,8,512]{3,2,1,0:T(8,128)(2,1)S(1)}, u32[]{:S(2)}, u32[]{:S(2)}) async-start(bf16[64,2,8,512]{3,2,1,0:T(8,128)(2,1)} %fusion), calls=%async_computation | async-start | bytes 2097152 | tf_op jit(solution)/shard_map/route/all_to_all | solution.py:29
  44.6 34.9 %copy-start.3 = (bf16[8,4,2,1,8,512]{5,0,1,2,4,3:T(8,128)(2,1)}, bf16[8,4,2,1,8,512]{5,0,1,2,4,3:T(8,128)(2,1)S(1)}, u32[]{:S(2)}) copy-start(bf16[8,4,2,1,8,512]{5,0,1,2,4,3:T(8,128)(2,1)S(1)} %copy.16) | copy-start | bytes 1572868
  45.0 34.6 %copy-start.4 = (bf16[8,4,2,1,8,512]{5,0,1,2,4,3:T(8,128)(2,1)}, bf16[8,4,2,1,8,512]{5,0,1,2,4,3:T(8,128)(2,1)S(1)}, u32[]{:S(2)}) copy-start(bf16[8,4,2,1,8,512]{5,0,1,2,4,3:T(8,128)(2,1)S(1)} %copy.17) | copy-start | bytes 1572868
  45.0 34.5 %all-to-all-start.1 = ((bf16[64,2,8,512]{3,2,1,0:T(8,128)(2,1)}), bf16[64,2,8,512]{3,2,1,0:T(8,128)(2,1)S(1)}, u32[]{:S(2)}, u32[]{:S(2)}) async-start(bf16[64,2,8,512]{3,2,1,0:T(8,128)(2,1)} %fusion.1), calls=%async_computation.1 | async-start | bytes 2097152 | tf_op jit(solution)/shard_map/route/all_to_all | solution.py:29
  50.6 16.1 %collective-permute-start.2 = (bf16[1,8,64,512]{3,2,1,0:T(8,128)(2,1)S(1)}, bf16[1,8,64,512]{3,2,1,0:T(8,128)(2,1)}, u32[]{:S(2)}, u32[]{:S(2)}) collective-permute-start(bf16[1,8,64,512]{3,2,1,0:T(8,128)(2,1)S(1)} %bitcast.62), channel_id=1, source_target_pairs={{0,1},{1,2},{2,3},{3,0},{4,5},{5,6},{6,7},{7,4},{8,9},{9,10},{10,1... | collective-permute-start | bytes 1572872 | tf_op jit(solution)/shard_map/ppermute | solution.py:39
  52.3 14.9 %collective-permute-start.1 = (bf16[1,8,64,512]{3,2,1,0:T(8,128)(2,1)S(1)}, bf16[1,8,64,512]{3,2,1,0:T(8,128)(2,1)}, u32[]{:S(2)}, u32[]{:S(2)}) collective-permute-start(bf16[1,8,64,512]{3,2,1,0:T(8,128)(2,1)S(1)} %bitcast.65), channel_id=1, source_target_pairs={{0,3},{1,0},{2,1},{3,2},{4,7},{5,4},{6,5},{7,6},{8,11},{9,8},{10,9... | collective-permute-start | bytes 1572872 | tf_op jit(solution)/shard_map/ppermute | solution.py:43
  54.0 26.3 %collective-permute-start = (bf16[1,8,64,512]{3,2,1,0:T(8,128)(2,1)S(1)}, bf16[1,8,64,512]{3,2,1,0:T(8,128)(2,1)}, u32[]{:S(2)}, u32[]{:S(2)}) collective-permute-start(bf16[1,8,64,512]{3,2,1,0:T(8,128)(2,1)S(1)} %bitcast.63), channel_id=1, source_target_pairs={{0,3},{1,0},{2,1},{3,2},{4,7},{5,4},{6,5},{7,6},{8,11},{9,8},{10,9... | collective-permute-start | bytes 1572872 | tf_op jit(solution)/shard_map/ppermute | solution.py:43
  55.8 24.5 %collective-permute-start.3 = (bf16[1,8,64,512]{3,2,1,0:T(8,128)(2,1)S(1)}, bf16[1,8,64,512]{3,2,1,0:T(8,128)(2,1)}, u32[]{:S(2)}, u32[]{:S(2)}) collective-permute-start(bf16[1,8,64,512]{3,2,1,0:T(8,128)(2,1)S(1)} %bitcast.66), channel_id=1, source_target_pairs={{0,1},{1,2},{2,3},{3,0},{4,5},{5,6},{6,7},{7,4},{8,9},{9,10},{10,1... | collective-permute-start | bytes 1572872 | tf_op jit(solution)/shard_map/ppermute | solution.py:39
  66.8 26.6 %collective-permute-start.4 = (bf16[1,8,64,512]{3,2,1,0:T(8,128)(2,1)}, bf16[1,8,64,512]{3,2,1,0:T(8,128)(2,1)S(1)}, u32[]{:S(2)}, u32[]{:S(2)}) collective-permute-start(bf16[1,8,64,512]{3,2,1,0:T(8,128)(2,1)} %collective-permute-done.2.refs_4_), channel_id=1, source_target_pairs={{0,1},{1,2},{2,3},{3,0},{4,5},{5,6},{6,7},{7,4},{8,9},{9,10},{10,1... | collective-permute-start | bytes 1572872 | tf_op jit(solution)/shard_map/ppermute | solution.py:39
  67.2 26.2 %collective-permute-start.5 = (bf16[1,8,64,512]{3,2,1,0:T(8,128)(2,1)}, bf16[1,8,64,512]{3,2,1,0:T(8,128)(2,1)S(1)}, u32[]{:S(2)}, u32[]{:S(2)}) collective-permute-start(bf16[1,8,64,512]{3,2,1,0:T(8,128)(2,1)} %collective-permute-done.1.refs_3_), channel_id=1, source_target_pairs={{0,3},{1,0},{2,1},{3,2},{4,7},{5,4},{6,5},{7,6},{8,11},{9,8},{10,9... | collective-permute-start | bytes 1572872 | tf_op jit(solution)/shard_map/ppermute | solution.py:43
  79.9 3.7 %copy-start.2 = (bf16[8,4,2,1,8,512]{5,0,1,2,4,3:T(8,128)(2,1)}, bf16[8,4,2,1,8,512]{5,0,1,2,4,3:T(8,128)(2,1)S(1)}, u32[]{:S(2)}) copy-start(bf16[8,4,2,1,8,512]{5,0,1,2,4,3:T(8,128)(2,1)S(1)} %copy.18) | copy-start | bytes 1572868
  80.2 19.5 %collective-permute-start.6 = (bf16[1,8,64,512]{3,2,1,0:T(8,128)(2,1)S(1)}, bf16[1,8,64,512]{3,2,1,0:T(8,128)(2,1)}, u32[]{:S(2)}, u32[]{:S(2)}) collective-permute-start(bf16[1,8,64,512]{3,2,1,0:T(8,128)(2,1)S(1)} %bitcast.59), channel_id=1, source_target_pairs={{0,1},{1,2},{2,3},{3,0},{4,5},{5,6},{6,7},{7,4},{8,9},{9,10},{10,1... | collective-permute-start | bytes 1572872 | tf_op jit(solution)/shard_map/ppermute | solution.py:39
  81.9 17.9 %collective-permute-start.7 = (bf16[1,8,64,512]{3,2,1,0:T(8,128)(2,1)S(1)}, bf16[1,8,64,512]{3,2,1,0:T(8,128)(2,1)}, u32[]{:S(2)}, u32[]{:S(2)}) collective-permute-start(bf16[1,8,64,512]{3,2,1,0:T(8,128)(2,1)S(1)} %bitcast.56), channel_id=1, source_target_pairs={{0,3},{1,0},{2,1},{3,2},{4,7},{5,4},{6,5},{7,6},{8,11},{9,8},{10,9... | collective-permute-start | bytes 1572872 | tf_op jit(solution)/shard_map/ppermute | solution.py:43
  93.4 15.0 %copy-start.8 = (bf16[1,8,64,512]{3,2,1,0:T(8,128)(2,1)}, bf16[1,8,64,512]{3,2,1,0:T(8,128)(2,1)S(1)}, u32[]{:S(2)}) copy-start(bf16[1,8,64,512]{3,2,1,0:T(8,128)(2,1)S(1)} %collective-permute-done.4.refs_0_) | copy-start | bytes 1572868
  93.4 15.0 %copy-start.9 = (bf16[1,8,64,512]{3,2,1,0:T(8,128)(2,1)}, bf16[1,8,64,512]{3,2,1,0:T(8,128)(2,1)S(1)}, u32[]{:S(2)}) copy-start(bf16[1,8,64,512]{3,2,1,0:T(8,128)(2,1)S(1)} %collective-permute-done.5.refs_1_) | copy-start | bytes 1572868
  99.8 6.3 %collective-permute-start.8 = (f32[32,8,1024]{2,1,0:T(8,128)}, f32[32,8,1024]{2,1,0:T(8,128)S(1)}, u32[]{:S(2)}, u32[]{:S(2)}) collective-permute-start(f32[32,8,1024]{2,1,0:T(8,128)} %get-tuple-element.29), channel_id=1, source_target_pairs={{0,4},{4,0},{1,5},{5,1},{2,6},{6,2},{3,7},{7,3},{8,12},{12,8},{9,1... | collective-permute-start | bytes 3145736 | tf_op jit(solution)/shard_map/reduce_core/ppermute | solution.py:120
  99.8 18.5 %collective-permute-start.9 = (bf16[1,8,64,512]{3,2,1,0:T(8,128)(2,1)}, bf16[1,8,64,512]{3,2,1,0:T(8,128)(2,1)S(1)}, u32[]{:S(2)}, u32[]{:S(2)}) collective-permute-start(bf16[1,8,64,512]{3,2,1,0:T(8,128)(2,1)} %bitcast.61), channel_id=1, source_target_pairs={{0,3},{1,0},{2,1},{3,2},{4,7},{5,4},{6,5},{7,6},{8,11},{9,8},{10,9... | collective-permute-start | bytes 1572872 | tf_op jit(solution)/shard_map/ppermute | solution.py:43
  102.8 16.2 %collective-permute-start.10 = (bf16[1,8,64,512]{3,2,1,0:T(8,128)(2,1)}, bf16[1,8,64,512]{3,2,1,0:T(8,128)(2,1)S(1)}, u32[]{:S(2)}, u32[]{:S(2)}) collective-permute-start(bf16[1,8,64,512]{3,2,1,0:T(8,128)(2,1)} %bitcast.58), channel_id=1, source_target_pairs={{0,1},{1,2},{2,3},{3,0},{4,5},{5,6},{6,7},{7,4},{8,9},{9,10},{10,1... | collective-permute-start | bytes 1572872 | tf_op jit(solution)/shard_map/ppermute | solution.py:39
  102.8 26.8 %collective-permute-start.11 = (bf16[1,8,64,512]{3,2,1,0:T(8,128)(2,1)}, bf16[1,8,64,512]{3,2,1,0:T(8,128)(2,1)}, u32[]{:S(2)}, u32[]{:S(2)}) collective-permute-start(bf16[1,8,64,512]{3,2,1,0:T(8,128)(2,1)} %collective-permute-done.6.refs_4_), channel_id=1, source_target_pairs={{0,1},{1,2},{2,3},{3,0},{4,5},{5,6},{6,7},{7,4},{8,9},{9,10},{10,1... | collective-permute-start | bytes 1572872 | tf_op jit(solution)/shard_map/ppermute | solution.py:39
  103.4 26.2 %collective-permute-start.12 = (bf16[1,8,64,512]{3,2,1,0:T(8,128)(2,1)}, bf16[1,8,64,512]{3,2,1,0:T(8,128)(2,1)}, u32[]{:S(2)}, u32[]{:S(2)}) collective-permute-start(bf16[1,8,64,512]{3,2,1,0:T(8,128)(2,1)} %collective-permute-done.7.refs_3_), channel_id=1, source_target_pairs={{0,3},{1,0},{2,1},{3,2},{4,7},{5,4},{6,5},{7,6},{8,11},{9,8},{10,9... | collective-permute-start | bytes 1572872 | tf_op jit(solution)/shard_map/ppermute | solution.py:43
  108.4 52.8 %all-to-all-start.2 = ((f32[32,8,1024]{2,1,0:T(8,128)}), f32[32,8,1024]{2,1,0:T(8,128)S(1)}, u32[]{:S(2)}, u32[]{:S(2)}) async-start(f32[32,8,1024]{2,1,0:T(8,128)} %add.56), calls=%async_computation.2 | async-start | bytes 2097152 | tf_op jit(solution)/shard_map/reduce_xz/all_to_all | solution.py:125
  118.4 11.3 %copy-start.10 = (bf16[1,8,64,512]{3,2,1,0:T(8,128)(2,1)}, bf16[1,8,64,512]{3,2,1,0:T(8,128)(2,1)S(1)}, u32[]{:S(2)}) copy-start(bf16[1,8,64,512]{3,2,1,0:T(8,128)(2,1)S(1)} %collective-permute-done.9.refs_2_) | copy-start | bytes 1572868
  119.0 10.6 %copy-start.11 = (bf16[1,8,64,512]{3,2,1,0:T(8,128)(2,1)}, bf16[1,8,64,512]{3,2,1,0:T(8,128)(2,1)S(1)}, u32[]{:S(2)}) copy-start(bf16[1,8,64,512]{3,2,1,0:T(8,128)(2,1)S(1)} %collective-permute-done.10.refs_5_) | copy-start | bytes 1572868
  139.4 2.9 %collective-permute-start.13 = (f32[32,8,1024]{2,1,0:T(8,128)}, f32[32,8,1024]{2,1,0:T(8,128)S(1)}, u32[]{:S(2)}, u32[]{:S(2)}) collective-permute-start(f32[32,8,1024]{2,1,0:T(8,128)} %get-tuple-element.33), channel_id=1, source_target_pairs={{0,4},{4,0},{1,5},{5,1},{2,6},{6,2},{3,7},{7,3},{8,12},{12,8},{9,1... | collective-permute-start | bytes 3145736 | tf_op jit(solution)/shard_map/reduce_core/ppermute | solution.py:120
  143.8 36.5 %copy-start.5 = (bf16[16,1024]{1,0:T(8,128)(2,1)S(1)}, bf16[16,1024]{1,0:T(8,128)(2,1)}, u32[]{:S(2)}) copy-start(bf16[16,1024]{1,0:T(8,128)(2,1)} %param.9) | copy-start | bytes 98308
  143.8 36.5 %copy-start.6 = (f32[1024]{0:T(1024)S(1)}, f32[1024]{0:T(1024)}, u32[]{:S(2)}) copy-start(f32[1024]{0:T(1024)} %param.11) | copy-start | bytes 12292
  143.8 36.5 %copy-start.7 = (f32[16]{0:T(128)S(1)}, f32[16]{0:T(128)}, u32[]{:S(2)}) copy-start(f32[16]{0:T(128)} %param.10) | copy-start | bytes 196
  143.8 10.8 %collective-permute-start.16 = (f32[8,8,1024]{2,1,0:T(8,128)S(1)}, f32[8,8,1024]{2,1,0:T(8,128)S(1)}, u32[]{:S(2)}, u32[]{:S(2)}) collective-permute-start(f32[8,8,1024]{2,1,0:T(8,128)S(1)} %get-tuple-element.36), channel_id=1, source_target_pairs={{0,16},{8,24},{16,0},{24,8},{1,17},{9,25},{17,1},{25,9},{2,18},{10... | collective-permute-start | bytes 786440 | tf_op jit(solution)/shard_map/reduce_x/ppermute | solution.py:135
  146.0 13.4 %collective-permute-start.15 = (f32[8,8,1024]{2,1,0:T(8,128)S(1)}, f32[8,8,1024]{2,1,0:T(8,128)S(1)}, u32[]{:S(2)}, u32[]{:S(2)}) collective-permute-start(f32[8,8,1024]{2,1,0:T(8,128)S(1)} %get-tuple-element.37), channel_id=1, source_target_pairs={{0,24},{8,0},{16,8},{24,16},{1,25},{9,1},{17,9},{25,17},{2,26},{10... | collective-permute-start | bytes 786440 | tf_op jit(solution)/shard_map/reduce_x/ppermute | solution.py:135
  147.4 12.1 %collective-permute-start.14 = (f32[8,8,1024]{2,1,0:T(8,128)S(1)}, f32[8,8,1024]{2,1,0:T(8,128)}, u32[]{:S(2)}, u32[]{:S(2)}) collective-permute-start(f32[8,8,1024]{2,1,0:T(8,128)S(1)} %get-tuple-element.35), channel_id=1, source_target_pairs={{0,8},{8,16},{16,24},{24,0},{1,9},{9,17},{17,25},{25,1},{2,10},{10... | collective-permute-start | bytes 786440 | tf_op jit(solution)/shard_map/reduce_x/ppermute | solution.py:135
  161.3 18.8 %all-to-all-start.3 = ((f32[8,8,1024]{2,1,0:T(8,128)}), f32[8,8,1024]{2,1,0:T(8,128)S(1)}, u32[]{:S(2)}, u32[]{:S(2)}) async-start(f32[8,8,1024]{2,1,0:T(8,128)} %fusion.10), calls=%async_computation.3 | async-start | bytes 524288 | tf_op jit(solution)/shard_map/reduce_z/all_to_all | solution.py:138
  (1 other events, 3.4 us)

commit v7 on v6

--- a/solution.py
+++ b/solution.py
@@ -125,59 +125,65 @@
         return jnp.sum(lax.all_to_all(outgoing, ("x", "z"), 0, 0, tiled=True), axis=0)
 
 
+def over_axis(outgoing, axis):
+    size = lax.axis_size(axis)
+    place = lax.axis_index(axis)
+    total = lax.dynamic_index_in_dim(outgoing, place, 0, keepdims=False)
+    for shift in range(1, size):
+        away = lax.dynamic_index_in_dim(outgoing, (place + shift) % size, 0, keepdims=False)
+        total += lax.ppermute(away, axis, ring(size, shift))
+    return total
+
+
 def over_x_then_z(outgoing, earlier):
-    x = lax.axis_index("x")
     outgoing = outgoing.reshape(NX, NZ, *outgoing.shape[1:])
     with jax.named_scope("reduce_x"):
-        total = lax.dynamic_index_in_dim(outgoing, x, 0, keepdims=False)
-        for shift in (1, 3, 2):
-            away = lax.dynamic_index_in_dim(outgoing, (x + shift) % NX, 0, keepdims=False)
-            total += lax.ppermute(away, "x", ring(NX, shift))
+        outgoing = over_axis(outgoing, "x")
+    (outgoing,) = after_that(earlier, outgoing)
     with jax.named_scope("reduce_z"):
-        (total,) = after_that(earlier, total)
-        return jnp.sum(lax.all_to_all(total, "z", 0, 0, tiled=True), axis=0)
+        return over_axis(outgoing, "z")
 
 
 def per_device(amplitudes, integrals, slot_block, rest, occ_energy, vir_energy):
     nblocks = amplitudes.shape[1]
     cap = integrals.shape[0]
-    n = integrals.shape[2]
     picker = (slot_block[:, None] == jnp.arange(nblocks, dtype=jnp.int32)[None, :]).astype(
         jnp.bfloat16
     )
     picker = picker.reshape(-1, cap, nblocks)
-    step = amplitudes.shape[0] // 2
-
-    outgoing = gather_rows(amplitudes[:step], picker)
-    outgoing_later = gather_rows(amplitudes[step:], picker)
-    own = route(outgoing)
-    (outgoing_later,) = after_that(own, outgoing_later)
+    cuts = [(0, 2), (2, 3), (3, 4)]
+    outgoing = [gather_rows(amplitudes[low:high], picker) for low, high in cuts]
+
+    own = route(outgoing[0])
+    (outgoing[1],) = after_that(own, outgoing[1])
     after = [backward(row) for row in own]
     before = [forward(row) for row in own]
-    later = route(outgoing_later)
-    (later,) = after_that((after, before), later)
     across = [forward(before[0]), backward(after[1])]
-    before_later = [forward(later[0])]
-    after_later = [backward(later[1])]
-    kept, away = product([*own, *after, *before, *later], integrals)
-    (away,) = after_that((across, before_later, after_later), away)
+
+    own_later = route(outgoing[1])
+    (outgoing[2],) = after_that(own_later, outgoing[2])
+    (own_later,) = after_that((after, before), own_later)
+    after_later = [backward(row) for row in own_later]
+    before_later = [forward(row) for row in own_later]
+    across_later = [forward(before_later[0])]
+    kept, away = product([*own, *after, *across, *before], integrals)
+
+    last = route(outgoing[2])
+    (away,) = after_that(last, away)
+    (last,) = after_that((after_later, before_later), last)
+    own_later += last
+    after_later += [backward(row) for row in last]
+    before_later += [forward(row) for row in last]
+    across_later += [backward(after_later[1])]
+
     early = over_core((kept, away))
-    (across,) = after_that(early, across)
+    (across_later,) = after_that(early, across_later)
     early = over_xz(early)
-
-    across_later = [forward(before_later[0]), backward(after_later[0])]
-    before_later = [before_later[0], forward(later[1])]
-    after_later = [backward(later[0]), after_later[0]]
-    late = product([*across, *after_later, *before_later, *across_later], integrals)
+    late = product([*own_later, *after_later, *across_later, *before_later], integrals)
     late = over_x_then_z(over_core(late), early)
 
-    early = early.reshape(4, step, n)
-    late = late.reshape(4, step, n)
-    own, after, before, later = (early[i] for i in range(4))
-    across, after_later, before_later, across_later = (late[i] for i in range(4))
-    relative = jnp.concatenate(
-        [own, later, after, after_later, across, across_later, before, before_later]
-    ).reshape(NY, 2 * step, n)
+    n = integrals.shape[2]
+    relative = jnp.concatenate([early.reshape(NY, 2, n), late.reshape(NY, 2, n)], axis=1)
     k = lax.axis_index("y")
     doubled = jnp.concatenate([relative, relative], axis=0)
     ladder = lax.dynamic_slice_in_dim(doubled, (NY - k) % NY, NY, 0).reshape(rest.shape)

time: 182 us -> 189 us (1.038)
  starting transfers between devices: 56.8 us -> 71.6 us
  waiting for transfers between devices: 91.5 us -> 80 us
  matrix products: 3.96 us -> 6.74 us
    ppermute x6, waiting for transfers between devices: 28.4 us -> 11.8 us  [forward(): return lax.ppermute(row, 'y', ring(NY, 1))]
    ppermute x3 -> x10, starting transfers between devices: 4.18 us -> 20.5 us  [over_axis(): total += lax.ppermute(away, axis, ring(size, shift))]
    ppermute x6, waiting for transfers between devices: 0.07 us -> 12.4 us  [backward(): return lax.ppermute(row, 'y', ring(NY, -1))]
    all_to_all x1 -> x0, waiting for transfers between devices: 12 us -> none  [over_x_then_z(): return jnp.sum(lax.all_to_all(total, 'z', 0, 0, tiled=True), axis=0)]
    all_to_all x1 -> x0, starting transfers between devices: 6.78 us -> none  [over_x_then_z(): return jnp.sum(lax.all_to_all(total, 'z', 0, 0, tiled=True), axis=0)]
    all_to_all x2 -> x3, starting transfers between devices: 17.7 us -> 23.6 us  [route(): routed = lax.all_to_all(outgoing, ('z', 'x', 'core'), 0, 0, tiled=True)]
    ppermute x3 -> x10, waiting for transfers between devices: 11.5 us -> 16.2 us  [over_axis(): total += lax.ppermute(away, axis, ring(size, shift))]
    dot_general x2 -> x3, matrix products: 3.96 us -> 6.74 us  [gather_rows(): jnp.einsum('tsg,rgb->trsb', picker, amp_rows, preferred_element_type=jnp....]
  transfers between devices with their start and end apart: 21 -> 28, of which waited for: 11 -> 12; matrix products, arithmetic and copies ran while one was open for 4% -> 5% of each run, Pallas kernels for 11% -> 10%
where the time goes in v7:
time: 189 us; the launch traced here: 187 us
  waiting for transfers between devices  80 us (42%)
  starting transfers between devices  71.6 us (38%)
  Pallas kernels  19.6 us (10%)
  matrix products  6.74 us (4%)
  other arithmetic  5.71 us (3%)
  local copies, waits for them, and re-layouts  3.39 us (2%)
    all_to_all x3, waiting for transfers between devices, route(): routed = lax.all_to_all(outgoing, ('z', 'x', 'core'), 0, 0, tiled=True)  36.8 us
    all_to_all x3, starting transfers between devices, route(): routed = lax.all_to_all(outgoing, ('z', 'x', 'core'), 0, 0, tiled=True)  23.6 us
    ppermute x10, starting transfers between devices, over_axis(): total += lax.ppermute(away, axis, ring(size, shift))  20.5 us
    pallas_call x2, Pallas kernels, product(): pl.pallas_call(body, grid_spec=pltpu.PrefetchScalarGridSpec(num_scalar_pr...  19.6 us
    ppermute x10, waiting for transfers between devices, over_axis(): total += lax.ppermute(away, axis, ring(size, shift))  16.2 us
    ppermute x6, starting transfers between devices, backward(): return lax.ppermute(row, 'y', ring(NY, -1))  14 us
    ppermute x6, waiting for transfers between devices, backward(): return lax.ppermute(row, 'y', ring(NY, -1))  12.4 us
    ppermute x6, waiting for transfers between devices, forward(): return lax.ppermute(row, 'y', ring(NY, 1))  11.8 us
  transfers between devices with their start and end apart: 28, of which 12 were waited for; matrix products, arithmetic and copies ran while one was open for 5% of the time, Pallas kernels for 10%

profile of v7, /device:TPU:2, one launch (start us, length us, event | category | flops | bytes accessed | tf_op | source)
XLA Modules:
  0.0 187.5 jit_solution(8504383496166897430)
XLA Ops:
  0.8 2.5 %fusion = bf16[64,2,8,512]{3,2,1,0:T(8,128)(2,1)} fusion(bf16[4,256,512]{2,1,0:T(8,128)(2,1)} %param.6, s32[64,8]{1,0:T(8,128)S(1)} %eq.53), kind=kOutput, calls=%fused_computation.1 | convolution fusion | flops 269090816 | bytes 1574912 | tf_op jit(solution)/shard_map/pick/tsg,rgb->trsb/dot_general | solution.py:21
  3.3 12.0 %all-to-all-start = ((bf16[64,2,8,512]{3,2,1,0:T(8,128)(2,1)}), bf16[64,2,8,512]{3,2,1,0:T(8,128)(2,1)S(1)}, u32[]{:S(2)}, u32[]{:S(2)}) async-start(bf16[64,2,8,512]{3,2,1,0:T(8,128)(2,1)} %fusion), calls=%async_computation | async-start | bytes 2097152 | tf_op jit(solution)/shard_map/route/all_to_all | solution.py:29
  15.3 2.1 %fusion.1 = bf16[64,1,8,512]{3,2,0,1:T(8,128)(2,1)} fusion(bf16[4,256,512]{2,1,0:T(8,128)(2,1)} %param.6, s32[64,8]{1,0:T(8,128)S(1)} %eq.53), kind=kOutput, calls=%fused_computation.4 | convolution fusion | flops 134610944 | bytes 788480 | tf_op jit(solution)/shard_map/pick/tsg,rgb->trsb/dot_general | solution.py:21
  17.4 26.7 %all-to-all-done = bf16[64,2,8,512]{3,2,1,0:T(8,128)(2,1)S(1)} async-done(((bf16[64,2,8,512]{3,2,1,0:T(8,128)(2,1)}), bf16[64,2,8,512]{3,2,1,0:T(8,128)(2,1)S(1)}, u32[]{:S(2)}, u32[]{:S(2)}) %all-to-all-start) | async-done | bytes 1048608 | tf_op jit(solution)/shard_map/route/all_to_all | solution.py:29
  44.9 5.7 %all-to-all-start.1 = ((bf16[64,1,8,512]{3,2,1,0:T(8,128)(2,1)}), bf16[64,1,8,512]{3,2,1,0:T(8,128)(2,1)S(1)}, u32[]{:S(2)}, u32[]{:S(2)}) async-start(bf16[64,1,8,512]{3,2,1,0:T(8,128)(2,1)} %bitcast.18), calls=%async_computation.1 | async-start | bytes 1048576 | tf_op jit(solution)/shard_map/route/all_to_all | solution.py:29
  52.2 1.7 collective-permute-start.1
  53.9 1.8 collective-permute-start
  55.9 2.1 %fusion.2 = bf16[64,1,8,512]{3,2,0,1:T(8,128)(2,1)} fusion(bf16[4,256,512]{2,1,0:T(8,128)(2,1)} %param.6, s32[64,8]{1,0:T(8,128)S(1)} %eq.53), kind=kOutput, calls=%fused_computation.5 | convolution fusion | flops 134610944 | bytes 788480 | tf_op jit(solution)/shard_map/pick/tsg,rgb->trsb/dot_general | solution.py:21
  58.0 10.1 %all-to-all-done.1 = bf16[64,1,8,512]{3,2,1,0:T(8,128)(2,1)S(1)} async-done(((bf16[64,1,8,512]{3,2,1,0:T(8,128)(2,1)}), bf16[64,1,8,512]{3,2,1,0:T(8,128)(2,1)S(1)}, u32[]{:S(2)}, u32[]{:S(2)}) %all-to-all-start.1) | async-done | bytes 524320 | tf_op jit(solution)/shard_map/route/all_to_all | solution.py:29
  68.4 5.9 %all-to-all-start.2 = ((bf16[64,1,8,512]{3,2,1,0:T(8,128)(2,1)}), bf16[64,1,8,512]{3,2,1,0:T(8,128)(2,1)S(1)}, u32[]{:S(2)}, u32[]{:S(2)}) async-start(bf16[64,1,8,512]{3,2,1,0:T(8,128)(2,1)} %bitcast.27), calls=%async_computation.2 | async-start | bytes 1048576 | tf_op jit(solution)/shard_map/route/all_to_all | solution.py:29
  76.0 1.7 collective-permute-start.4
  78.5 2.5 %collective-permute-start.7 = (bf16[1,8,64,512]{3,2,1,0:T(8,128)(2,1)S(1)}, bf16[1,8,64,512]{3,2,1,0:T(8,128)(2,1)S(1)}, u32[]{:S(2)}, u32[]{:S(2)}) collective-permute-start(bf16[1,8,64,512]{3,2,1,0:T(8,128)(2,1)S(1)} %bitcast.102), channel_id=1, source_target_pairs={{0,3},{1,0},{2,1},{3,2},{4,7},{5,4},{6,5},{7,6},{8,11},{9,8},{10,9... | collective-permute-start | bytes 1572872 | tf_op jit(solution)/shard_map/ppermute | solution.py:43
  81.0 9.6 %collective-permute-done.3.refs_4_ = bf16[1,8,64,512]{3,2,1,0:T(8,128)(2,1)S(1)} collective-permute-done((bf16[1,8,64,512]{3,2,1,0:T(8,128)(2,1)}, bf16[1,8,64,512]{3,2,1,0:T(8,128)(2,1)S(1)}, u32[]{:S(2)}, u32[]{:S(2)}) %collective-permute-start.3) | collective-permute-done | bytes 524320 | tf_op jit(solution)/shard_map/ppermute | solution.py:39
  91.4 9.8 %product.2 = (f32[32,8,1024]{2,1,0:T(8,128)}, f32[32,8,1024]{2,1,0:T(8,128)}) custom-call(s32[1]{0:T(128)} %bitcast.place_ref, bf16[1,8,64,512]{3,2,1,0:T(8,128)(2,1)} %bitcast.107, bf16[1,8,64,512]{3,2,1,0:T(8,128)(2,1)} %bitcast.110, bf16[1,8,64,512]{3,2,1,0:T(8,128)(2,1)} %copy-done.8, bf16[1,8,64,512]{3,2,1,0:T(8,128)(2,1)} %collective-permute-done.1.refs_3_, ...), custom_call_target="tpu_custom_call" | custom-call | flops 4294967296 | bytes 14680064 | tf_op jit(solution)/shard_map/product/pallas_call | solution.py:96
  101.7 2.7 %collective-permute-start.9 = (bf16[1,8,64,512]{3,2,1,0:T(8,128)(2,1)S(1)}, bf16[1,8,64,512]{3,2,1,0:T(8,128)(2,1)S(1)}, u32[]{:S(2)}, u32[]{:S(2)}) collective-permute-start(bf16[1,8,64,512]{3,2,1,0:T(8,128)(2,1)S(1)} %bitcast.111), channel_id=1, source_target_pairs={{0,3},{1,0},{2,1},{3,2},{4,7},{5,4},{6,5},{7,6},{8,11},{9,8},{10,9... | collective-permute-start | bytes 1572872 | tf_op jit(solution)/shard_map/ppermute | solution.py:43
  104.3 11.8 %collective-permute-done.9.refs_3_ = bf16[1,8,64,512]{3,2,1,0:T(8,128)(2,1)S(1)} collective-permute-done((bf16[1,8,64,512]{3,2,1,0:T(8,128)(2,1)S(1)}, bf16[1,8,64,512]{3,2,1,0:T(8,128)(2,1)S(1)}, u32[]{:S(2)}, u32[]{:S(2)}) %collective-permute-start.9) | collective-permute-done | bytes 524320 | tf_op jit(solution)/shard_map/ppermute | solution.py:43
  116.2 3.7 %collective-permute-start.11 = (bf16[1,8,64,512]{3,2,1,0:T(8,128)(2,1)S(1)}, bf16[1,8,64,512]{3,2,1,0:T(8,128)(2,1)}, u32[]{:S(2)}, u32[]{:S(2)}) collective-permute-start(bf16[1,8,64,512]{3,2,1,0:T(8,128)(2,1)S(1)} %collective-permute-done.9.refs_3_), channel_id=1, source_target_pairs={{0,3},{1,0},{2,1},{3,2},{4,7},{5,4},{6,5},{7,6},{8,11},{9,8},{10,9... | collective-permute-start | bytes 1572872 | tf_op jit(solution)/shard_map/ppermute | solution.py:43
  119.9 2.4 %add.144 = f32[32,8,1024]{2,1,0:T(8,128)} add(f32[32,8,1024]{2,1,0:T(8,128)} %get-tuple-element.21, f32[32,8,1024]{2,1,0:T(8,128)S(1)} %collective-permute-done.6) | non-fusion elementwise | flops 262144 | bytes 3145728 | tf_op jit(solution)/shard_map/reduce_core/add | solution.py:120
  122.2 9.9 %all-to-all-start.3 = ((f32[32,8,1024]{2,1,0:T(8,128)}), f32[32,8,1024]{2,1,0:T(8,128)S(1)}, u32[]{:S(2)}, u32[]{:S(2)}) async-start(f32[32,8,1024]{2,1,0:T(8,128)} %add.144), calls=%async_computation.3 | async-start | bytes 2097152 | tf_op jit(solution)/shard_map/reduce_xz/all_to_all | solution.py:125
  132.2 2.2 %collective-permute-done.12.refs_7_ = bf16[1,8,64,512]{3,2,1,0:T(8,128)(2,1)} collective-permute-done((bf16[1,8,64,512]{3,2,1,0:T(8,128)(2,1)S(1)}, bf16[1,8,64,512]{3,2,1,0:T(8,128)(2,1)}, u32[]{:S(2)}, u32[]{:S(2)}) %collective-permute-start.12) | collective-permute-done | bytes 524320 | tf_op jit(solution)/shard_map/ppermute | solution.py:39
  134.4 9.8 %product.3 = (f32[32,8,1024]{2,1,0:T(8,128)}, f32[32,8,1024]{2,1,0:T(8,128)}) custom-call(s32[1]{0:T(128)} %bitcast.place_ref, bf16[1,8,64,512]{3,2,1,0:T(8,128)(2,1)} %bitcast.104, bf16[1,8,64,512]{3,2,1,0:T(8,128)(2,1)} %bitcast.113, bf16[1,8,64,512]{3,2,1,0:T(8,128)(2,1)} %copy-done.7, bf16[1,8,64,512]{3,2,1,0:T(8,128)(2,1)} %copy-done.9, ...), custom_call_target="tpu_custom_call" | custom-call | flops 4294967296 | bytes 14680064 | tf_op jit(solution)/shard_map/product/pallas_call | solution.py:96
  144.3 2.8 %collective-permute-done.13 = f32[32,8,1024]{2,1,0:T(8,128)S(1)} collective-permute-done((f32[32,8,1024]{2,1,0:T(8,128)}, f32[32,8,1024]{2,1,0:T(8,128)S(1)}, u32[]{:S(2)}, u32[]{:S(2)}) %collective-permute-start.13) | collective-permute-done | bytes 1048608 | tf_op jit(solution)/shard_map/reduce_core/ppermute | solution.py:120
  149.2 2.5 %collective-permute-start.15 = (f32[8,8,1024]{2,1,0:T(8,128)S(1)}, f32[8,8,1024]{2,1,0:T(8,128)S(1)}, u32[]{:S(2)}, u32[]{:S(2)}) collective-permute-start(f32[8,8,1024]{2,1,0:T(8,128)S(1)} %get-tuple-element.35), channel_id=1, source_target_pairs={{0,16},{8,24},{16,0},{24,8},{1,17},{9,25},{17,1},{25,9},{2,18},{10... | collective-permute-start | bytes 786440 | tf_op jit(solution)/shard_map/reduce_x/ppermute | solution.py:134
  151.6 1.8 collective-permute-start.14
  153.4 7.0 %collective-permute-done.16 = f32[8,8,1024]{2,1,0:T(8,128)S(1)} collective-permute-done((f32[8,8,1024]{2,1,0:T(8,128)S(1)}, f32[8,8,1024]{2,1,0:T(8,128)S(1)}, u32[]{:S(2)}, u32[]{:S(2)}) %collective-permute-start.16) | collective-permute-done | bytes 262176 | tf_op jit(solution)/shard_map/reduce_x/ppermute | solution.py:134
  160.4 5.8 %collective-permute-done.15 = f32[8,8,1024]{2,1,0:T(8,128)S(1)} collective-permute-done((f32[8,8,1024]{2,1,0:T(8,128)S(1)}, f32[8,8,1024]{2,1,0:T(8,128)S(1)}, u32[]{:S(2)}, u32[]{:S(2)}) %collective-permute-start.15) | collective-permute-done | bytes 262176 | tf_op jit(solution)/shard_map/reduce_x/ppermute | solution.py:134
  167.4 2.2 %collective-permute-start.23 = (f32[8,1024]{1,0:T(8,128)S(1)}, f32[8,1024]{1,0:T(8,128)S(1)}, u32[]{:S(2)}, u32[]{:S(2)}) collective-permute-start(f32[8,1024]{1,0:T(8,128)S(1)} %get-tuple-element.39), channel_id=1, source_target_pairs={{0,224},{32,0},{64,32},{96,64},{128,96},{160,128},{192,160},{224,1... | collective-permute-start | bytes 98312 | tf_op jit(solution)/shard_map/reduce_z/ppermute | solution.py:134
  169.6 1.9 collective-permute-start.22
  171.5 2.3 %collective-permute-start.21 = (f32[8,1024]{1,0:T(8,128)S(1)}, f32[8,1024]{1,0:T(8,128)S(1)}, u32[]{:S(2)}, u32[]{:S(2)}) collective-permute-start(f32[8,1024]{1,0:T(8,128)S(1)} %get-tuple-element.41), channel_id=1, source_target_pairs={{0,160},{32,192},{64,224},{96,0},{128,32},{160,64},{192,96},{224,1... | collective-permute-start | bytes 98312 | tf_op jit(solution)/shard_map/reduce_z/ppermute | solution.py:134
  173.7 3.8 %collective-permute-start.20 = (f32[8,1024]{1,0:T(8,128)S(1)}, f32[8,1024]{1,0:T(8,128)S(1)}, u32[]{:S(2)}, u32[]{:S(2)}) collective-permute-start(f32[8,1024]{1,0:T(8,128)S(1)} %get-tuple-element.42), channel_id=1, source_target_pairs={{0,128},{32,160},{64,192},{96,224},{128,0},{160,32},{192,64},{224,... | collective-permute-start | bytes 98312 | tf_op jit(solution)/shard_map/reduce_z/ppermute | solution.py:134
  177.9 3.5 %collective-permute-start.18 = (f32[8,1024]{1,0:T(8,128)S(1)}, f32[8,1024]{1,0:T(8,128)S(1)}, u32[]{:S(2)}, u32[]{:S(2)}) collective-permute-start(f32[8,1024]{1,0:T(8,128)S(1)} %get-tuple-element.44), channel_id=1, source_target_pairs={{0,64},{32,96},{64,128},{96,160},{128,192},{160,224},{192,0},{224,... | collective-permute-start | bytes 98312 | tf_op jit(solution)/shard_map/reduce_z/ppermute | solution.py:134
  181.4 1.7 collective-permute-start.17
  (71 shorter events, 15.2 us)
Async XLA Ops:
  3.3 40.8 %all-to-all-start = ((bf16[64,2,8,512]{3,2,1,0:T(8,128)(2,1)}), bf16[64,2,8,512]{3,2,1,0:T(8,128)(2,1)S(1)}, u32[]{:S(2)}, u32[]{:S(2)}) async-start(bf16[64,2,8,512]{3,2,1,0:T(8,128)(2,1)} %fusion), calls=%async_computation | async-start | bytes 2097152 | tf_op jit(solution)/shard_map/route/all_to_all | solution.py:29
  44.6 46.5 %copy-start.1 = (bf16[8,4,2,1,8,512]{5,0,1,2,4,3:T(8,128)(2,1)}, bf16[8,4,2,1,8,512]{5,0,1,2,4,3:T(8,128)(2,1)S(1)}, u32[]{:S(2)}) copy-start(bf16[8,4,2,1,8,512]{5,0,1,2,4,3:T(8,128)(2,1)S(1)} %copy.22) | copy-start | bytes 1572868
  44.9 23.2 %all-to-all-start.1 = ((bf16[64,1,8,512]{3,2,1,0:T(8,128)(2,1)}), bf16[64,1,8,512]{3,2,1,0:T(8,128)(2,1)S(1)}, u32[]{:S(2)}, u32[]{:S(2)}) async-start(bf16[64,1,8,512]{3,2,1,0:T(8,128)(2,1)} %bitcast.18), calls=%async_computation.1 | async-start | bytes 1048576 | tf_op jit(solution)/shard_map/route/all_to_all | solution.py:29
  50.6 23.8 %collective-permute-start.2 = (bf16[1,8,64,512]{3,2,1,0:T(8,128)(2,1)S(1)}, bf16[1,8,64,512]{3,2,1,0:T(8,128)(2,1)}, u32[]{:S(2)}, u32[]{:S(2)}) collective-permute-start(bf16[1,8,64,512]{3,2,1,0:T(8,128)(2,1)S(1)} %bitcast.105), channel_id=1, source_target_pairs={{0,1},{1,2},{2,3},{3,0},{4,5},{5,6},{6,7},{7,4},{8,9},{9,10},{10,1... | collective-permute-start | bytes 1572872 | tf_op jit(solution)/shard_map/ppermute | solution.py:39
  52.2 23.8 %collective-permute-start.1 = (bf16[1,8,64,512]{3,2,1,0:T(8,128)(2,1)S(1)}, bf16[1,8,64,512]{3,2,1,0:T(8,128)(2,1)}, u32[]{:S(2)}, u32[]{:S(2)}) collective-permute-start(bf16[1,8,64,512]{3,2,1,0:T(8,128)(2,1)S(1)} %bitcast.108), channel_id=1, source_target_pairs={{0,3},{1,0},{2,1},{3,2},{4,7},{5,4},{6,5},{7,6},{8,11},{9,8},{10,9... | collective-permute-start | bytes 1572872 | tf_op jit(solution)/shard_map/ppermute | solution.py:43
  53.9 23.8 %collective-permute-start = (bf16[1,8,64,512]{3,2,1,0:T(8,128)(2,1)S(1)}, bf16[1,8,64,512]{3,2,1,0:T(8,128)(2,1)S(1)}, u32[]{:S(2)}, u32[]{:S(2)}) collective-permute-start(bf16[1,8,64,512]{3,2,1,0:T(8,128)(2,1)S(1)} %bitcast.106), channel_id=1, source_target_pairs={{0,3},{1,0},{2,1},{3,2},{4,7},{5,4},{6,5},{7,6},{8,11},{9,8},{10,9... | collective-permute-start | bytes 1572872 | tf_op jit(solution)/shard_map/ppermute | solution.py:43
  55.7 22.8 %collective-permute-start.5 = (bf16[1,8,64,512]{3,2,1,0:T(8,128)(2,1)S(1)}, bf16[1,8,64,512]{3,2,1,0:T(8,128)(2,1)}, u32[]{:S(2)}, u32[]{:S(2)}) collective-permute-start(bf16[1,8,64,512]{3,2,1,0:T(8,128)(2,1)S(1)} %bitcast.109), channel_id=1, source_target_pairs={{0,1},{1,2},{2,3},{3,0},{4,5},{5,6},{6,7},{7,4},{8,9},{9,10},{10,1... | collective-permute-start | bytes 1572872 | tf_op jit(solution)/shard_map/ppermute | solution.py:39
  68.4 32.8 %all-to-all-start.2 = ((bf16[64,1,8,512]{3,2,1,0:T(8,128)(2,1)}), bf16[64,1,8,512]{3,2,1,0:T(8,128)(2,1)S(1)}, u32[]{:S(2)}, u32[]{:S(2)}) async-start(bf16[64,1,8,512]{3,2,1,0:T(8,128)(2,1)} %bitcast.27), calls=%async_computation.2 | async-start | bytes 1048576 | tf_op jit(solution)/shard_map/route/all_to_all | solution.py:29
  74.3 16.3 %collective-permute-start.3 = (bf16[1,8,64,512]{3,2,1,0:T(8,128)(2,1)}, bf16[1,8,64,512]{3,2,1,0:T(8,128)(2,1)S(1)}, u32[]{:S(2)}, u32[]{:S(2)}) collective-permute-start(bf16[1,8,64,512]{3,2,1,0:T(8,128)(2,1)} %collective-permute-done.2.refs_6_), channel_id=1, source_target_pairs={{0,1},{1,2},{2,3},{3,0},{4,5},{5,6},{6,7},{7,4},{8,9},{9,10},{10,1... | collective-permute-start | bytes 1572872 | tf_op jit(solution)/shard_map/ppermute | solution.py:39
  76.0 15.1 %collective-permute-start.4 = (bf16[1,8,64,512]{3,2,1,0:T(8,128)(2,1)}, bf16[1,8,64,512]{3,2,1,0:T(8,128)(2,1)}, u32[]{:S(2)}, u32[]{:S(2)}) collective-permute-start(bf16[1,8,64,512]{3,2,1,0:T(8,128)(2,1)} %collective-permute-done.1.refs_3_), channel_id=1, source_target_pairs={{0,3},{1,0},{2,1},{3,2},{4,7},{5,4},{6,5},{7,6},{8,11},{9,8},{10,9... | collective-permute-start | bytes 1572872 | tf_op jit(solution)/shard_map/ppermute | solution.py:43
  78.5 23.2 %collective-permute-start.7 = (bf16[1,8,64,512]{3,2,1,0:T(8,128)(2,1)S(1)}, bf16[1,8,64,512]{3,2,1,0:T(8,128)(2,1)S(1)}, u32[]{:S(2)}, u32[]{:S(2)}) collective-permute-start(bf16[1,8,64,512]{3,2,1,0:T(8,128)(2,1)S(1)} %bitcast.102), channel_id=1, source_target_pairs={{0,3},{1,0},{2,1},{3,2},{4,7},{5,4},{6,5},{7,6},{8,11},{9,8},{10,9... | collective-permute-start | bytes 1572872 | tf_op jit(solution)/shard_map/ppermute | solution.py:43
  81.0 20.7 %collective-permute-start.8 = (bf16[1,8,64,512]{3,2,1,0:T(8,128)(2,1)S(1)}, bf16[1,8,64,512]{3,2,1,0:T(8,128)(2,1)}, u32[]{:S(2)}, u32[]{:S(2)}) collective-permute-start(bf16[1,8,64,512]{3,2,1,0:T(8,128)(2,1)S(1)} %bitcast.103), channel_id=1, source_target_pairs={{0,1},{1,2},{2,3},{3,0},{4,5},{5,6},{6,7},{7,4},{8,9},{9,10},{10,1... | collective-permute-start | bytes 1572872 | tf_op jit(solution)/shard_map/ppermute | solution.py:39
  101.6 18.3 %collective-permute-start.6 = (f32[32,8,1024]{2,1,0:T(8,128)}, f32[32,8,1024]{2,1,0:T(8,128)S(1)}, u32[]{:S(2)}, u32[]{:S(2)}) collective-permute-start(f32[32,8,1024]{2,1,0:T(8,128)} %get-tuple-element.25), channel_id=1, source_target_pairs={{0,4},{4,0},{1,5},{5,1},{2,6},{6,2},{3,7},{7,3},{8,12},{12,8},{9,1... | collective-permute-start | bytes 3145736 | tf_op jit(solution)/shard_map/reduce_core/ppermute | solution.py:120
  101.7 14.5 %collective-permute-start.9 = (bf16[1,8,64,512]{3,2,1,0:T(8,128)(2,1)S(1)}, bf16[1,8,64,512]{3,2,1,0:T(8,128)(2,1)S(1)}, u32[]{:S(2)}, u32[]{:S(2)}) collective-permute-start(bf16[1,8,64,512]{3,2,1,0:T(8,128)(2,1)S(1)} %bitcast.111), channel_id=1, source_target_pairs={{0,3},{1,0},{2,1},{3,2},{4,7},{5,4},{6,5},{7,6},{8,11},{9,8},{10,9... | collective-permute-start | bytes 1572872 | tf_op jit(solution)/shard_map/ppermute | solution.py:43
  104.3 27.8 %collective-permute-start.10 = (bf16[1,8,64,512]{3,2,1,0:T(8,128)(2,1)}, bf16[1,8,64,512]{3,2,1,0:T(8,128)(2,1)S(1)}, u32[]{:S(2)}, u32[]{:S(2)}) collective-permute-start(bf16[1,8,64,512]{3,2,1,0:T(8,128)(2,1)} %collective-permute-done.8.refs_6_), channel_id=1, source_target_pairs={{0,1},{1,2},{2,3},{3,0},{4,5},{5,6},{6,7},{7,4},{8,9},{9,10},{10,1... | collective-permute-start | bytes 1572872 | tf_op jit(solution)/shard_map/ppermute | solution.py:39
  116.2 16.0 %collective-permute-start.11 = (bf16[1,8,64,512]{3,2,1,0:T(8,128)(2,1)S(1)}, bf16[1,8,64,512]{3,2,1,0:T(8,128)(2,1)}, u32[]{:S(2)}, u32[]{:S(2)}) collective-permute-start(bf16[1,8,64,512]{3,2,1,0:T(8,128)(2,1)S(1)} %collective-permute-done.9.refs_3_), channel_id=1, source_target_pairs={{0,3},{1,0},{2,1},{3,2},{4,7},{5,4},{6,5},{7,6},{8,11},{9,8},{10,9... | collective-permute-start | bytes 1572872 | tf_op jit(solution)/shard_map/ppermute | solution.py:43
  119.9 14.6 %collective-permute-start.12 = (bf16[1,8,64,512]{3,2,1,0:T(8,128)(2,1)S(1)}, bf16[1,8,64,512]{3,2,1,0:T(8,128)(2,1)}, u32[]{:S(2)}, u32[]{:S(2)}) collective-permute-start(bf16[1,8,64,512]{3,2,1,0:T(8,128)(2,1)S(1)} %bitcast.112), channel_id=1, source_target_pairs={{0,1},{1,2},{2,3},{3,0},{4,5},{5,6},{6,7},{7,4},{8,9},{9,10},{10,1... | collective-permute-start | bytes 1572872 | tf_op jit(solution)/shard_map/ppermute | solution.py:39
  122.2 45.0 %all-to-all-start.3 = ((f32[32,8,1024]{2,1,0:T(8,128)}), f32[32,8,1024]{2,1,0:T(8,128)S(1)}, u32[]{:S(2)}, u32[]{:S(2)}) async-start(f32[32,8,1024]{2,1,0:T(8,128)} %add.144), calls=%async_computation.3 | async-start | bytes 2097152 | tf_op jit(solution)/shard_map/reduce_xz/all_to_all | solution.py:125
  132.2 54.6 %copy-start.4 = (bf16[16,1024]{1,0:T(8,128)(2,1)S(1)}, bf16[16,1024]{1,0:T(8,128)(2,1)}, u32[]{:S(2)}) copy-start(bf16[16,1024]{1,0:T(8,128)(2,1)} %param.9) | copy-start | bytes 98308
  132.2 54.6 %copy-start.5 = (f32[1024]{0:T(1024)S(1)}, f32[1024]{0:T(1024)}, u32[]{:S(2)}) copy-start(f32[1024]{0:T(1024)} %param.11) | copy-start | bytes 12292
  132.2 54.6 %copy-start.6 = (f32[16]{0:T(128)S(1)}, f32[16]{0:T(128)}, u32[]{:S(2)}) copy-start(f32[16]{0:T(128)} %param.10) | copy-start | bytes 196
  144.2 2.9 %collective-permute-start.13 = (f32[32,8,1024]{2,1,0:T(8,128)}, f32[32,8,1024]{2,1,0:T(8,128)S(1)}, u32[]{:S(2)}, u32[]{:S(2)}) collective-permute-start(f32[32,8,1024]{2,1,0:T(8,128)} %get-tuple-element.31), channel_id=1, source_target_pairs={{0,4},{4,0},{1,5},{5,1},{2,6},{6,2},{3,7},{7,3},{8,12},{12,8},{9,1... | collective-permute-start | bytes 3145736 | tf_op jit(solution)/shard_map/reduce_core/ppermute | solution.py:120
  148.6 11.8 %collective-permute-start.16 = (f32[8,8,1024]{2,1,0:T(8,128)S(1)}, f32[8,8,1024]{2,1,0:T(8,128)S(1)}, u32[]{:S(2)}, u32[]{:S(2)}) collective-permute-start(f32[8,8,1024]{2,1,0:T(8,128)S(1)} %get-tuple-element.34), channel_id=1, source_target_pairs={{0,24},{8,0},{16,8},{24,16},{1,25},{9,1},{17,9},{25,17},{2,26},{10... | collective-permute-start | bytes 786440 | tf_op jit(solution)/shard_map/reduce_x/ppermute | solution.py:134
  149.2 17.0 %collective-permute-start.15 = (f32[8,8,1024]{2,1,0:T(8,128)S(1)}, f32[8,8,1024]{2,1,0:T(8,128)S(1)}, u32[]{:S(2)}, u32[]{:S(2)}) collective-permute-start(f32[8,8,1024]{2,1,0:T(8,128)S(1)} %get-tuple-element.35), channel_id=1, source_target_pairs={{0,16},{8,24},{16,0},{24,8},{1,17},{9,25},{17,1},{25,9},{2,18},{10... | collective-permute-start | bytes 786440 | tf_op jit(solution)/shard_map/reduce_x/ppermute | solution.py:134
  151.6 14.6 %collective-permute-start.14 = (f32[8,8,1024]{2,1,0:T(8,128)S(1)}, f32[8,8,1024]{2,1,0:T(8,128)}, u32[]{:S(2)}, u32[]{:S(2)}) collective-permute-start(f32[8,8,1024]{2,1,0:T(8,128)S(1)} %get-tuple-element.33), channel_id=1, source_target_pairs={{0,8},{8,16},{16,24},{24,0},{1,9},{9,17},{17,25},{25,1},{2,10},{10... | collective-permute-start | bytes 786440 | tf_op jit(solution)/shard_map/reduce_x/ppermute | solution.py:134
  167.4 10.5 %collective-permute-start.23 = (f32[8,1024]{1,0:T(8,128)S(1)}, f32[8,1024]{1,0:T(8,128)S(1)}, u32[]{:S(2)}, u32[]{:S(2)}) collective-permute-start(f32[8,1024]{1,0:T(8,128)S(1)} %get-tuple-element.39), channel_id=1, source_target_pairs={{0,224},{32,0},{64,32},{96,64},{128,96},{160,128},{192,160},{224,1... | collective-permute-start | bytes 98312 | tf_op jit(solution)/shard_map/reduce_z/ppermute | solution.py:134
  169.6 11.8 %collective-permute-start.22 = (f32[8,1024]{1,0:T(8,128)S(1)}, f32[8,1024]{1,0:T(8,128)S(1)}, u32[]{:S(2)}, u32[]{:S(2)}) collective-permute-start(f32[8,1024]{1,0:T(8,128)S(1)} %get-tuple-element.40), channel_id=1, source_target_pairs={{0,192},{32,224},{64,0},{96,32},{128,64},{160,96},{192,128},{224,1... | collective-permute-start | bytes 98312 | tf_op jit(solution)/shard_map/reduce_z/ppermute | solution.py:134
  171.5 11.7 %collective-permute-start.21 = (f32[8,1024]{1,0:T(8,128)S(1)}, f32[8,1024]{1,0:T(8,128)S(1)}, u32[]{:S(2)}, u32[]{:S(2)}) collective-permute-start(f32[8,1024]{1,0:T(8,128)S(1)} %get-tuple-element.41), channel_id=1, source_target_pairs={{0,160},{32,192},{64,224},{96,0},{128,32},{160,64},{192,96},{224,1... | collective-permute-start | bytes 98312 | tf_op jit(solution)/shard_map/reduce_z/ppermute | solution.py:134
  173.7 9.5 %collective-permute-start.20 = (f32[8,1024]{1,0:T(8,128)S(1)}, f32[8,1024]{1,0:T(8,128)S(1)}, u32[]{:S(2)}, u32[]{:S(2)}) collective-permute-start(f32[8,1024]{1,0:T(8,128)S(1)} %get-tuple-element.42), channel_id=1, source_target_pairs={{0,128},{32,160},{64,192},{96,224},{128,0},{160,32},{192,64},{224,... | collective-permute-start | bytes 98312 | tf_op jit(solution)/shard_map/reduce_z/ppermute | solution.py:134
  177.5 7.0 %collective-permute-start.19 = (f32[8,1024]{1,0:T(8,128)S(1)}, f32[8,1024]{1,0:T(8,128)S(1)}, u32[]{:S(2)}, u32[]{:S(2)}) collective-permute-start(f32[8,1024]{1,0:T(8,128)S(1)} %get-tuple-element.43), channel_id=1, source_target_pairs={{0,96},{32,128},{64,160},{96,192},{128,224},{160,0},{192,32},{224,... | collective-permute-start | bytes 98312 | tf_op jit(solution)/shard_map/reduce_z/ppermute | solution.py:134
  177.9 7.3 %collective-permute-start.18 = (f32[8,1024]{1,0:T(8,128)S(1)}, f32[8,1024]{1,0:T(8,128)S(1)}, u32[]{:S(2)}, u32[]{:S(2)}) collective-permute-start(f32[8,1024]{1,0:T(8,128)S(1)} %get-tuple-element.44), channel_id=1, source_target_pairs={{0,64},{32,96},{64,128},{96,160},{128,192},{160,224},{192,0},{224,... | collective-permute-start | bytes 98312 | tf_op jit(solution)/shard_map/reduce_z/ppermute | solution.py:134
  181.4 5.1 %collective-permute-start.17 = (f32[8,1024]{1,0:T(8,128)S(1)}, f32[8,1024]{1,0:T(8,128)S(1)}, u32[]{:S(2)}, u32[]{:S(2)}) collective-permute-start(f32[8,1024]{1,0:T(8,128)S(1)} %get-tuple-element.38), channel_id=1, source_target_pairs={{0,32},{32,64},{64,96},{96,128},{128,160},{160,192},{192,224},{224... | collective-permute-start | bytes 98312 | tf_op jit(solution)/shard_map/reduce_z/ppermute | solution.py:134
  (8 other events, 166.8 us)

commit v8 on v6

--- a/solution.py
+++ b/solution.py
@@ -157,17 +157,15 @@
     later = route(outgoing_later)
     (later,) = after_that((after, before), later)
     across = [forward(before[0]), backward(after[1])]
-    before_later = [forward(later[0])]
-    after_later = [backward(later[1])]
+    before_later = [forward(row) for row in later]
+    after_later = [backward(row) for row in later]
     kept, away = product([*own, *after, *before, *later], integrals)
     (away,) = after_that((across, before_later, after_later), away)
     early = over_core((kept, away))
     (across,) = after_that(early, across)
     early = over_xz(early)
 
-    across_later = [forward(before_later[0]), backward(after_later[0])]
-    before_later = [before_later[0], forward(later[1])]
-    after_later = [backward(later[0]), after_later[0]]
+    across_later = [forward(before_later[0]), backward(after_later[1])]
     late = product([*across, *after_later, *before_later, *across_later], integrals)
     late = over_x_then_z(over_core(late), early)
 

time: 182 us -> 183 us (level)
    ppermute x3, waiting for transfers between devices: 11.5 us -> 14.6 us  [over_x_then_z(): total += lax.ppermute(away, 'x', ring(NX, shift))]
    ppermute x6, starting transfers between devices: 13.7 us -> 11.5 us  [backward(): return lax.ppermute(row, 'y', ring(NY, -1))]
    ppermute x6, waiting for transfers between devices: 28.4 us -> 26.4 us  [forward(): return lax.ppermute(row, 'y', ring(NY, 1))]
where the time goes in v8:
time: 183 us
  waiting for transfers between devices  92.7 us (51%)
  starting transfers between devices  55.6 us (30%)
  Pallas kernels  19.6 us (11%)
  other arithmetic  6.23 us (3%)
  local copies, waits for them, and re-layouts  4.16 us (2%)
  matrix products  3.96 us (2%)
    all_to_all x2, waiting for transfers between devices, route(): routed = lax.all_to_all(outgoing, ('z', 'x', 'core'), 0, 0, tiled=True)  36.7 us
    ppermute x6, waiting for transfers between devices, forward(): return lax.ppermute(row, 'y', ring(NY, 1))  26.4 us
    pallas_call x2, Pallas kernels, product(): pl.pallas_call(body, grid_spec=pltpu.PrefetchScalarGridSpec(num_scalar_pr...  19.6 us
    all_to_all x2, starting transfers between devices, route(): routed = lax.all_to_all(outgoing, ('z', 'x', 'core'), 0, 0, tiled=True)  17.7 us
    ppermute x3, waiting for transfers between devices, over_x_then_z(): total += lax.ppermute(away, 'x', ring(NX, shift))  14.6 us
    all_to_all x1, waiting for transfers between devices, over_x_then_z(): return jnp.sum(lax.all_to_all(total, 'z', 0, 0, tiled=True), axis=0)  12 us
    ppermute x6, starting transfers between devices, backward(): return lax.ppermute(row, 'y', ring(NY, -1))  11.5 us
    all_to_all x1, starting transfers between devices, over_xz(): lax.all_to_all(outgoing, ('x', 'z'), 0, 0, tiled=True)  9.91 us
  transfers between devices with their start and end apart: 21, of which 11 were waited for; matrix products, arithmetic and copies ran while one was open for 4% of the time, Pallas kernels for 11%

profile of v8, /device:TPU:2, one launch (start us, length us, event | category | flops | bytes accessed | tf_op | source)
XLA Modules:
  0.0 182.6 jit_solution(17088199325901004223)
XLA Ops:
  0.0 0.9 eq.21
  0.9 2.5 %fusion = bf16[64,2,8,512]{3,2,1,0:T(8,128)(2,1)} fusion(bf16[4,256,512]{2,1,0:T(8,128)(2,1)} %param.6, s32[64,8]{1,0:T(8,128)S(1)} %eq.21), kind=kOutput, calls=%fused_computation.2 | convolution fusion | flops 269090816 | bytes 1574912 | tf_op jit(solution)/shard_map/pick/tsg,rgb->trsb/dot_general | solution.py:21
  3.4 12.0 %all-to-all-start = ((bf16[64,2,8,512]{3,2,1,0:T(8,128)(2,1)}), bf16[64,2,8,512]{3,2,1,0:T(8,128)(2,1)S(1)}, u32[]{:S(2)}, u32[]{:S(2)}) async-start(bf16[64,2,8,512]{3,2,1,0:T(8,128)(2,1)} %fusion), calls=%async_computation | async-start | bytes 2097152 | tf_op jit(solution)/shard_map/route/all_to_all | solution.py:29
  15.4 1.5 fusion.1
  16.9 27.3 %all-to-all-done = bf16[64,2,8,512]{3,2,1,0:T(8,128)(2,1)S(1)} async-done(((bf16[64,2,8,512]{3,2,1,0:T(8,128)(2,1)}), bf16[64,2,8,512]{3,2,1,0:T(8,128)(2,1)S(1)}, u32[]{:S(2)}, u32[]{:S(2)}) %all-to-all-start) | async-done | bytes 1048608 | tf_op jit(solution)/shard_map/route/all_to_all | solution.py:29
  45.0 5.7 %all-to-all-start.1 = ((bf16[64,2,8,512]{3,2,1,0:T(8,128)(2,1)}), bf16[64,2,8,512]{3,2,1,0:T(8,128)(2,1)S(1)}, u32[]{:S(2)}, u32[]{:S(2)}) async-start(bf16[64,2,8,512]{3,2,1,0:T(8,128)(2,1)} %fusion.1), calls=%async_computation.1 | async-start | bytes 2097152 | tf_op jit(solution)/shard_map/route/all_to_all | solution.py:29
  50.6 1.7 collective-permute-start.2
  52.3 1.7 collective-permute-start.1
  53.9 1.8 collective-permute-start
  56.0 10.8 %collective-permute-done.2.refs_4_ = bf16[1,8,64,512]{3,2,1,0:T(8,128)(2,1)} collective-permute-done((bf16[1,8,64,512]{3,2,1,0:T(8,128)(2,1)S(1)}, bf16[1,8,64,512]{3,2,1,0:T(8,128)(2,1)}, u32[]{:S(2)}, u32[]{:S(2)}) %collective-permute-start.2) | collective-permute-done | bytes 524320 | tf_op jit(solution)/shard_map/ppermute | solution.py:39
  67.2 2.9 %collective-permute-start.5 = (bf16[1,8,64,512]{3,2,1,0:T(8,128)(2,1)}, bf16[1,8,64,512]{3,2,1,0:T(8,128)(2,1)S(1)}, u32[]{:S(2)}, u32[]{:S(2)}) collective-permute-start(bf16[1,8,64,512]{3,2,1,0:T(8,128)(2,1)} %collective-permute-done.1.refs_3_), channel_id=1, source_target_pairs={{0,3},{1,0},{2,1},{3,2},{4,7},{5,4},{6,5},{7,6},{8,11},{9,8},{10,9... | collective-permute-start | bytes 1572872 | tf_op jit(solution)/shard_map/ppermute | solution.py:43
  70.0 9.4 %all-to-all-done.1 = bf16[64,2,8,512]{3,2,1,0:T(8,128)(2,1)S(1)} async-done(((bf16[64,2,8,512]{3,2,1,0:T(8,128)(2,1)}), bf16[64,2,8,512]{3,2,1,0:T(8,128)(2,1)S(1)}, u32[]{:S(2)}, u32[]{:S(2)}) %all-to-all-start.1) | async-done | bytes 1048608 | tf_op jit(solution)/shard_map/route/all_to_all | solution.py:29
  80.2 1.7 collective-permute-start.6
  81.9 1.7 collective-permute-start.8
  83.9 5.2 %collective-permute-done.4.refs_0_ = bf16[1,8,64,512]{3,2,1,0:T(8,128)(2,1)S(1)} collective-permute-done((bf16[1,8,64,512]{3,2,1,0:T(8,128)(2,1)}, bf16[1,8,64,512]{3,2,1,0:T(8,128)(2,1)S(1)}, u32[]{:S(2)}, u32[]{:S(2)}) %collective-permute-start.4) | collective-permute-done | bytes 524320 | tf_op jit(solution)/shard_map/ppermute | solution.py:39
  89.1 1.8 collective-permute-start.9
  91.0 9.8 %product.2 = (f32[32,8,1024]{2,1,0:T(8,128)}, f32[32,8,1024]{2,1,0:T(8,128)}) custom-call(s32[1]{0:T(128)} %bitcast.place_ref, bf16[1,8,64,512]{3,2,1,0:T(8,128)(2,1)} %bitcast.58, bf16[1,8,64,512]{3,2,1,0:T(8,128)(2,1)} %bitcast.61, bf16[1,8,64,512]{3,2,1,0:T(8,128)(2,1)} %collective-permute-done.refs_2_, ...), custom_call_target="tpu_custom_call" | custom-call | flops 4294967296 | bytes 14680064 | tf_op jit(solution)/shard_map/product/pallas_call | solution.py:96
  100.8 10.1 %collective-permute-done.7.refs_5_ = bf16[1,8,64,512]{3,2,1,0:T(8,128)(2,1)S(1)} collective-permute-done((bf16[1,8,64,512]{3,2,1,0:T(8,128)(2,1)S(1)}, bf16[1,8,64,512]{3,2,1,0:T(8,128)(2,1)S(1)}, u32[]{:S(2)}, u32[]{:S(2)}) %collective-permute-start.7) | collective-permute-done | bytes 524320 | tf_op jit(solution)/shard_map/ppermute | solution.py:39
  111.0 1.6 collective-permute-start.11
  112.6 1.7 collective-permute-start.12
  114.3 2.3 %add.56 = f32[32,8,1024]{2,1,0:T(8,128)} add(f32[32,8,1024]{2,1,0:T(8,128)} %get-tuple-element.27, f32[32,8,1024]{2,1,0:T(8,128)S(1)} %collective-permute-done.10) | non-fusion elementwise | flops 262144 | bytes 3145728 | tf_op jit(solution)/shard_map/reduce_core/add | solution.py:120
  116.7 9.9 %all-to-all-start.2 = ((f32[32,8,1024]{2,1,0:T(8,128)}), f32[32,8,1024]{2,1,0:T(8,128)S(1)}, u32[]{:S(2)}, u32[]{:S(2)}) async-start(f32[32,8,1024]{2,1,0:T(8,128)} %add.56), calls=%async_computation.2 | async-start | bytes 2097152 | tf_op jit(solution)/shard_map/reduce_xz/all_to_all | solution.py:125
  128.4 9.8 %product.3 = (f32[32,8,1024]{2,1,0:T(8,128)}, f32[32,8,1024]{2,1,0:T(8,128)}) custom-call(s32[1]{0:T(128)} %bitcast.place_ref, bf16[1,8,64,512]{3,2,1,0:T(8,128)(2,1)} %copy-done.8, bf16[1,8,64,512]{3,2,1,0:T(8,128)(2,1)} %copy-done.9, bf16[1,8,64,512]{3,2,1,0:T(8,128)(2,1)} %copy-done.10, bf16[1,8,64,512]{3,2,1,0:T(8,128)(2,1)} %collective-permute-done.9.refs_3_, ...), custom_call_target="tpu_custom_call" | custom-call | flops 4294967296 | bytes 14680064 | tf_op jit(solution)/shard_map/product/pallas_call | solution.py:96
  138.3 2.8 %collective-permute-done.13 = f32[32,8,1024]{2,1,0:T(8,128)S(1)} collective-permute-done((f32[32,8,1024]{2,1,0:T(8,128)}, f32[32,8,1024]{2,1,0:T(8,128)S(1)}, u32[]{:S(2)}, u32[]{:S(2)}) %collective-permute-start.13) | collective-permute-done | bytes 1048608 | tf_op jit(solution)/shard_map/reduce_core/ppermute | solution.py:120
  141.1 1.4 add.57
  142.6 2.2 %collective-permute-start.16 = (f32[8,8,1024]{2,1,0:T(8,128)S(1)}, f32[8,8,1024]{2,1,0:T(8,128)S(1)}, u32[]{:S(2)}, u32[]{:S(2)}) collective-permute-start(f32[8,8,1024]{2,1,0:T(8,128)S(1)} %get-tuple-element.36), channel_id=1, source_target_pairs={{0,16},{8,24},{16,0},{24,8},{1,17},{9,25},{17,1},{25,9},{2,18},{10... | collective-permute-start | bytes 786440 | tf_op jit(solution)/shard_map/reduce_x/ppermute | solution.py:135
  144.7 1.5 collective-permute-start.15
  146.7 9.3 %collective-permute-done.16 = f32[8,8,1024]{2,1,0:T(8,128)S(1)} collective-permute-done((f32[8,8,1024]{2,1,0:T(8,128)S(1)}, f32[8,8,1024]{2,1,0:T(8,128)S(1)}, u32[]{:S(2)}, u32[]{:S(2)}) %collective-permute-start.16) | collective-permute-done | bytes 262176 | tf_op jit(solution)/shard_map/reduce_x/ppermute | solution.py:135
  156.0 5.3 %collective-permute-done.15 = f32[8,8,1024]{2,1,0:T(8,128)S(1)} collective-permute-done((f32[8,8,1024]{2,1,0:T(8,128)S(1)}, f32[8,8,1024]{2,1,0:T(8,128)S(1)}, u32[]{:S(2)}, u32[]{:S(2)}) %collective-permute-start.15) | collective-permute-done | bytes 262176 | tf_op jit(solution)/shard_map/reduce_x/ppermute | solution.py:135
  161.3 1.7 fusion.10
  163.1 6.5 %all-to-all-start.3 = ((f32[8,8,1024]{2,1,0:T(8,128)}), f32[8,8,1024]{2,1,0:T(8,128)S(1)}, u32[]{:S(2)}, u32[]{:S(2)}) async-start(f32[8,8,1024]{2,1,0:T(8,128)} %fusion.10), calls=%async_computation.3 | async-start | bytes 524288 | tf_op jit(solution)/shard_map/reduce_z/all_to_all | solution.py:138
  169.6 12.0 %all-to-all-done.3 = f32[8,8,1024]{2,1,0:T(8,128)S(1)} async-done(((f32[8,8,1024]{2,1,0:T(8,128)}), f32[8,8,1024]{2,1,0:T(8,128)S(1)}, u32[]{:S(2)}, u32[]{:S(2)}) %all-to-all-start.3) | async-done | bytes 262176 | tf_op jit(solution)/shard_map/reduce_z/all_to_all | solution.py:138
  (62 shorter events, 6.1 us)
Async XLA Ops:
  0.0 15.4 %copy-start = (bf16[4,256,512]{2,1,0:T(8,128)(2,1)S(1)}, bf16[4,256,512]{2,1,0:T(8,128)(2,1)}, u32[]{:S(2)}) copy-start(bf16[4,256,512]{2,1,0:T(8,128)(2,1)} %param.6) | copy-start | bytes 3145732
  3.4 40.8 %all-to-all-start = ((bf16[64,2,8,512]{3,2,1,0:T(8,128)(2,1)}), bf16[64,2,8,512]{3,2,1,0:T(8,128)(2,1)S(1)}, u32[]{:S(2)}, u32[]{:S(2)}) async-start(bf16[64,2,8,512]{3,2,1,0:T(8,128)(2,1)} %fusion), calls=%async_computation | async-start | bytes 2097152 | tf_op jit(solution)/shard_map/route/all_to_all | solution.py:29
  44.6 34.9 %copy-start.1 = (bf16[8,4,2,1,8,512]{5,0,1,2,4,3:T(8,128)(2,1)}, bf16[8,4,2,1,8,512]{5,0,1,2,4,3:T(8,128)(2,1)S(1)}, u32[]{:S(2)}) copy-start(bf16[8,4,2,1,8,512]{5,0,1,2,4,3:T(8,128)(2,1)S(1)} %copy.16) | copy-start | bytes 1572868
  44.9 34.6 %copy-start.2 = (bf16[8,4,2,1,8,512]{5,0,1,2,4,3:T(8,128)(2,1)}, bf16[8,4,2,1,8,512]{5,0,1,2,4,3:T(8,128)(2,1)S(1)}, u32[]{:S(2)}) copy-start(bf16[8,4,2,1,8,512]{5,0,1,2,4,3:T(8,128)(2,1)S(1)} %copy.17) | copy-start | bytes 1572868
  45.0 34.5 %all-to-all-start.1 = ((bf16[64,2,8,512]{3,2,1,0:T(8,128)(2,1)}), bf16[64,2,8,512]{3,2,1,0:T(8,128)(2,1)S(1)}, u32[]{:S(2)}, u32[]{:S(2)}) async-start(bf16[64,2,8,512]{3,2,1,0:T(8,128)(2,1)} %fusion.1), calls=%async_computation.1 | async-start | bytes 2097152 | tf_op jit(solution)/shard_map/route/all_to_all | solution.py:29
  50.6 16.1 %collective-permute-start.2 = (bf16[1,8,64,512]{3,2,1,0:T(8,128)(2,1)S(1)}, bf16[1,8,64,512]{3,2,1,0:T(8,128)(2,1)}, u32[]{:S(2)}, u32[]{:S(2)}) collective-permute-start(bf16[1,8,64,512]{3,2,1,0:T(8,128)(2,1)S(1)} %bitcast.56), channel_id=1, source_target_pairs={{0,1},{1,2},{2,3},{3,0},{4,5},{5,6},{6,7},{7,4},{8,9},{9,10},{10,1... | collective-permute-start | bytes 1572872 | tf_op jit(solution)/shard_map/ppermute | solution.py:39
  52.3 14.9 %collective-permute-start.1 = (bf16[1,8,64,512]{3,2,1,0:T(8,128)(2,1)S(1)}, bf16[1,8,64,512]{3,2,1,0:T(8,128)(2,1)}, u32[]{:S(2)}, u32[]{:S(2)}) collective-permute-start(bf16[1,8,64,512]{3,2,1,0:T(8,128)(2,1)S(1)} %bitcast.59), channel_id=1, source_target_pairs={{0,3},{1,0},{2,1},{3,2},{4,7},{5,4},{6,5},{7,6},{8,11},{9,8},{10,9... | collective-permute-start | bytes 1572872 | tf_op jit(solution)/shard_map/ppermute | solution.py:43
  53.9 26.3 %collective-permute-start = (bf16[1,8,64,512]{3,2,1,0:T(8,128)(2,1)S(1)}, bf16[1,8,64,512]{3,2,1,0:T(8,128)(2,1)}, u32[]{:S(2)}, u32[]{:S(2)}) collective-permute-start(bf16[1,8,64,512]{3,2,1,0:T(8,128)(2,1)S(1)} %bitcast.57), channel_id=1, source_target_pairs={{0,3},{1,0},{2,1},{3,2},{4,7},{5,4},{6,5},{7,6},{8,11},{9,8},{10,9... | collective-permute-start | bytes 1572872 | tf_op jit(solution)/shard_map/ppermute | solution.py:43
  55.7 24.5 %collective-permute-start.3 = (bf16[1,8,64,512]{3,2,1,0:T(8,128)(2,1)S(1)}, bf16[1,8,64,512]{3,2,1,0:T(8,128)(2,1)}, u32[]{:S(2)}, u32[]{:S(2)}) collective-permute-start(bf16[1,8,64,512]{3,2,1,0:T(8,128)(2,1)S(1)} %bitcast.60), channel_id=1, source_target_pairs={{0,1},{1,2},{2,3},{3,0},{4,5},{5,6},{6,7},{7,4},{8,9},{9,10},{10,1... | collective-permute-start | bytes 1572872 | tf_op jit(solution)/shard_map/ppermute | solution.py:39
  66.8 22.4 %collective-permute-start.4 = (bf16[1,8,64,512]{3,2,1,0:T(8,128)(2,1)}, bf16[1,8,64,512]{3,2,1,0:T(8,128)(2,1)S(1)}, u32[]{:S(2)}, u32[]{:S(2)}) collective-permute-start(bf16[1,8,64,512]{3,2,1,0:T(8,128)(2,1)} %collective-permute-done.2.refs_4_), channel_id=1, source_target_pairs={{0,1},{1,2},{2,3},{3,0},{4,5},{5,6},{6,7},{7,4},{8,9},{9,10},{10,1... | collective-permute-start | bytes 1572872 | tf_op jit(solution)/shard_map/ppermute | solution.py:39
  67.2 33.6 %collective-permute-start.5 = (bf16[1,8,64,512]{3,2,1,0:T(8,128)(2,1)}, bf16[1,8,64,512]{3,2,1,0:T(8,128)(2,1)S(1)}, u32[]{:S(2)}, u32[]{:S(2)}) collective-permute-start(bf16[1,8,64,512]{3,2,1,0:T(8,128)(2,1)} %collective-permute-done.1.refs_3_), channel_id=1, source_target_pairs={{0,3},{1,0},{2,1},{3,2},{4,7},{5,4},{6,5},{7,6},{8,11},{9,8},{10,9... | collective-permute-start | bytes 1572872 | tf_op jit(solution)/shard_map/ppermute | solution.py:43
  79.9 11.1 %copy-start.4 = (bf16[8,4,2,1,8,512]{5,0,1,2,4,3:T(8,128)(2,1)}, bf16[8,4,2,1,8,512]{5,0,1,2,4,3:T(8,128)(2,1)S(1)}, u32[]{:S(2)}) copy-start(bf16[8,4,2,1,8,512]{5,0,1,2,4,3:T(8,128)(2,1)S(1)} %copy.18) | copy-start | bytes 1572868
  80.2 10.8 %copy-start.3 = (bf16[8,4,2,1,8,512]{5,0,1,2,4,3:T(8,128)(2,1)}, bf16[8,4,2,1,8,512]{5,0,1,2,4,3:T(8,128)(2,1)S(1)}, u32[]{:S(2)}) copy-start(bf16[8,4,2,1,8,512]{5,0,1,2,4,3:T(8,128)(2,1)S(1)} %copy.19) | copy-start | bytes 1572868
  80.2 20.6 %collective-permute-start.6 = (bf16[1,8,64,512]{3,2,1,0:T(8,128)(2,1)S(1)}, bf16[1,8,64,512]{3,2,1,0:T(8,128)(2,1)}, u32[]{:S(2)}, u32[]{:S(2)}) collective-permute-start(bf16[1,8,64,512]{3,2,1,0:T(8,128)(2,1)S(1)} %bitcast.65), channel_id=1, source_target_pairs={{0,1},{1,2},{2,3},{3,0},{4,5},{5,6},{6,7},{7,4},{8,9},{9,10},{10,1... | collective-permute-start | bytes 1572872 | tf_op jit(solution)/shard_map/ppermute | solution.py:39
  81.9 29.0 %collective-permute-start.8 = (bf16[1,8,64,512]{3,2,1,0:T(8,128)(2,1)S(1)}, bf16[1,8,64,512]{3,2,1,0:T(8,128)(2,1)S(1)}, u32[]{:S(2)}, u32[]{:S(2)}) collective-permute-start(bf16[1,8,64,512]{3,2,1,0:T(8,128)(2,1)S(1)} %bitcast.66), channel_id=1, source_target_pairs={{0,3},{1,0},{2,1},{3,2},{4,7},{5,4},{6,5},{7,6},{8,11},{9,8},{10,9... | collective-permute-start | bytes 1572872 | tf_op jit(solution)/shard_map/ppermute | solution.py:43
  83.5 27.4 %collective-permute-start.7 = (bf16[1,8,64,512]{3,2,1,0:T(8,128)(2,1)S(1)}, bf16[1,8,64,512]{3,2,1,0:T(8,128)(2,1)S(1)}, u32[]{:S(2)}, u32[]{:S(2)}) collective-permute-start(bf16[1,8,64,512]{3,2,1,0:T(8,128)(2,1)S(1)} %bitcast.62), channel_id=1, source_target_pairs={{0,1},{1,2},{2,3},{3,0},{4,5},{5,6},{6,7},{7,4},{8,9},{9,10},{10,1... | collective-permute-start | bytes 1572872 | tf_op jit(solution)/shard_map/ppermute | solution.py:39
  89.1 11.6 %copy-start.8 = (bf16[1,8,64,512]{3,2,1,0:T(8,128)(2,1)}, bf16[1,8,64,512]{3,2,1,0:T(8,128)(2,1)S(1)}, u32[]{:S(2)}) copy-start(bf16[1,8,64,512]{3,2,1,0:T(8,128)(2,1)S(1)} %collective-permute-done.4.refs_0_) | copy-start | bytes 1572868
  89.1 21.9 %collective-permute-start.9 = (bf16[1,8,64,512]{3,2,1,0:T(8,128)(2,1)S(1)}, bf16[1,8,64,512]{3,2,1,0:T(8,128)(2,1)}, u32[]{:S(2)}, u32[]{:S(2)}) collective-permute-start(bf16[1,8,64,512]{3,2,1,0:T(8,128)(2,1)S(1)} %bitcast.63), channel_id=1, source_target_pairs={{0,3},{1,0},{2,1},{3,2},{4,7},{5,4},{6,5},{7,6},{8,11},{9,8},{10,9... | collective-permute-start | bytes 1572872 | tf_op jit(solution)/shard_map/ppermute | solution.py:43
  100.8 15.9 %copy-start.9 = (bf16[1,8,64,512]{3,2,1,0:T(8,128)(2,1)}, bf16[1,8,64,512]{3,2,1,0:T(8,128)(2,1)S(1)}, u32[]{:S(2)}) copy-start(bf16[1,8,64,512]{3,2,1,0:T(8,128)(2,1)S(1)} %collective-permute-done.5.refs_1_) | copy-start | bytes 1572868
  110.9 5.8 %copy-start.11 = (bf16[1,8,64,512]{3,2,1,0:T(8,128)(2,1)}, bf16[1,8,64,512]{3,2,1,0:T(8,128)(2,1)S(1)}, u32[]{:S(2)}) copy-start(bf16[1,8,64,512]{3,2,1,0:T(8,128)(2,1)S(1)} %collective-permute-done.7.refs_5_) | copy-start | bytes 1572868
  111.0 3.3 %collective-permute-start.10 = (f32[32,8,1024]{2,1,0:T(8,128)}, f32[32,8,1024]{2,1,0:T(8,128)S(1)}, u32[]{:S(2)}, u32[]{:S(2)}) collective-permute-start(f32[32,8,1024]{2,1,0:T(8,128)} %get-tuple-element.29), channel_id=1, source_target_pairs={{0,4},{4,0},{1,5},{5,1},{2,6},{6,2},{3,7},{7,3},{8,12},{12,8},{9,1... | collective-permute-start | bytes 3145736 | tf_op jit(solution)/shard_map/reduce_core/ppermute | solution.py:120
  111.0 15.8 %collective-permute-start.11 = (bf16[1,8,64,512]{3,2,1,0:T(8,128)(2,1)}, bf16[1,8,64,512]{3,2,1,0:T(8,128)(2,1)S(1)}, u32[]{:S(2)}, u32[]{:S(2)}) collective-permute-start(bf16[1,8,64,512]{3,2,1,0:T(8,128)(2,1)} %collective-permute-done.6.refs_4_), channel_id=1, source_target_pairs={{0,1},{1,2},{2,3},{3,0},{4,5},{5,6},{6,7},{7,4},{8,9},{9,10},{10,1... | collective-permute-start | bytes 1572872 | tf_op jit(solution)/shard_map/ppermute | solution.py:39
  112.6 14.3 %collective-permute-start.12 = (bf16[1,8,64,512]{3,2,1,0:T(8,128)(2,1)}, bf16[1,8,64,512]{3,2,1,0:T(8,128)(2,1)S(1)}, u32[]{:S(2)}, u32[]{:S(2)}) collective-permute-start(bf16[1,8,64,512]{3,2,1,0:T(8,128)(2,1)} %collective-permute-done.9.refs_3_), channel_id=1, source_target_pairs={{0,3},{1,0},{2,1},{3,2},{4,7},{5,4},{6,5},{7,6},{8,11},{9,8},{10,9... | collective-permute-start | bytes 1572872 | tf_op jit(solution)/shard_map/ppermute | solution.py:43
  116.7 46.3 %all-to-all-start.2 = ((f32[32,8,1024]{2,1,0:T(8,128)}), f32[32,8,1024]{2,1,0:T(8,128)S(1)}, u32[]{:S(2)}, u32[]{:S(2)}) async-start(f32[32,8,1024]{2,1,0:T(8,128)} %add.56), calls=%async_computation.2 | async-start | bytes 2097152 | tf_op jit(solution)/shard_map/reduce_xz/all_to_all | solution.py:125
  138.2 2.9 %collective-permute-start.13 = (f32[32,8,1024]{2,1,0:T(8,128)}, f32[32,8,1024]{2,1,0:T(8,128)S(1)}, u32[]{:S(2)}, u32[]{:S(2)}) collective-permute-start(f32[32,8,1024]{2,1,0:T(8,128)} %get-tuple-element.33), channel_id=1, source_target_pairs={{0,4},{4,0},{1,5},{5,1},{2,6},{6,2},{3,7},{7,3},{8,12},{12,8},{9,1... | collective-permute-start | bytes 3145736 | tf_op jit(solution)/shard_map/reduce_core/ppermute | solution.py:120
  142.5 39.3 %copy-start.5 = (bf16[16,1024]{1,0:T(8,128)(2,1)S(1)}, bf16[16,1024]{1,0:T(8,128)(2,1)}, u32[]{:S(2)}) copy-start(bf16[16,1024]{1,0:T(8,128)(2,1)} %param.9) | copy-start | bytes 98308
  142.5 39.3 %copy-start.6 = (f32[1024]{0:T(1024)S(1)}, f32[1024]{0:T(1024)}, u32[]{:S(2)}) copy-start(f32[1024]{0:T(1024)} %param.11) | copy-start | bytes 12292
  142.6 39.3 %copy-start.7 = (f32[16]{0:T(128)S(1)}, f32[16]{0:T(128)}, u32[]{:S(2)}) copy-start(f32[16]{0:T(128)} %param.10) | copy-start | bytes 196
  142.6 13.4 %collective-permute-start.16 = (f32[8,8,1024]{2,1,0:T(8,128)S(1)}, f32[8,8,1024]{2,1,0:T(8,128)S(1)}, u32[]{:S(2)}, u32[]{:S(2)}) collective-permute-start(f32[8,8,1024]{2,1,0:T(8,128)S(1)} %get-tuple-element.36), channel_id=1, source_target_pairs={{0,16},{8,24},{16,0},{24,8},{1,17},{9,25},{17,1},{25,9},{2,18},{10... | collective-permute-start | bytes 786440 | tf_op jit(solution)/shard_map/reduce_x/ppermute | solution.py:135
  144.7 16.6 %collective-permute-start.15 = (f32[8,8,1024]{2,1,0:T(8,128)S(1)}, f32[8,8,1024]{2,1,0:T(8,128)S(1)}, u32[]{:S(2)}, u32[]{:S(2)}) collective-permute-start(f32[8,8,1024]{2,1,0:T(8,128)S(1)} %get-tuple-element.37), channel_id=1, source_target_pairs={{0,24},{8,0},{16,8},{24,16},{1,25},{9,1},{17,9},{25,17},{2,26},{10... | collective-permute-start | bytes 786440 | tf_op jit(solution)/shard_map/reduce_x/ppermute | solution.py:135
  146.2 15.1 %collective-permute-start.14 = (f32[8,8,1024]{2,1,0:T(8,128)S(1)}, f32[8,8,1024]{2,1,0:T(8,128)}, u32[]{:S(2)}, u32[]{:S(2)}) collective-permute-start(f32[8,8,1024]{2,1,0:T(8,128)S(1)} %get-tuple-element.35), channel_id=1, source_target_pairs={{0,8},{8,16},{16,24},{24,0},{1,9},{9,17},{17,25},{25,1},{2,10},{10... | collective-permute-start | bytes 786440 | tf_op jit(solution)/shard_map/reduce_x/ppermute | solution.py:135
  163.1 18.6 %all-to-all-start.3 = ((f32[8,8,1024]{2,1,0:T(8,128)}), f32[8,8,1024]{2,1,0:T(8,128)S(1)}, u32[]{:S(2)}, u32[]{:S(2)}) async-start(f32[8,8,1024]{2,1,0:T(8,128)} %fusion.10), calls=%async_computation.3 | async-start | bytes 524288 | tf_op jit(solution)/shard_map/reduce_z/all_to_all | solution.py:138
  (3 other events, 7.4 us)

commit v9 on v8

--- a/solution.py
+++ b/solution.py
@@ -6,6 +6,7 @@
 from jax.sharding import Mesh, PartitionSpec as P
 
 NZ, NX, NC, NY = 8, 4, 2, 4
+LANES = 128
 
 
 def ring(size, shift):
@@ -76,8 +77,10 @@
 
             def put(first_ref, second_ref):
                 for r in range(total):
-                    first_ref[:, r, :] = sums[r, :near]
-                    second_ref[:, r, :] = sums[r, near:]
+                    for c in range(n // LANES):
+                        piece = sums[r, :, c * LANES : (c + 1) * LANES]
+                        first_ref[:, r * (n // LANES) + c, :] = piece[:near]
+                        second_ref[:, r * (n // LANES) + c, :] = piece[near:]
 
             @pl.when(place_ref[0] == 0)
             def _():
@@ -87,8 +90,8 @@
             def _():
                 put(away_ref, kept_ref)
 
-    out = jax.ShapeDtypeStruct((near, total, n), jnp.float32)
-    out_spec = pl.BlockSpec((near, total, n), lambda i, place: (0, 0, 0))
+    out = jax.ShapeDtypeStruct((near, total * n // LANES, LANES), jnp.float32)
+    out_spec = pl.BlockSpec(out.shape, lambda i, place: (0, 0, 0))
     row_specs = [
         pl.BlockSpec((part.shape[0], group, tiles, width), lambda i, place: (0, i, 0, 0))
         for part in parts
@@ -159,20 +162,18 @@
     across = [forward(before[0]), backward(after[1])]
     before_later = [forward(row) for row in later]
     after_later = [backward(row) for row in later]
-    kept, away = product([*own, *after, *before, *later], integrals)
-    (away,) = after_that((across, before_later, after_later), away)
+    kept, away = product([*own, *after, *before, *later, across[0]], integrals)
+    (away,) = after_that((before_later, after_later, across), away)
     early = over_core((kept, away))
-    (across,) = after_that(early, across)
+
+    across_later = [forward(before_later[0]), backward(after_later[1])]
+    sides = after_that(early, *after_later, *before_later)
     early = over_xz(early)
-
-    across_later = [forward(before_later[0]), backward(after_later[1])]
-    late = product([*across, *after_later, *before_later, *across_later], integrals)
+    late = product([across[1], *sides, *across_later], integrals)
     late = over_x_then_z(over_core(late), early)
 
-    early = early.reshape(4, step, n)
-    late = late.reshape(4, step, n)
-    own, after, before, later = (early[i] for i in range(4))
-    across, after_later, before_later, across_later = (late[i] for i in range(4))
+    sums = jnp.concatenate([early, late]).reshape(8, step, n)
+    own, after, before, later, across, after_later, before_later, across_later = sums
     relative = jnp.concatenate(
         [own, later, after, after_later, across, across_later, before, before_later]
     ).reshape(NY, 2 * step, n)

time: 183 us -> 179 us (0.978)
  waiting for transfers between devices: 92.7 us -> 90.4 us
    ppermute x6, waiting for transfers between devices: 26.4 us -> 24.1 us  [forward(): return lax.ppermute(row, 'y', ring(NY, 1))]
  transfers between devices with their start and end apart: 21 -> 21, of which waited for: 11 -> 11; matrix products, arithmetic and copies ran while one was open for 4% -> 4% of each run, Pallas kernels for 11% -> 12%
where the time goes in v9:
time: 179 us
  waiting for transfers between devices  90.4 us (51%)
  starting transfers between devices  54.6 us (31%)
  Pallas kernels  20.8 us (12%)
  other arithmetic  5.26 us (3%)
  matrix products  3.95 us (2%)
  local copies, waits for them, and re-layouts  3.35 us (2%)
    all_to_all x2, waiting for transfers between devices, route(): routed = lax.all_to_all(outgoing, ('z', 'x', 'core'), 0, 0, tiled=True)  36.7 us
    ppermute x6, waiting for transfers between devices, forward(): return lax.ppermute(row, 'y', ring(NY, 1))  24.1 us
    pallas_call x2, Pallas kernels, product(): pl.pallas_call(body, grid_spec=pltpu.PrefetchScalarGridSpec(num_scalar_pr...  20.8 us
    all_to_all x2, starting transfers between devices, route(): routed = lax.all_to_all(outgoing, ('z', 'x', 'core'), 0, 0, tiled=True)  17.8 us
    ppermute x3, waiting for transfers between devices, over_x_then_z(): total += lax.ppermute(away, 'x', ring(NX, shift))  16.1 us
    ppermute x6, starting transfers between devices, backward(): return lax.ppermute(row, 'y', ring(NY, -1))  11.4 us
    all_to_all x1, waiting for transfers between devices, over_x_then_z(): return jnp.sum(lax.all_to_all(total, 'z', 0, 0, tiled=True), axis=0)  10.8 us
    all_to_all x1, starting transfers between devices, over_xz(): lax.all_to_all(outgoing, ('x', 'z'), 0, 0, tiled=True)  9.91 us
  transfers between devices with their start and end apart: 21, of which 11 were waited for; matrix products, arithmetic and copies ran while one was open for 4% of the time, Pallas kernels for 12%

profile of v9, /device:TPU:2, one launch (start us, length us, event | category | flops | bytes accessed | tf_op | source)
XLA Modules:
  0.0 178.7 jit_solution(2853585994196427013)
XLA Ops:
  0.8 2.5 %fusion = bf16[64,2,8,512]{3,2,1,0:T(8,128)(2,1)} fusion(bf16[4,256,512]{2,1,0:T(8,128)(2,1)} %param.6, s32[64,8]{1,0:T(8,128)S(1)} %eq.21), kind=kOutput, calls=%fused_computation.2 | convolution fusion | flops 269090816 | bytes 1574912 | tf_op jit(solution)/shard_map/pick/tsg,rgb->trsb/dot_general | solution.py:22
  3.3 12.2 %all-to-all-start = ((bf16[64,2,8,512]{3,2,1,0:T(8,128)(2,1)}), bf16[64,2,8,512]{3,2,1,0:T(8,128)(2,1)S(1)}, u32[]{:S(2)}, u32[]{:S(2)}) async-start(bf16[64,2,8,512]{3,2,1,0:T(8,128)(2,1)} %fusion), calls=%async_computation | async-start | bytes 2097152 | tf_op jit(solution)/shard_map/route/all_to_all | solution.py:30
  15.4 1.5 fusion.1
  16.9 27.3 %all-to-all-done = bf16[64,2,8,512]{3,2,1,0:T(8,128)(2,1)S(1)} async-done(((bf16[64,2,8,512]{3,2,1,0:T(8,128)(2,1)}), bf16[64,2,8,512]{3,2,1,0:T(8,128)(2,1)S(1)}, u32[]{:S(2)}, u32[]{:S(2)}) %all-to-all-start) | async-done | bytes 1048608 | tf_op jit(solution)/shard_map/route/all_to_all | solution.py:30
  45.0 5.7 %all-to-all-start.1 = ((bf16[64,2,8,512]{3,2,1,0:T(8,128)(2,1)}), bf16[64,2,8,512]{3,2,1,0:T(8,128)(2,1)S(1)}, u32[]{:S(2)}, u32[]{:S(2)}) async-start(bf16[64,2,8,512]{3,2,1,0:T(8,128)(2,1)} %fusion.1), calls=%async_computation.1 | async-start | bytes 2097152 | tf_op jit(solution)/shard_map/route/all_to_all | solution.py:30
  50.7 1.7 collective-permute-start.2
  52.3 1.7 collective-permute-start.1
  54.0 1.8 %collective-permute-start = (bf16[1,8,64,512]{3,2,1,0:T(8,128)(2,1)S(1)}, bf16[1,8,64,512]{3,2,1,0:T(8,128)(2,1)S(1)}, u32[]{:S(2)}, u32[]{:S(2)}) collective-permute-start(bf16[1,8,64,512]{3,2,1,0:T(8,128)(2,1)S(1)} %bitcast.60), channel_id=1, source_target_pairs={{0,3},{1,0},{2,1},{3,2},{4,7},{5,4},{6,5},{7,6},{8,11},{9,8},{10,9... | collective-permute-start | bytes 1572872 | tf_op jit(solution)/shard_map/ppermute | solution.py:44
  56.0 10.8 %collective-permute-done.2.refs_4_ = bf16[1,8,64,512]{3,2,1,0:T(8,128)(2,1)} collective-permute-done((bf16[1,8,64,512]{3,2,1,0:T(8,128)(2,1)S(1)}, bf16[1,8,64,512]{3,2,1,0:T(8,128)(2,1)}, u32[]{:S(2)}, u32[]{:S(2)}) %collective-permute-start.2) | collective-permute-done | bytes 524320 | tf_op jit(solution)/shard_map/ppermute | solution.py:40
  67.2 2.9 %collective-permute-start.9 = (bf16[1,8,64,512]{3,2,1,0:T(8,128)(2,1)}, bf16[1,8,64,512]{3,2,1,0:T(8,128)(2,1)S(1)}, u32[]{:S(2)}, u32[]{:S(2)}) collective-permute-start(bf16[1,8,64,512]{3,2,1,0:T(8,128)(2,1)} %collective-permute-done.1.refs_3_), channel_id=1, source_target_pairs={{0,3},{1,0},{2,1},{3,2},{4,7},{5,4},{6,5},{7,6},{8,11},{9,8},{10,9... | collective-permute-start | bytes 1572872 | tf_op jit(solution)/shard_map/ppermute | solution.py:44
  70.1 9.4 %all-to-all-done.1 = bf16[64,2,8,512]{3,2,1,0:T(8,128)(2,1)S(1)} async-done(((bf16[64,2,8,512]{3,2,1,0:T(8,128)(2,1)}), bf16[64,2,8,512]{3,2,1,0:T(8,128)(2,1)S(1)}, u32[]{:S(2)}, u32[]{:S(2)}) %all-to-all-start.1) | async-done | bytes 1048608 | tf_op jit(solution)/shard_map/route/all_to_all | solution.py:30
  80.3 0.8 copy-done.11
  81.1 1.6 collective-permute-start.5
  82.7 1.7 collective-permute-start.8
  84.7 4.6 %collective-permute-done.4.refs_8_ = bf16[1,8,64,512]{3,2,1,0:T(8,128)(2,1)} collective-permute-done((bf16[1,8,64,512]{3,2,1,0:T(8,128)(2,1)}, bf16[1,8,64,512]{3,2,1,0:T(8,128)(2,1)}, u32[]{:S(2)}, u32[]{:S(2)}) %collective-permute-start.4) | collective-permute-done | bytes 524320 | tf_op jit(solution)/shard_map/ppermute | solution.py:40
  89.3 1.8 %collective-permute-start.7 = (bf16[1,8,64,512]{3,2,1,0:T(8,128)(2,1)S(1)}, bf16[1,8,64,512]{3,2,1,0:T(8,128)(2,1)}, u32[]{:S(2)}, u32[]{:S(2)}) collective-permute-start(bf16[1,8,64,512]{3,2,1,0:T(8,128)(2,1)S(1)} %bitcast.63), channel_id=1, source_target_pairs={{0,3},{1,0},{2,1},{3,2},{4,7},{5,4},{6,5},{7,6},{8,11},{9,8},{10,9... | collective-permute-start | bytes 1572872 | tf_op jit(solution)/shard_map/ppermute | solution.py:44
  91.1 11.3 %product.2 = (f32[32,72,128]{2,1,0:T(8,128)}, f32[32,72,128]{2,1,0:T(8,128)}) custom-call(s32[1]{0:T(128)} %bitcast.place_ref, bf16[1,8,64,512]{3,2,1,0:T(8,128)(2,1)} %bitcast.61, bf16[1,8,64,512]{3,2,1,0:T(8,128)(2,1)} %bitcast.58, bf16[1,8,64,512]{3,2,1,0:T(8,128)(2,1)} %copy-done.11, bf16[1,8,64,512]{3,2,1,0:T(8,128)(2,1)} %collective-permute-done.1.refs_3_, ...), custom_call_target="tpu_custom_call" | custom-call | flops 4831838208 | bytes 15466496 | tf_op jit(solution)/shard_map/product/pallas_call | solution.py:99
  102.5 8.6 %collective-permute-done.6.refs_4_ = bf16[1,8,64,512]{3,2,1,0:T(8,128)(2,1)} collective-permute-done((bf16[1,8,64,512]{3,2,1,0:T(8,128)(2,1)S(1)}, bf16[1,8,64,512]{3,2,1,0:T(8,128)(2,1)}, u32[]{:S(2)}, u32[]{:S(2)}) %collective-permute-start.6) | collective-permute-done | bytes 524320 | tf_op jit(solution)/shard_map/ppermute | solution.py:40
  111.1 1.6 collective-permute-start.11
  112.6 1.7 collective-permute-start.12
  114.3 2.4 %add.56 = f32[32,72,128]{2,1,0:T(8,128)} add(f32[32,72,128]{2,1,0:T(8,128)} %get-tuple-element.29, f32[32,72,128]{2,1,0:T(8,128)S(1)} %collective-permute-done.10) | non-fusion elementwise | flops 294912 | bytes 3538944 | tf_op jit(solution)/shard_map/reduce_core/add | solution.py:123
  116.7 9.9 %all-to-all-start.2 = ((f32[32,72,128]{2,1,0:T(8,128)}), f32[32,72,128]{2,1,0:T(8,128)S(1)}, u32[]{:S(2)}, u32[]{:S(2)}) async-start(f32[32,72,128]{2,1,0:T(8,128)} %add.56), calls=%async_computation.2 | async-start | bytes 2359296 | tf_op jit(solution)/shard_map/reduce_xz/all_to_all | solution.py:128
  126.8 9.4 %product.3 = (f32[32,56,128]{2,1,0:T(8,128)}, f32[32,56,128]{2,1,0:T(8,128)}) custom-call(s32[1]{0:T(128)} %bitcast.place_ref, bf16[1,8,64,512]{3,2,1,0:T(8,128)(2,1)} %copy-done.8, bf16[1,8,64,512]{3,2,1,0:T(8,128)(2,1)} %collective-permute-done.7.refs_1_, bf16[1,8,64,512]{3,2,1,0:T(8,128)(2,1)} %copy-done.10, bf16[1,8,64,512]{3,2,1,0:T(8,128)(2,1)} %copy-done.9, ...), custom_call_target="tpu_custom_call" | custom-call | flops 3758096384 | bytes 13893632 | tf_op jit(solution)/shard_map/product/pallas_call | solution.py:99
  136.3 2.6 %collective-permute-done.13 = f32[32,56,128]{2,1,0:T(8,128)S(1)} collective-permute-done((f32[32,56,128]{2,1,0:T(8,128)}, f32[32,56,128]{2,1,0:T(8,128)S(1)}, u32[]{:S(2)}, u32[]{:S(2)}) %collective-permute-start.13) | collective-permute-done | bytes 917536 | tf_op jit(solution)/shard_map/reduce_core/ppermute | solution.py:123
  138.9 1.3 add.57
  140.3 1.5 collective-permute-start.14
  142.4 2.1 %collective-permute-start.16 = (f32[8,56,128]{2,1,0:T(8,128)S(1)}, f32[8,56,128]{2,1,0:T(8,128)S(1)}, u32[]{:S(2)}, u32[]{:S(2)}) collective-permute-start(f32[8,56,128]{2,1,0:T(8,128)S(1)} %get-tuple-element.44), channel_id=1, source_target_pairs={{0,16},{8,24},{16,0},{24,8},{1,17},{9,25},{17,1},{25,9},{2,18},{10... | collective-permute-start | bytes 688136 | tf_op jit(solution)/shard_map/reduce_x/ppermute | solution.py:138
  144.4 8.7 %collective-permute-done.14 = f32[8,56,128]{2,1,0:T(8,128)S(1)} collective-permute-done((f32[8,56,128]{2,1,0:T(8,128)S(1)}, f32[8,56,128]{2,1,0:T(8,128)S(1)}, u32[]{:S(2)}, u32[]{:S(2)}) %collective-permute-start.14) | collective-permute-done | bytes 229408 | tf_op jit(solution)/shard_map/reduce_x/ppermute | solution.py:138
  153.2 2.0 %collective-permute-done.15 = f32[8,56,128]{2,1,0:T(8,128)S(1)} collective-permute-done((f32[8,56,128]{2,1,0:T(8,128)S(1)}, f32[8,56,128]{2,1,0:T(8,128)S(1)}, u32[]{:S(2)}, u32[]{:S(2)}) %collective-permute-start.15) | collective-permute-done | bytes 229408 | tf_op jit(solution)/shard_map/reduce_x/ppermute | solution.py:138
  155.1 5.4 %collective-permute-done.16 = f32[8,56,128]{2,1,0:T(8,128)S(1)} collective-permute-done((f32[8,56,128]{2,1,0:T(8,128)S(1)}, f32[8,56,128]{2,1,0:T(8,128)S(1)}, u32[]{:S(2)}, u32[]{:S(2)}) %collective-permute-start.16) | collective-permute-done | bytes 229408 | tf_op jit(solution)/shard_map/reduce_x/ppermute | solution.py:138
  161.3 5.5 %all-to-all-start.3 = ((f32[8,56,128]{2,1,0:T(8,128)}), f32[8,56,128]{2,1,0:T(8,128)S(1)}, u32[]{:S(2)}, u32[]{:S(2)}) async-start(f32[8,56,128]{2,1,0:T(8,128)} %fusion.12), calls=%async_computation.3 | async-start | bytes 458752 | tf_op jit(solution)/shard_map/reduce_z/all_to_all | solution.py:141
  166.8 10.8 %all-to-all-done.3 = f32[8,56,128]{2,1,0:T(8,128)S(1)} async-done(((f32[8,56,128]{2,1,0:T(8,128)}), f32[8,56,128]{2,1,0:T(8,128)S(1)}, u32[]{:S(2)}, u32[]{:S(2)}) %all-to-all-start.3) | async-done | bytes 229408 | tf_op jit(solution)/shard_map/reduce_z/all_to_all | solution.py:141
  (65 shorter events, 5.9 us)
Async XLA Ops:
  3.3 12.2 %copy-start = (bf16[4,256,512]{2,1,0:T(8,128)(2,1)S(1)}, bf16[4,256,512]{2,1,0:T(8,128)(2,1)}, u32[]{:S(2)}) copy-start(bf16[4,256,512]{2,1,0:T(8,128)(2,1)} %param.6) | copy-start | bytes 3145732
  3.3 41.0 %all-to-all-start = ((bf16[64,2,8,512]{3,2,1,0:T(8,128)(2,1)}), bf16[64,2,8,512]{3,2,1,0:T(8,128)(2,1)S(1)}, u32[]{:S(2)}, u32[]{:S(2)}) async-start(bf16[64,2,8,512]{3,2,1,0:T(8,128)(2,1)} %fusion), calls=%async_computation | async-start | bytes 2097152 | tf_op jit(solution)/shard_map/route/all_to_all | solution.py:30
  44.7 11.1 %copy-start.1 = (bf16[8,4,2,1,8,512]{5,0,1,2,4,3:T(8,128)(2,1)}, bf16[8,4,2,1,8,512]{5,0,1,2,4,3:T(8,128)(2,1)S(1)}, u32[]{:S(2)}) copy-start(bf16[8,4,2,1,8,512]{5,0,1,2,4,3:T(8,128)(2,1)S(1)} %copy.17) | copy-start | bytes 1572868
  45.0 34.6 %copy-start.2 = (bf16[8,4,2,1,8,512]{5,0,1,2,4,3:T(8,128)(2,1)}, bf16[8,4,2,1,8,512]{5,0,1,2,4,3:T(8,128)(2,1)S(1)}, u32[]{:S(2)}) copy-start(bf16[8,4,2,1,8,512]{5,0,1,2,4,3:T(8,128)(2,1)S(1)} %copy.16) | copy-start | bytes 1572868
  45.0 34.5 %all-to-all-start.1 = ((bf16[64,2,8,512]{3,2,1,0:T(8,128)(2,1)}), bf16[64,2,8,512]{3,2,1,0:T(8,128)(2,1)S(1)}, u32[]{:S(2)}, u32[]{:S(2)}) async-start(bf16[64,2,8,512]{3,2,1,0:T(8,128)(2,1)} %fusion.1), calls=%async_computation.1 | async-start | bytes 2097152 | tf_op jit(solution)/shard_map/route/all_to_all | solution.py:30
  50.7 16.1 %collective-permute-start.2 = (bf16[1,8,64,512]{3,2,1,0:T(8,128)(2,1)S(1)}, bf16[1,8,64,512]{3,2,1,0:T(8,128)(2,1)}, u32[]{:S(2)}, u32[]{:S(2)}) collective-permute-start(bf16[1,8,64,512]{3,2,1,0:T(8,128)(2,1)S(1)} %bitcast.59), channel_id=1, source_target_pairs={{0,1},{1,2},{2,3},{3,0},{4,5},{5,6},{6,7},{7,4},{8,9},{9,10},{10,1... | collective-permute-start | bytes 1572872 | tf_op jit(solution)/shard_map/ppermute | solution.py:40
  52.3 14.9 %collective-permute-start.1 = (bf16[1,8,64,512]{3,2,1,0:T(8,128)(2,1)S(1)}, bf16[1,8,64,512]{3,2,1,0:T(8,128)(2,1)}, u32[]{:S(2)}, u32[]{:S(2)}) collective-permute-start(bf16[1,8,64,512]{3,2,1,0:T(8,128)(2,1)S(1)} %bitcast.56), channel_id=1, source_target_pairs={{0,3},{1,0},{2,1},{3,2},{4,7},{5,4},{6,5},{7,6},{8,11},{9,8},{10,9... | collective-permute-start | bytes 1572872 | tf_op jit(solution)/shard_map/ppermute | solution.py:44
  54.0 26.3 %collective-permute-start = (bf16[1,8,64,512]{3,2,1,0:T(8,128)(2,1)S(1)}, bf16[1,8,64,512]{3,2,1,0:T(8,128)(2,1)S(1)}, u32[]{:S(2)}, u32[]{:S(2)}) collective-permute-start(bf16[1,8,64,512]{3,2,1,0:T(8,128)(2,1)S(1)} %bitcast.60), channel_id=1, source_target_pairs={{0,3},{1,0},{2,1},{3,2},{4,7},{5,4},{6,5},{7,6},{8,11},{9,8},{10,9... | collective-permute-start | bytes 1572872 | tf_op jit(solution)/shard_map/ppermute | solution.py:44
  55.8 24.5 %collective-permute-start.3 = (bf16[1,8,64,512]{3,2,1,0:T(8,128)(2,1)S(1)}, bf16[1,8,64,512]{3,2,1,0:T(8,128)(2,1)}, u32[]{:S(2)}, u32[]{:S(2)}) collective-permute-start(bf16[1,8,64,512]{3,2,1,0:T(8,128)(2,1)S(1)} %bitcast.57), channel_id=1, source_target_pairs={{0,1},{1,2},{2,3},{3,0},{4,5},{5,6},{6,7},{7,4},{8,9},{9,10},{10,1... | collective-permute-start | bytes 1572872 | tf_op jit(solution)/shard_map/ppermute | solution.py:40
  66.8 22.5 %collective-permute-start.4 = (bf16[1,8,64,512]{3,2,1,0:T(8,128)(2,1)}, bf16[1,8,64,512]{3,2,1,0:T(8,128)(2,1)}, u32[]{:S(2)}, u32[]{:S(2)}) collective-permute-start(bf16[1,8,64,512]{3,2,1,0:T(8,128)(2,1)} %collective-permute-done.2.refs_4_), channel_id=1, source_target_pairs={{0,1},{1,2},{2,3},{3,0},{4,5},{5,6},{6,7},{7,4},{8,9},{9,10},{10,1... | collective-permute-start | bytes 1572872 | tf_op jit(solution)/shard_map/ppermute | solution.py:40
  67.2 35.2 %collective-permute-start.9 = (bf16[1,8,64,512]{3,2,1,0:T(8,128)(2,1)}, bf16[1,8,64,512]{3,2,1,0:T(8,128)(2,1)S(1)}, u32[]{:S(2)}, u32[]{:S(2)}) collective-permute-start(bf16[1,8,64,512]{3,2,1,0:T(8,128)(2,1)} %collective-permute-done.1.refs_3_), channel_id=1, source_target_pairs={{0,3},{1,0},{2,1},{3,2},{4,7},{5,4},{6,5},{7,6},{8,11},{9,8},{10,9... | collective-permute-start | bytes 1572872 | tf_op jit(solution)/shard_map/ppermute | solution.py:44
  79.9 11.2 %copy-start.3 = (bf16[8,4,2,1,8,512]{5,0,1,2,4,3:T(8,128)(2,1)}, bf16[8,4,2,1,8,512]{5,0,1,2,4,3:T(8,128)(2,1)S(1)}, u32[]{:S(2)}) copy-start(bf16[8,4,2,1,8,512]{5,0,1,2,4,3:T(8,128)(2,1)S(1)} %copy.18) | copy-start | bytes 1572868
  80.2 10.9 %copy-start.4 = (bf16[8,4,2,1,8,512]{5,0,1,2,4,3:T(8,128)(2,1)}, bf16[8,4,2,1,8,512]{5,0,1,2,4,3:T(8,128)(2,1)S(1)}, u32[]{:S(2)}) copy-start(bf16[8,4,2,1,8,512]{5,0,1,2,4,3:T(8,128)(2,1)S(1)} %copy.19) | copy-start | bytes 1572868
  81.1 21.4 %collective-permute-start.5 = (bf16[1,8,64,512]{3,2,1,0:T(8,128)(2,1)S(1)}, bf16[1,8,64,512]{3,2,1,0:T(8,128)(2,1)S(1)}, u32[]{:S(2)}, u32[]{:S(2)}) collective-permute-start(bf16[1,8,64,512]{3,2,1,0:T(8,128)(2,1)S(1)} %bitcast.62), channel_id=1, source_target_pairs={{0,1},{1,2},{2,3},{3,0},{4,5},{5,6},{6,7},{7,4},{8,9},{9,10},{10,1... | collective-permute-start | bytes 1572872 | tf_op jit(solution)/shard_map/ppermute | solution.py:40
  82.7 19.8 %collective-permute-start.8 = (bf16[1,8,64,512]{3,2,1,0:T(8,128)(2,1)S(1)}, bf16[1,8,64,512]{3,2,1,0:T(8,128)(2,1)S(1)}, u32[]{:S(2)}, u32[]{:S(2)}) collective-permute-start(bf16[1,8,64,512]{3,2,1,0:T(8,128)(2,1)S(1)} %bitcast.65), channel_id=1, source_target_pairs={{0,3},{1,0},{2,1},{3,2},{4,7},{5,4},{6,5},{7,6},{8,11},{9,8},{10,9... | collective-permute-start | bytes 1572872 | tf_op jit(solution)/shard_map/ppermute | solution.py:44
  84.3 26.7 %collective-permute-start.6 = (bf16[1,8,64,512]{3,2,1,0:T(8,128)(2,1)S(1)}, bf16[1,8,64,512]{3,2,1,0:T(8,128)(2,1)}, u32[]{:S(2)}, u32[]{:S(2)}) collective-permute-start(bf16[1,8,64,512]{3,2,1,0:T(8,128)(2,1)S(1)} %bitcast.66), channel_id=1, source_target_pairs={{0,1},{1,2},{2,3},{3,0},{4,5},{5,6},{6,7},{7,4},{8,9},{9,10},{10,1... | collective-permute-start | bytes 1572872 | tf_op jit(solution)/shard_map/ppermute | solution.py:40
  89.3 21.8 %collective-permute-start.7 = (bf16[1,8,64,512]{3,2,1,0:T(8,128)(2,1)S(1)}, bf16[1,8,64,512]{3,2,1,0:T(8,128)(2,1)}, u32[]{:S(2)}, u32[]{:S(2)}) collective-permute-start(bf16[1,8,64,512]{3,2,1,0:T(8,128)(2,1)S(1)} %bitcast.63), channel_id=1, source_target_pairs={{0,3},{1,0},{2,1},{3,2},{4,7},{5,4},{6,5},{7,6},{8,11},{9,8},{10,9... | collective-permute-start | bytes 1572872 | tf_op jit(solution)/shard_map/ppermute | solution.py:44
  102.4 14.3 %copy-start.8 = (bf16[1,8,64,512]{3,2,1,0:T(8,128)(2,1)}, bf16[1,8,64,512]{3,2,1,0:T(8,128)(2,1)S(1)}, u32[]{:S(2)}) copy-start(bf16[1,8,64,512]{3,2,1,0:T(8,128)(2,1)S(1)} %collective-permute-done.9.refs_0_) | copy-start | bytes 1572868
  102.5 14.3 %copy-start.9 = (bf16[1,8,64,512]{3,2,1,0:T(8,128)(2,1)}, bf16[1,8,64,512]{3,2,1,0:T(8,128)(2,1)S(1)}, u32[]{:S(2)}) copy-start(bf16[1,8,64,512]{3,2,1,0:T(8,128)(2,1)S(1)} %collective-permute-done.5.refs_3_) | copy-start | bytes 1572868
  102.5 14.3 %copy-start.10 = (bf16[1,8,64,512]{3,2,1,0:T(8,128)(2,1)}, bf16[1,8,64,512]{3,2,1,0:T(8,128)(2,1)S(1)}, u32[]{:S(2)}) copy-start(bf16[1,8,64,512]{3,2,1,0:T(8,128)(2,1)S(1)} %collective-permute-done.8.refs_2_) | copy-start | bytes 1572868
  111.1 3.2 %collective-permute-start.10 = (f32[32,72,128]{2,1,0:T(8,128)}, f32[32,72,128]{2,1,0:T(8,128)S(1)}, u32[]{:S(2)}, u32[]{:S(2)}) collective-permute-start(f32[32,72,128]{2,1,0:T(8,128)} %get-tuple-element.31), channel_id=1, source_target_pairs={{0,4},{4,0},{1,5},{5,1},{2,6},{6,2},{3,7},{7,3},{8,12},{12,8},{9,1... | collective-permute-start | bytes 3538952 | tf_op jit(solution)/shard_map/reduce_core/ppermute | solution.py:123
  111.1 15.7 %collective-permute-start.11 = (bf16[1,8,64,512]{3,2,1,0:T(8,128)(2,1)S(1)}, bf16[1,8,64,512]{3,2,1,0:T(8,128)(2,1)}, u32[]{:S(2)}, u32[]{:S(2)}) collective-permute-start(bf16[1,8,64,512]{3,2,1,0:T(8,128)(2,1)S(1)} %collective-permute-done.5.refs_3_), channel_id=1, source_target_pairs={{0,1},{1,2},{2,3},{3,0},{4,5},{5,6},{6,7},{7,4},{8,9},{9,10},{10,1... | collective-permute-start | bytes 1572872 | tf_op jit(solution)/shard_map/ppermute | solution.py:40
  112.6 14.2 %collective-permute-start.12 = (bf16[1,8,64,512]{3,2,1,0:T(8,128)(2,1)S(1)}, bf16[1,8,64,512]{3,2,1,0:T(8,128)(2,1)}, u32[]{:S(2)}, u32[]{:S(2)}) collective-permute-start(bf16[1,8,64,512]{3,2,1,0:T(8,128)(2,1)S(1)} %collective-permute-done.8.refs_2_), channel_id=1, source_target_pairs={{0,3},{1,0},{2,1},{3,2},{4,7},{5,4},{6,5},{7,6},{8,11},{9,8},{10,9... | collective-permute-start | bytes 1572872 | tf_op jit(solution)/shard_map/ppermute | solution.py:44
  116.7 44.5 %all-to-all-start.2 = ((f32[32,72,128]{2,1,0:T(8,128)}), f32[32,72,128]{2,1,0:T(8,128)S(1)}, u32[]{:S(2)}, u32[]{:S(2)}) async-start(f32[32,72,128]{2,1,0:T(8,128)} %add.56), calls=%async_computation.2 | async-start | bytes 2359296 | tf_op jit(solution)/shard_map/reduce_xz/all_to_all | solution.py:128
  136.2 2.7 %collective-permute-start.13 = (f32[32,56,128]{2,1,0:T(8,128)}, f32[32,56,128]{2,1,0:T(8,128)S(1)}, u32[]{:S(2)}, u32[]{:S(2)}) collective-permute-start(f32[32,56,128]{2,1,0:T(8,128)} %get-tuple-element.37), channel_id=1, source_target_pairs={{0,4},{4,0},{1,5},{5,1},{2,6},{6,2},{3,7},{7,3},{8,12},{12,8},{9,1... | collective-permute-start | bytes 2752520 | tf_op jit(solution)/shard_map/reduce_core/ppermute | solution.py:123
  140.3 12.9 %collective-permute-start.14 = (f32[8,56,128]{2,1,0:T(8,128)S(1)}, f32[8,56,128]{2,1,0:T(8,128)S(1)}, u32[]{:S(2)}, u32[]{:S(2)}) collective-permute-start(f32[8,56,128]{2,1,0:T(8,128)S(1)} %get-tuple-element.43), channel_id=1, source_target_pairs={{0,8},{8,16},{16,24},{24,0},{1,9},{9,17},{17,25},{25,1},{2,10},{10... | collective-permute-start | bytes 688136 | tf_op jit(solution)/shard_map/reduce_x/ppermute | solution.py:138
  141.8 13.3 %collective-permute-start.15 = (f32[8,56,128]{2,1,0:T(8,128)S(1)}, f32[8,56,128]{2,1,0:T(8,128)S(1)}, u32[]{:S(2)}, u32[]{:S(2)}) collective-permute-start(f32[8,56,128]{2,1,0:T(8,128)S(1)} %get-tuple-element.45), channel_id=1, source_target_pairs={{0,24},{8,0},{16,8},{24,16},{1,25},{9,1},{17,9},{25,17},{2,26},{10... | collective-permute-start | bytes 688136 | tf_op jit(solution)/shard_map/reduce_x/ppermute | solution.py:138
  142.4 18.2 %collective-permute-start.16 = (f32[8,56,128]{2,1,0:T(8,128)S(1)}, f32[8,56,128]{2,1,0:T(8,128)S(1)}, u32[]{:S(2)}, u32[]{:S(2)}) collective-permute-start(f32[8,56,128]{2,1,0:T(8,128)S(1)} %get-tuple-element.44), channel_id=1, source_target_pairs={{0,16},{8,24},{16,0},{24,8},{1,17},{9,25},{17,1},{25,9},{2,18},{10... | collective-permute-start | bytes 688136 | tf_op jit(solution)/shard_map/reduce_x/ppermute | solution.py:138
  161.2 16.7 %copy-start.5 = (bf16[16,1024]{1,0:T(8,128)(2,1)S(1)}, bf16[16,1024]{1,0:T(8,128)(2,1)}, u32[]{:S(2)}) copy-start(bf16[16,1024]{1,0:T(8,128)(2,1)} %param.9) | copy-start | bytes 98308
  161.2 16.7 %copy-start.6 = (f32[1024]{0:T(1024)S(1)}, f32[1024]{0:T(1024)}, u32[]{:S(2)}) copy-start(f32[1024]{0:T(1024)} %param.11) | copy-start | bytes 12292
  161.2 16.7 %copy-start.7 = (f32[16]{0:T(128)S(1)}, f32[16]{0:T(128)}, u32[]{:S(2)}) copy-start(f32[16]{0:T(128)} %param.10) | copy-start | bytes 196
  161.3 16.3 %all-to-all-start.3 = ((f32[8,56,128]{2,1,0:T(8,128)}), f32[8,56,128]{2,1,0:T(8,128)S(1)}, u32[]{:S(2)}, u32[]{:S(2)}) async-start(f32[8,56,128]{2,1,0:T(8,128)} %fusion.12), calls=%async_computation.3 | async-start | bytes 458752 | tf_op jit(solution)/shard_map/reduce_z/all_to_all | solution.py:141
  (1 other events, 0.8 us)

commit v10 on v9

--- a/solution.py
+++ b/solution.py
@@ -133,7 +133,7 @@
     outgoing = outgoing.reshape(NX, NZ, *outgoing.shape[1:])
     with jax.named_scope("reduce_x"):
         total = lax.dynamic_index_in_dim(outgoing, x, 0, keepdims=False)
-        for shift in (1, 3, 2):
+        for shift in (2, 1, 3):
             away = lax.dynamic_index_in_dim(outgoing, (x + shift) % NX, 0, keepdims=False)
             total += lax.ppermute(away, "x", ring(NX, shift))
     with jax.named_scope("reduce_z"):

time: 179 us -> 180 us (level)
  no operation moved by 1% of the time
where the time goes in v10:
time: 180 us; the launch traced here: 179 us
  waiting for transfers between devices  90.7 us (50%)
  starting transfers between devices  54.7 us (30%)
  Pallas kernels  20.8 us (12%)
  other arithmetic  5.26 us (3%)
  matrix products  3.95 us (2%)
  local copies, waits for them, and re-layouts  3.35 us (2%)
    all_to_all x2, waiting for transfers between devices, route(): routed = lax.all_to_all(outgoing, ('z', 'x', 'core'), 0, 0, tiled=True)  36.7 us
    ppermute x6, waiting for transfers between devices, forward(): return lax.ppermute(row, 'y', ring(NY, 1))  24.1 us
    pallas_call x2, Pallas kernels, product(): pl.pallas_call(body, grid_spec=pltpu.PrefetchScalarGridSpec(num_scalar_pr...  20.8 us
    all_to_all x2, starting transfers between devices, route(): routed = lax.all_to_all(outgoing, ('z', 'x', 'core'), 0, 0, tiled=True)  17.8 us
    ppermute x3, waiting for transfers between devices, over_x_then_z(): total += lax.ppermute(away, 'x', ring(NX, shift))  15.8 us
    ppermute x6, starting transfers between devices, backward(): return lax.ppermute(row, 'y', ring(NY, -1))  11.4 us
    all_to_all x1, waiting for transfers between devices, over_x_then_z(): return jnp.sum(lax.all_to_all(total, 'z', 0, 0, tiled=True), axis=0)  11.4 us
    all_to_all x1, starting transfers between devices, over_xz(): lax.all_to_all(outgoing, ('x', 'z'), 0, 0, tiled=True)  9.91 us
  transfers between devices with their start and end apart: 21, of which 11 were waited for; matrix products, arithmetic and copies ran while one was open for 4% of the time, Pallas kernels for 12%

profile of v10, /device:TPU:2, one launch (start us, length us, event | category | flops | bytes accessed | tf_op | source)
XLA Modules:
  0.0 179.1 jit_solution(9650880552440339826)
XLA Ops:
  0.8 2.5 %fusion = bf16[64,2,8,512]{3,2,1,0:T(8,128)(2,1)} fusion(bf16[4,256,512]{2,1,0:T(8,128)(2,1)} %param.6, s32[64,8]{1,0:T(8,128)S(1)} %eq.21), kind=kOutput, calls=%fused_computation.2 | convolution fusion | flops 269090816 | bytes 1574912 | tf_op jit(solution)/shard_map/pick/tsg,rgb->trsb/dot_general | solution.py:22
  3.3 12.2 %all-to-all-start = ((bf16[64,2,8,512]{3,2,1,0:T(8,128)(2,1)}), bf16[64,2,8,512]{3,2,1,0:T(8,128)(2,1)S(1)}, u32[]{:S(2)}, u32[]{:S(2)}) async-start(bf16[64,2,8,512]{3,2,1,0:T(8,128)(2,1)} %fusion), calls=%async_computation | async-start | bytes 2097152 | tf_op jit(solution)/shard_map/route/all_to_all | solution.py:30
  15.4 1.5 fusion.1
  16.9 27.3 %all-to-all-done = bf16[64,2,8,512]{3,2,1,0:T(8,128)(2,1)S(1)} async-done(((bf16[64,2,8,512]{3,2,1,0:T(8,128)(2,1)}), bf16[64,2,8,512]{3,2,1,0:T(8,128)(2,1)S(1)}, u32[]{:S(2)}, u32[]{:S(2)}) %all-to-all-start) | async-done | bytes 1048608 | tf_op jit(solution)/shard_map/route/all_to_all | solution.py:30
  45.0 5.7 %all-to-all-start.1 = ((bf16[64,2,8,512]{3,2,1,0:T(8,128)(2,1)}), bf16[64,2,8,512]{3,2,1,0:T(8,128)(2,1)S(1)}, u32[]{:S(2)}, u32[]{:S(2)}) async-start(bf16[64,2,8,512]{3,2,1,0:T(8,128)(2,1)} %fusion.1), calls=%async_computation.1 | async-start | bytes 2097152 | tf_op jit(solution)/shard_map/route/all_to_all | solution.py:30
  50.7 1.7 collective-permute-start.2
  52.3 1.7 collective-permute-start.1
  54.0 1.8 %collective-permute-start = (bf16[1,8,64,512]{3,2,1,0:T(8,128)(2,1)S(1)}, bf16[1,8,64,512]{3,2,1,0:T(8,128)(2,1)S(1)}, u32[]{:S(2)}, u32[]{:S(2)}) collective-permute-start(bf16[1,8,64,512]{3,2,1,0:T(8,128)(2,1)S(1)} %bitcast.60), channel_id=1, source_target_pairs={{0,3},{1,0},{2,1},{3,2},{4,7},{5,4},{6,5},{7,6},{8,11},{9,8},{10,9... | collective-permute-start | bytes 1572872 | tf_op jit(solution)/shard_map/ppermute | solution.py:44
  56.0 10.8 %collective-permute-done.2.refs_4_ = bf16[1,8,64,512]{3,2,1,0:T(8,128)(2,1)} collective-permute-done((bf16[1,8,64,512]{3,2,1,0:T(8,128)(2,1)S(1)}, bf16[1,8,64,512]{3,2,1,0:T(8,128)(2,1)}, u32[]{:S(2)}, u32[]{:S(2)}) %collective-permute-start.2) | collective-permute-done | bytes 524320 | tf_op jit(solution)/shard_map/ppermute | solution.py:40
  67.2 2.9 %collective-permute-start.9 = (bf16[1,8,64,512]{3,2,1,0:T(8,128)(2,1)}, bf16[1,8,64,512]{3,2,1,0:T(8,128)(2,1)S(1)}, u32[]{:S(2)}, u32[]{:S(2)}) collective-permute-start(bf16[1,8,64,512]{3,2,1,0:T(8,128)(2,1)} %collective-permute-done.1.refs_3_), channel_id=1, source_target_pairs={{0,3},{1,0},{2,1},{3,2},{4,7},{5,4},{6,5},{7,6},{8,11},{9,8},{10,9... | collective-permute-start | bytes 1572872 | tf_op jit(solution)/shard_map/ppermute | solution.py:44
  70.1 9.4 %all-to-all-done.1 = bf16[64,2,8,512]{3,2,1,0:T(8,128)(2,1)S(1)} async-done(((bf16[64,2,8,512]{3,2,1,0:T(8,128)(2,1)}), bf16[64,2,8,512]{3,2,1,0:T(8,128)(2,1)S(1)}, u32[]{:S(2)}, u32[]{:S(2)}) %all-to-all-start.1) | async-done | bytes 1048608 | tf_op jit(solution)/shard_map/route/all_to_all | solution.py:30
  80.3 0.8 copy-done.11
  81.1 1.6 collective-permute-start.5
  82.7 1.7 collective-permute-start.8
  84.7 4.6 %collective-permute-done.4.refs_8_ = bf16[1,8,64,512]{3,2,1,0:T(8,128)(2,1)} collective-permute-done((bf16[1,8,64,512]{3,2,1,0:T(8,128)(2,1)}, bf16[1,8,64,512]{3,2,1,0:T(8,128)(2,1)}, u32[]{:S(2)}, u32[]{:S(2)}) %collective-permute-start.4) | collective-permute-done | bytes 524320 | tf_op jit(solution)/shard_map/ppermute | solution.py:40
  89.3 1.8 %collective-permute-start.7 = (bf16[1,8,64,512]{3,2,1,0:T(8,128)(2,1)S(1)}, bf16[1,8,64,512]{3,2,1,0:T(8,128)(2,1)}, u32[]{:S(2)}, u32[]{:S(2)}) collective-permute-start(bf16[1,8,64,512]{3,2,1,0:T(8,128)(2,1)S(1)} %bitcast.63), channel_id=1, source_target_pairs={{0,3},{1,0},{2,1},{3,2},{4,7},{5,4},{6,5},{7,6},{8,11},{9,8},{10,9... | collective-permute-start | bytes 1572872 | tf_op jit(solution)/shard_map/ppermute | solution.py:44
  91.1 11.3 %product.2 = (f32[32,72,128]{2,1,0:T(8,128)}, f32[32,72,128]{2,1,0:T(8,128)}) custom-call(s32[1]{0:T(128)} %bitcast.place_ref, bf16[1,8,64,512]{3,2,1,0:T(8,128)(2,1)} %bitcast.61, bf16[1,8,64,512]{3,2,1,0:T(8,128)(2,1)} %bitcast.58, bf16[1,8,64,512]{3,2,1,0:T(8,128)(2,1)} %copy-done.11, bf16[1,8,64,512]{3,2,1,0:T(8,128)(2,1)} %collective-permute-done.1.refs_3_, ...), custom_call_target="tpu_custom_call" | custom-call | flops 4831838208 | bytes 15466496 | tf_op jit(solution)/shard_map/product/pallas_call | solution.py:99
  102.5 8.6 %collective-permute-done.6.refs_4_ = bf16[1,8,64,512]{3,2,1,0:T(8,128)(2,1)} collective-permute-done((bf16[1,8,64,512]{3,2,1,0:T(8,128)(2,1)S(1)}, bf16[1,8,64,512]{3,2,1,0:T(8,128)(2,1)}, u32[]{:S(2)}, u32[]{:S(2)}) %collective-permute-start.6) | collective-permute-done | bytes 524320 | tf_op jit(solution)/shard_map/ppermute | solution.py:40
  111.1 1.6 collective-permute-start.11
  112.6 1.7 collective-permute-start.12
  114.3 2.4 %add.56 = f32[32,72,128]{2,1,0:T(8,128)} add(f32[32,72,128]{2,1,0:T(8,128)} %get-tuple-element.29, f32[32,72,128]{2,1,0:T(8,128)S(1)} %collective-permute-done.10) | non-fusion elementwise | flops 294912 | bytes 3538944 | tf_op jit(solution)/shard_map/reduce_core/add | solution.py:123
  116.7 9.9 %all-to-all-start.2 = ((f32[32,72,128]{2,1,0:T(8,128)}), f32[32,72,128]{2,1,0:T(8,128)S(1)}, u32[]{:S(2)}, u32[]{:S(2)}) async-start(f32[32,72,128]{2,1,0:T(8,128)} %add.56), calls=%async_computation.2 | async-start | bytes 2359296 | tf_op jit(solution)/shard_map/reduce_xz/all_to_all | solution.py:128
  126.8 9.4 %product.3 = (f32[32,56,128]{2,1,0:T(8,128)}, f32[32,56,128]{2,1,0:T(8,128)}) custom-call(s32[1]{0:T(128)} %bitcast.place_ref, bf16[1,8,64,512]{3,2,1,0:T(8,128)(2,1)} %copy-done.8, bf16[1,8,64,512]{3,2,1,0:T(8,128)(2,1)} %collective-permute-done.7.refs_1_, bf16[1,8,64,512]{3,2,1,0:T(8,128)(2,1)} %copy-done.10, bf16[1,8,64,512]{3,2,1,0:T(8,128)(2,1)} %copy-done.9, ...), custom_call_target="tpu_custom_call" | custom-call | flops 3758096384 | bytes 13893632 | tf_op jit(solution)/shard_map/product/pallas_call | solution.py:99
  136.3 2.6 %collective-permute-done.13 = f32[32,56,128]{2,1,0:T(8,128)S(1)} collective-permute-done((f32[32,56,128]{2,1,0:T(8,128)}, f32[32,56,128]{2,1,0:T(8,128)S(1)}, u32[]{:S(2)}, u32[]{:S(2)}) %collective-permute-start.13) | collective-permute-done | bytes 917536 | tf_op jit(solution)/shard_map/reduce_core/ppermute | solution.py:123
  138.9 1.3 add.57
  140.3 2.2 %collective-permute-start.14 = (f32[8,56,128]{2,1,0:T(8,128)S(1)}, f32[8,56,128]{2,1,0:T(8,128)S(1)}, u32[]{:S(2)}, u32[]{:S(2)}) collective-permute-start(f32[8,56,128]{2,1,0:T(8,128)S(1)} %get-tuple-element.43), channel_id=1, source_target_pairs={{0,16},{8,24},{16,0},{24,8},{1,17},{9,25},{17,1},{25,9},{2,18},{10... | collective-permute-start | bytes 688136 | tf_op jit(solution)/shard_map/reduce_x/ppermute | solution.py:138
  142.4 2.0 %collective-permute-start.16 = (f32[8,56,128]{2,1,0:T(8,128)S(1)}, f32[8,56,128]{2,1,0:T(8,128)S(1)}, u32[]{:S(2)}, u32[]{:S(2)}) collective-permute-start(f32[8,56,128]{2,1,0:T(8,128)S(1)} %get-tuple-element.44), channel_id=1, source_target_pairs={{0,24},{8,0},{16,8},{24,16},{1,25},{9,1},{17,9},{25,17},{2,26},{10... | collective-permute-start | bytes 688136 | tf_op jit(solution)/shard_map/reduce_x/ppermute | solution.py:138
  144.5 11.3 %collective-permute-done.14 = f32[8,56,128]{2,1,0:T(8,128)S(1)} collective-permute-done((f32[8,56,128]{2,1,0:T(8,128)S(1)}, f32[8,56,128]{2,1,0:T(8,128)S(1)}, u32[]{:S(2)}, u32[]{:S(2)}) %collective-permute-start.14) | collective-permute-done | bytes 229408 | tf_op jit(solution)/shard_map/reduce_x/ppermute | solution.py:138
  155.8 3.1 %collective-permute-done.15 = f32[8,56,128]{2,1,0:T(8,128)S(1)} collective-permute-done((f32[8,56,128]{2,1,0:T(8,128)S(1)}, f32[8,56,128]{2,1,0:T(8,128)S(1)}, u32[]{:S(2)}, u32[]{:S(2)}) %collective-permute-start.15) | collective-permute-done | bytes 229408 | tf_op jit(solution)/shard_map/reduce_x/ppermute | solution.py:138
  158.8 1.5 collective-permute-done.16
  161.1 5.6 %all-to-all-start.3 = ((f32[8,56,128]{2,1,0:T(8,128)}), f32[8,56,128]{2,1,0:T(8,128)S(1)}, u32[]{:S(2)}, u32[]{:S(2)}) async-start(f32[8,56,128]{2,1,0:T(8,128)} %fusion.12), calls=%async_computation.3 | async-start | bytes 458752 | tf_op jit(solution)/shard_map/reduce_z/all_to_all | solution.py:141
  166.7 11.4 %all-to-all-done.3 = f32[8,56,128]{2,1,0:T(8,128)S(1)} async-done(((f32[8,56,128]{2,1,0:T(8,128)}), f32[8,56,128]{2,1,0:T(8,128)S(1)}, u32[]{:S(2)}, u32[]{:S(2)}) %all-to-all-start.3) | async-done | bytes 229408 | tf_op jit(solution)/shard_map/reduce_z/all_to_all | solution.py:141
  (65 shorter events, 5.3 us)
Async XLA Ops:
  3.3 12.2 %copy-start = (bf16[4,256,512]{2,1,0:T(8,128)(2,1)S(1)}, bf16[4,256,512]{2,1,0:T(8,128)(2,1)}, u32[]{:S(2)}) copy-start(bf16[4,256,512]{2,1,0:T(8,128)(2,1)} %param.6) | copy-start | bytes 3145732
  3.3 41.0 %all-to-all-start = ((bf16[64,2,8,512]{3,2,1,0:T(8,128)(2,1)}), bf16[64,2,8,512]{3,2,1,0:T(8,128)(2,1)S(1)}, u32[]{:S(2)}, u32[]{:S(2)}) async-start(bf16[64,2,8,512]{3,2,1,0:T(8,128)(2,1)} %fusion), calls=%async_computation | async-start | bytes 2097152 | tf_op jit(solution)/shard_map/route/all_to_all | solution.py:30
  44.7 11.1 %copy-start.1 = (bf16[8,4,2,1,8,512]{5,0,1,2,4,3:T(8,128)(2,1)}, bf16[8,4,2,1,8,512]{5,0,1,2,4,3:T(8,128)(2,1)S(1)}, u32[]{:S(2)}) copy-start(bf16[8,4,2,1,8,512]{5,0,1,2,4,3:T(8,128)(2,1)S(1)} %copy.17) | copy-start | bytes 1572868
  45.0 34.6 %copy-start.2 = (bf16[8,4,2,1,8,512]{5,0,1,2,4,3:T(8,128)(2,1)}, bf16[8,4,2,1,8,512]{5,0,1,2,4,3:T(8,128)(2,1)S(1)}, u32[]{:S(2)}) copy-start(bf16[8,4,2,1,8,512]{5,0,1,2,4,3:T(8,128)(2,1)S(1)} %copy.16) | copy-start | bytes 1572868
  45.0 34.5 %all-to-all-start.1 = ((bf16[64,2,8,512]{3,2,1,0:T(8,128)(2,1)}), bf16[64,2,8,512]{3,2,1,0:T(8,128)(2,1)S(1)}, u32[]{:S(2)}, u32[]{:S(2)}) async-start(bf16[64,2,8,512]{3,2,1,0:T(8,128)(2,1)} %fusion.1), calls=%async_computation.1 | async-start | bytes 2097152 | tf_op jit(solution)/shard_map/route/all_to_all | solution.py:30
  50.7 16.1 %collective-permute-start.2 = (bf16[1,8,64,512]{3,2,1,0:T(8,128)(2,1)S(1)}, bf16[1,8,64,512]{3,2,1,0:T(8,128)(2,1)}, u32[]{:S(2)}, u32[]{:S(2)}) collective-permute-start(bf16[1,8,64,512]{3,2,1,0:T(8,128)(2,1)S(1)} %bitcast.59), channel_id=1, source_target_pairs={{0,1},{1,2},{2,3},{3,0},{4,5},{5,6},{6,7},{7,4},{8,9},{9,10},{10,1... | collective-permute-start | bytes 1572872 | tf_op jit(solution)/shard_map/ppermute | solution.py:40
  52.3 14.9 %collective-permute-start.1 = (bf16[1,8,64,512]{3,2,1,0:T(8,128)(2,1)S(1)}, bf16[1,8,64,512]{3,2,1,0:T(8,128)(2,1)}, u32[]{:S(2)}, u32[]{:S(2)}) collective-permute-start(bf16[1,8,64,512]{3,2,1,0:T(8,128)(2,1)S(1)} %bitcast.56), channel_id=1, source_target_pairs={{0,3},{1,0},{2,1},{3,2},{4,7},{5,4},{6,5},{7,6},{8,11},{9,8},{10,9... | collective-permute-start | bytes 1572872 | tf_op jit(solution)/shard_map/ppermute | solution.py:44
  54.0 26.3 %collective-permute-start = (bf16[1,8,64,512]{3,2,1,0:T(8,128)(2,1)S(1)}, bf16[1,8,64,512]{3,2,1,0:T(8,128)(2,1)S(1)}, u32[]{:S(2)}, u32[]{:S(2)}) collective-permute-start(bf16[1,8,64,512]{3,2,1,0:T(8,128)(2,1)S(1)} %bitcast.60), channel_id=1, source_target_pairs={{0,3},{1,0},{2,1},{3,2},{4,7},{5,4},{6,5},{7,6},{8,11},{9,8},{10,9... | collective-permute-start | bytes 1572872 | tf_op jit(solution)/shard_map/ppermute | solution.py:44
  55.8 24.5 %collective-permute-start.3 = (bf16[1,8,64,512]{3,2,1,0:T(8,128)(2,1)S(1)}, bf16[1,8,64,512]{3,2,1,0:T(8,128)(2,1)}, u32[]{:S(2)}, u32[]{:S(2)}) collective-permute-start(bf16[1,8,64,512]{3,2,1,0:T(8,128)(2,1)S(1)} %bitcast.57), channel_id=1, source_target_pairs={{0,1},{1,2},{2,3},{3,0},{4,5},{5,6},{6,7},{7,4},{8,9},{9,10},{10,1... | collective-permute-start | bytes 1572872 | tf_op jit(solution)/shard_map/ppermute | solution.py:40
  66.8 22.5 %collective-permute-start.4 = (bf16[1,8,64,512]{3,2,1,0:T(8,128)(2,1)}, bf16[1,8,64,512]{3,2,1,0:T(8,128)(2,1)}, u32[]{:S(2)}, u32[]{:S(2)}) collective-permute-start(bf16[1,8,64,512]{3,2,1,0:T(8,128)(2,1)} %collective-permute-done.2.refs_4_), channel_id=1, source_target_pairs={{0,1},{1,2},{2,3},{3,0},{4,5},{5,6},{6,7},{7,4},{8,9},{9,10},{10,1... | collective-permute-start | bytes 1572872 | tf_op jit(solution)/shard_map/ppermute | solution.py:40
  67.2 35.2 %collective-permute-start.9 = (bf16[1,8,64,512]{3,2,1,0:T(8,128)(2,1)}, bf16[1,8,64,512]{3,2,1,0:T(8,128)(2,1)S(1)}, u32[]{:S(2)}, u32[]{:S(2)}) collective-permute-start(bf16[1,8,64,512]{3,2,1,0:T(8,128)(2,1)} %collective-permute-done.1.refs_3_), channel_id=1, source_target_pairs={{0,3},{1,0},{2,1},{3,2},{4,7},{5,4},{6,5},{7,6},{8,11},{9,8},{10,9... | collective-permute-start | bytes 1572872 | tf_op jit(solution)/shard_map/ppermute | solution.py:44
  79.9 11.2 %copy-start.3 = (bf16[8,4,2,1,8,512]{5,0,1,2,4,3:T(8,128)(2,1)}, bf16[8,4,2,1,8,512]{5,0,1,2,4,3:T(8,128)(2,1)S(1)}, u32[]{:S(2)}) copy-start(bf16[8,4,2,1,8,512]{5,0,1,2,4,3:T(8,128)(2,1)S(1)} %copy.18) | copy-start | bytes 1572868
  80.2 10.9 %copy-start.4 = (bf16[8,4,2,1,8,512]{5,0,1,2,4,3:T(8,128)(2,1)}, bf16[8,4,2,1,8,512]{5,0,1,2,4,3:T(8,128)(2,1)S(1)}, u32[]{:S(2)}) copy-start(bf16[8,4,2,1,8,512]{5,0,1,2,4,3:T(8,128)(2,1)S(1)} %copy.19) | copy-start | bytes 1572868
  81.1 21.4 %collective-permute-start.5 = (bf16[1,8,64,512]{3,2,1,0:T(8,128)(2,1)S(1)}, bf16[1,8,64,512]{3,2,1,0:T(8,128)(2,1)S(1)}, u32[]{:S(2)}, u32[]{:S(2)}) collective-permute-start(bf16[1,8,64,512]{3,2,1,0:T(8,128)(2,1)S(1)} %bitcast.62), channel_id=1, source_target_pairs={{0,1},{1,2},{2,3},{3,0},{4,5},{5,6},{6,7},{7,4},{8,9},{9,10},{10,1... | collective-permute-start | bytes 1572872 | tf_op jit(solution)/shard_map/ppermute | solution.py:40
  82.7 19.8 %collective-permute-start.8 = (bf16[1,8,64,512]{3,2,1,0:T(8,128)(2,1)S(1)}, bf16[1,8,64,512]{3,2,1,0:T(8,128)(2,1)S(1)}, u32[]{:S(2)}, u32[]{:S(2)}) collective-permute-start(bf16[1,8,64,512]{3,2,1,0:T(8,128)(2,1)S(1)} %bitcast.65), channel_id=1, source_target_pairs={{0,3},{1,0},{2,1},{3,2},{4,7},{5,4},{6,5},{7,6},{8,11},{9,8},{10,9... | collective-permute-start | bytes 1572872 | tf_op jit(solution)/shard_map/ppermute | solution.py:44
  84.3 26.7 %collective-permute-start.6 = (bf16[1,8,64,512]{3,2,1,0:T(8,128)(2,1)S(1)}, bf16[1,8,64,512]{3,2,1,0:T(8,128)(2,1)}, u32[]{:S(2)}, u32[]{:S(2)}) collective-permute-start(bf16[1,8,64,512]{3,2,1,0:T(8,128)(2,1)S(1)} %bitcast.66), channel_id=1, source_target_pairs={{0,1},{1,2},{2,3},{3,0},{4,5},{5,6},{6,7},{7,4},{8,9},{9,10},{10,1... | collective-permute-start | bytes 1572872 | tf_op jit(solution)/shard_map/ppermute | solution.py:40
  89.3 21.8 %collective-permute-start.7 = (bf16[1,8,64,512]{3,2,1,0:T(8,128)(2,1)S(1)}, bf16[1,8,64,512]{3,2,1,0:T(8,128)(2,1)}, u32[]{:S(2)}, u32[]{:S(2)}) collective-permute-start(bf16[1,8,64,512]{3,2,1,0:T(8,128)(2,1)S(1)} %bitcast.63), channel_id=1, source_target_pairs={{0,3},{1,0},{2,1},{3,2},{4,7},{5,4},{6,5},{7,6},{8,11},{9,8},{10,9... | collective-permute-start | bytes 1572872 | tf_op jit(solution)/shard_map/ppermute | solution.py:44
  102.4 14.3 %copy-start.8 = (bf16[1,8,64,512]{3,2,1,0:T(8,128)(2,1)}, bf16[1,8,64,512]{3,2,1,0:T(8,128)(2,1)S(1)}, u32[]{:S(2)}) copy-start(bf16[1,8,64,512]{3,2,1,0:T(8,128)(2,1)S(1)} %collective-permute-done.9.refs_0_) | copy-start | bytes 1572868
  102.5 14.3 %copy-start.9 = (bf16[1,8,64,512]{3,2,1,0:T(8,128)(2,1)}, bf16[1,8,64,512]{3,2,1,0:T(8,128)(2,1)S(1)}, u32[]{:S(2)}) copy-start(bf16[1,8,64,512]{3,2,1,0:T(8,128)(2,1)S(1)} %collective-permute-done.5.refs_3_) | copy-start | bytes 1572868
  102.5 14.3 %copy-start.10 = (bf16[1,8,64,512]{3,2,1,0:T(8,128)(2,1)}, bf16[1,8,64,512]{3,2,1,0:T(8,128)(2,1)S(1)}, u32[]{:S(2)}) copy-start(bf16[1,8,64,512]{3,2,1,0:T(8,128)(2,1)S(1)} %collective-permute-done.8.refs_2_) | copy-start | bytes 1572868
  111.1 3.2 %collective-permute-start.10 = (f32[32,72,128]{2,1,0:T(8,128)}, f32[32,72,128]{2,1,0:T(8,128)S(1)}, u32[]{:S(2)}, u32[]{:S(2)}) collective-permute-start(f32[32,72,128]{2,1,0:T(8,128)} %get-tuple-element.31), channel_id=1, source_target_pairs={{0,4},{4,0},{1,5},{5,1},{2,6},{6,2},{3,7},{7,3},{8,12},{12,8},{9,1... | collective-permute-start | bytes 3538952 | tf_op jit(solution)/shard_map/reduce_core/ppermute | solution.py:123
  111.1 15.7 %collective-permute-start.11 = (bf16[1,8,64,512]{3,2,1,0:T(8,128)(2,1)S(1)}, bf16[1,8,64,512]{3,2,1,0:T(8,128)(2,1)}, u32[]{:S(2)}, u32[]{:S(2)}) collective-permute-start(bf16[1,8,64,512]{3,2,1,0:T(8,128)(2,1)S(1)} %collective-permute-done.5.refs_3_), channel_id=1, source_target_pairs={{0,1},{1,2},{2,3},{3,0},{4,5},{5,6},{6,7},{7,4},{8,9},{9,10},{10,1... | collective-permute-start | bytes 1572872 | tf_op jit(solution)/shard_map/ppermute | solution.py:40
  112.6 14.2 %collective-permute-start.12 = (bf16[1,8,64,512]{3,2,1,0:T(8,128)(2,1)S(1)}, bf16[1,8,64,512]{3,2,1,0:T(8,128)(2,1)}, u32[]{:S(2)}, u32[]{:S(2)}) collective-permute-start(bf16[1,8,64,512]{3,2,1,0:T(8,128)(2,1)S(1)} %collective-permute-done.8.refs_2_), channel_id=1, source_target_pairs={{0,3},{1,0},{2,1},{3,2},{4,7},{5,4},{6,5},{7,6},{8,11},{9,8},{10,9... | collective-permute-start | bytes 1572872 | tf_op jit(solution)/shard_map/ppermute | solution.py:44
  116.7 44.3 %all-to-all-start.2 = ((f32[32,72,128]{2,1,0:T(8,128)}), f32[32,72,128]{2,1,0:T(8,128)S(1)}, u32[]{:S(2)}, u32[]{:S(2)}) async-start(f32[32,72,128]{2,1,0:T(8,128)} %add.56), calls=%async_computation.2 | async-start | bytes 2359296 | tf_op jit(solution)/shard_map/reduce_xz/all_to_all | solution.py:128
  136.2 2.7 %collective-permute-start.13 = (f32[32,56,128]{2,1,0:T(8,128)}, f32[32,56,128]{2,1,0:T(8,128)S(1)}, u32[]{:S(2)}, u32[]{:S(2)}) collective-permute-start(f32[32,56,128]{2,1,0:T(8,128)} %get-tuple-element.37), channel_id=1, source_target_pairs={{0,4},{4,0},{1,5},{5,1},{2,6},{6,2},{3,7},{7,3},{8,12},{12,8},{9,1... | collective-permute-start | bytes 2752520 | tf_op jit(solution)/shard_map/reduce_core/ppermute | solution.py:123
  140.3 15.5 %collective-permute-start.14 = (f32[8,56,128]{2,1,0:T(8,128)S(1)}, f32[8,56,128]{2,1,0:T(8,128)S(1)}, u32[]{:S(2)}, u32[]{:S(2)}) collective-permute-start(f32[8,56,128]{2,1,0:T(8,128)S(1)} %get-tuple-element.43), channel_id=1, source_target_pairs={{0,16},{8,24},{16,0},{24,8},{1,17},{9,25},{17,1},{25,9},{2,18},{10... | collective-permute-start | bytes 688136 | tf_op jit(solution)/shard_map/reduce_x/ppermute | solution.py:138
  142.4 16.4 %collective-permute-start.15 = (f32[8,56,128]{2,1,0:T(8,128)S(1)}, f32[8,56,128]{2,1,0:T(8,128)S(1)}, u32[]{:S(2)}, u32[]{:S(2)}) collective-permute-start(f32[8,56,128]{2,1,0:T(8,128)S(1)} %get-tuple-element.45), channel_id=1, source_target_pairs={{0,8},{8,16},{16,24},{24,0},{1,9},{9,17},{17,25},{25,1},{2,10},{10... | collective-permute-start | bytes 688136 | tf_op jit(solution)/shard_map/reduce_x/ppermute | solution.py:138
  142.4 17.9 %collective-permute-start.16 = (f32[8,56,128]{2,1,0:T(8,128)S(1)}, f32[8,56,128]{2,1,0:T(8,128)S(1)}, u32[]{:S(2)}, u32[]{:S(2)}) collective-permute-start(f32[8,56,128]{2,1,0:T(8,128)S(1)} %get-tuple-element.44), channel_id=1, source_target_pairs={{0,24},{8,0},{16,8},{24,16},{1,25},{9,1},{17,9},{25,17},{2,26},{10... | collective-permute-start | bytes 688136 | tf_op jit(solution)/shard_map/reduce_x/ppermute | solution.py:138
  161.0 17.3 %copy-start.5 = (bf16[16,1024]{1,0:T(8,128)(2,1)S(1)}, bf16[16,1024]{1,0:T(8,128)(2,1)}, u32[]{:S(2)}) copy-start(bf16[16,1024]{1,0:T(8,128)(2,1)} %param.9) | copy-start | bytes 98308
  161.0 17.3 %copy-start.6 = (f32[1024]{0:T(1024)S(1)}, f32[1024]{0:T(1024)}, u32[]{:S(2)}) copy-start(f32[1024]{0:T(1024)} %param.11) | copy-start | bytes 12292
  161.0 17.4 %copy-start.7 = (f32[16]{0:T(128)S(1)}, f32[16]{0:T(128)}, u32[]{:S(2)}) copy-start(f32[16]{0:T(128)} %param.10) | copy-start | bytes 196
  161.1 16.9 %all-to-all-start.3 = ((f32[8,56,128]{2,1,0:T(8,128)}), f32[8,56,128]{2,1,0:T(8,128)S(1)}, u32[]{:S(2)}, u32[]{:S(2)}) async-start(f32[8,56,128]{2,1,0:T(8,128)} %fusion.12), calls=%async_computation.3 | async-start | bytes 458752 | tf_op jit(solution)/shard_map/reduce_z/all_to_all | solution.py:141
  (1 other events, 0.8 us)
